TPU v7x, 32 devices: a whole 2x2x4 slice. The times are simulated.
32 devices in a mesh: dp: 8 (over z, x), row: 2 (over y), col: 2 (over core).
Axes of the slice: x: 2, y: 2, z: 4, core: 2. Of those that a mesh axis runs over, the one named last changes fastest.
Arguments:
- tokens_in: bfloat16 [37824, 768], P('dp', ('row', 'col')), may hold values from -8 to 8
- out_grad: bfloat16 [37824, 768], P('dp', ('row', 'col')), may hold values from -6 to 6
- qkv_weight: float32 [768, 2304], P('row', 'col'), may hold values from -0.21875 to 0.21875
- proj_weight: float32 [768, 768], P('col', 'row'), may hold values from -0.875 to 0.875
- expand_weight: float32 [768, 3072], P('row', 'col'), may hold values from -0.21875 to 0.21875
- contract_weight: float32 [3072, 768], P('col', 'row'), may hold values from -0.15625 to 0.15625
- norm_params: float32 [4, 768], P(None, ('row', 'col')), may hold values from -1 to 1.7
- qkv_first: float32 [768, 2304], P('row', 'col'), may hold values from -64 to 64
- qkv_second: float32 [768, 2304], P('row', 'col'), may hold values from 5.6736 to 90.7776
- proj_first: float32 [768, 768], P('col', 'row'), may hold values from -24 to 24
- proj_second: float32 [768, 768], P('col', 'row'), may hold values from 0.56736 to 9.07776
- expand_first: float32 [768, 3072], P('row', 'col'), may hold values from -64 to 64
- expand_second: float32 [768, 3072], P('row', 'col'), may hold values from 4.16064 to 66.57024
- contract_first: float32 [3072, 768], P('col', 'row'), may hold values from -96 to 96
- contract_second: float32 [3072, 768], P('col', 'row'), may hold values from 9.456 to 151.296
- norm_first: float32 [4, 768], P(None, ('row', 'col')), may hold values from -112 to 112
- norm_second: float32 [4, 768], P(None, ('row', 'col')), may hold values from 15.1296 to 242.0736
Outputs:
- output_tokens: float32 [37824, 768], P('dp', ('row', 'col'))
- input_grad: float32 [37824, 768], P('dp', ('row', 'col'))
- qkv_new: float32 [768, 2304], P('row', 'col')
- qkv_first_new: float32 [768, 2304], P('row', 'col')
- qkv_second_new: float32 [768, 2304], P('row', 'col')
- proj_new: float32 [768, 768], P('col', 'row')
- proj_first_new: float32 [768, 768], P('col', 'row')
- proj_second_new: float32 [768, 768], P('col', 'row')
- expand_new: float32 [768, 3072], P('row', 'col')
- expand_first_new: float32 [768, 3072], P('row', 'col')
- expand_second_new: float32 [768, 3072], P('row', 'col')
- contract_new: float32 [3072, 768], P('col', 'row')
- contract_first_new: float32 [3072, 768], P('col', 'row')
- contract_second_new: float32 [3072, 768], P('col', 'row')
- norm_new: float32 [4, 768], P(None, ('row', 'col'))
- norm_first_new: float32 [4, 768], P(None, ('row', 'col'))
- norm_second_new: float32 [4, 768], P(None, ('row', 'col'))
All inputs are finite; a program needn't handle non-finite values.
Results may differ from a plain program's by a relative error of at most 0.012.
Values may be sent and summed in bfloat16 or wider, within the bound.
No kernel may reach another device: no remote copies, remote signals or barrier semaphores. Data moves between devices by JAX's collectives and lax.ppermute only.
A program may use at most 256 MiB of HBM per device.

v0:
```python
from functools import partial

import jax
import jax.numpy as jnp
from jax import lax
from jax.sharding import PartitionSpec as P

HEAD_DIM = 64
SEQ = 197
IMG_BLOCK = 3
STEP = 10


norm_epsilon = 1e-06
beta_first = 0.9
beta_second = 0.999
adam_epsilon = 1e-08
rate_matrix = 0.1
rate_norm = 0.5
decay_matrix = 0.05


def for_sending(array):
    return jax.tree.map(lambda a: a.astype(jnp.bfloat16) if a.dtype == jnp.float32 else a, array)


def norm_forward(values, gain_row, shift_row):
    full_width = values.shape[1] * lax.axis_size("row") * lax.axis_size("col")
    row_sums, row_squares = lax.psum(
        (jnp.sum(values, axis=1), jnp.sum(values * values, axis=1)), ("row", "col")
    )
    center = row_sums / full_width
    spread = row_squares / full_width - center * center
    scaled = lax.rsqrt(spread + norm_epsilon)
    normed = (values - center[:, None]) * scaled[:, None]
    return ((normed * gain_row + shift_row).astype(jnp.bfloat16), normed, scaled)


def norm_backward(grad_normed, normed, scaled, gain_row):
    full_width = grad_normed.shape[1] * lax.axis_size("row") * lax.axis_size("col")
    local_grad = grad_normed * gain_row
    first_sum, second_sum = lax.psum(
        (jnp.sum(local_grad, axis=1), jnp.sum(local_grad * normed, axis=1)), ("row", "col")
    )
    grad_values = scaled[:, None] * (
        local_grad - first_sum[:, None] / full_width - normed * (second_sum[:, None] / full_width)
    )
    return (grad_values, jnp.sum(grad_normed * normed, axis=0), jnp.sum(grad_normed, axis=0))


def inner_rows(left, right):
    return lax.dot_general(
        left, right, (((0,), (0,)), ((), ())), preferred_element_type=jnp.float32
    )


def inner_cols(left, right):
    return lax.dot_general(
        left, right, (((1,), (1,)), ((), ())), preferred_element_type=jnp.float32
    )


def first_product(normed_low, weight_low):
    half_input = lax.all_gather(normed_low, "col", axis=1, tiled=True)
    partial_out = jnp.dot(half_input, weight_low, preferred_element_type=jnp.float32)
    result = lax.psum_scatter(partial_out, "row", scatter_dimension=1, tiled=True)
    return (result, half_input)


def first_backward(grad_low, half_input, weight_low):
    grad_half = lax.all_gather(grad_low, "row", axis=1, tiled=True)
    weight_grad = inner_rows(half_input, grad_half)
    partial_in = inner_cols(grad_half, weight_low)
    return (lax.psum_scatter(partial_in, "col", scatter_dimension=1, tiled=True), weight_grad)


def second_product(acts_low, weight_low):
    half_input = lax.all_gather(for_sending(acts_low), "row", axis=1, tiled=True).astype(
        acts_low.dtype
    )
    partial_out = jnp.dot(half_input, weight_low, preferred_element_type=jnp.float32)
    return (lax.psum_scatter(partial_out, "col", scatter_dimension=1, tiled=True), half_input)


def second_backward(grad_low, half_input, weight_low):
    grad_half = lax.all_gather(grad_low, "col", axis=1, tiled=True)
    weight_grad = inner_rows(half_input, grad_half)
    partial_in = inner_cols(grad_half, weight_low)
    return (lax.psum_scatter(partial_in, "row", scatter_dimension=1, tiled=True), weight_grad)


def attend_forward(mixed_low, images):
    tokens = mixed_low.shape[0]
    heads_here = mixed_low.shape[1] // (3 * HEAD_DIM)
    score_scale = HEAD_DIM ** (-0.5)
    grouped = mixed_low.reshape(images // IMG_BLOCK, IMG_BLOCK, SEQ, heads_here, 3, HEAD_DIM)

    def one_block(image_block):
        queries = image_block[:, :, :, 0]
        key_rows = image_block[:, :, :, 1]
        value_rows = image_block[:, :, :, 2]
        scores = (
            jnp.einsum("bqhd,bkhd->bhqk", queries, key_rows, preferred_element_type=jnp.float32)
            * score_scale
        )
        row_max = jnp.max(scores, axis=-1, keepdims=True)
        exponent = jnp.exp(scores - row_max)
        row_total = jnp.sum(exponent, axis=-1, keepdims=True)
        probs_low = (exponent / row_total).astype(jnp.bfloat16)
        mixed_out = jnp.einsum(
            "bhqk,bkhd->bqhd", probs_low, value_rows, preferred_element_type=jnp.float32
        )
        return (mixed_out.astype(jnp.bfloat16), (row_max + jnp.log(row_total))[..., 0])

    attended, log_total = lax.map(one_block, grouped)
    return (attended.reshape(tokens, heads_here * HEAD_DIM), log_total)


def attend_backward(mixed_low, log_total, grad_attended, images):
    tokens = mixed_low.shape[0]
    heads_here = mixed_low.shape[1] // (3 * HEAD_DIM)
    score_scale = HEAD_DIM ** (-0.5)
    grouped = mixed_low.reshape(images // IMG_BLOCK, IMG_BLOCK, SEQ, heads_here, 3, HEAD_DIM)
    grad_grouped = grad_attended.reshape(images // IMG_BLOCK, IMG_BLOCK, SEQ, heads_here, HEAD_DIM)

    def one_block(pieces):
        image_block, block_total, grad_block = pieces
        queries = image_block[:, :, :, 0]
        key_rows = image_block[:, :, :, 1]
        value_rows = image_block[:, :, :, 2]
        scores = (
            jnp.einsum("bqhd,bkhd->bhqk", queries, key_rows, preferred_element_type=jnp.float32)
            * score_scale
        )
        attn_probs = jnp.exp(scores - block_total[..., None])
        probs_low = attn_probs.astype(jnp.bfloat16)
        grad_values = jnp.einsum(
            "bhqk,bqhd->bkhd", probs_low, grad_block, preferred_element_type=jnp.float32
        )
        grad_probs = jnp.einsum(
            "bqhd,bkhd->bhqk", grad_block, value_rows, preferred_element_type=jnp.float32
        )
        inner_sum = jnp.sum(attn_probs * grad_probs, axis=-1, keepdims=True)
        grad_scores = (attn_probs * (grad_probs - inner_sum)).astype(jnp.bfloat16)
        grad_queries = (
            jnp.einsum("bhqk,bkhd->bqhd", grad_scores, key_rows, preferred_element_type=jnp.float32)
            * score_scale
        )
        grad_keys = (
            jnp.einsum("bhqk,bqhd->bkhd", grad_scores, queries, preferred_element_type=jnp.float32)
            * score_scale
        )
        return jnp.stack((grad_queries, grad_keys, grad_values), axis=3).astype(jnp.bfloat16)

    grad_mixed = lax.map(one_block, (grouped, log_total, grad_grouped))
    return grad_mixed.reshape(tokens, mixed_low.shape[1])


def adamw_update(weight, gradient, first_old, second_old, rate_value, decay_value):
    first_new = beta_first * first_old + (1.0 - beta_first) * gradient
    second_new = beta_second * second_old + (1.0 - beta_second) * (gradient * gradient)
    first_hat = first_new / (1.0 - beta_first**STEP)
    second_hat = second_new / (1.0 - beta_second**STEP)
    moved = weight - rate_value * (
        first_hat / (jnp.sqrt(second_hat) + adam_epsilon) + decay_value * weight
    )
    return (moved, first_new, second_new)


def local(
    tokens_in,
    out_grad,
    qkv_weight,
    proj_weight,
    expand_weight,
    contract_weight,
    norm_params,
    qkv_first,
    qkv_second,
    proj_first,
    proj_second,
    expand_first,
    expand_second,
    contract_first,
    contract_second,
    norm_first,
    norm_second,
):
    qkv_low = qkv_weight.astype(jnp.bfloat16)
    proj_low = proj_weight.astype(jnp.bfloat16)
    expand_low = expand_weight.astype(jnp.bfloat16)
    contract_low = contract_weight.astype(jnp.bfloat16)
    images = tokens_in.shape[0] // SEQ
    resid = tokens_in.astype(jnp.float32)
    h_one, normed_one, scaled_one = norm_forward(resid, norm_params[0], norm_params[1])
    mixed_sum, input_one = first_product(h_one, qkv_low)
    mixed_low = mixed_sum.astype(jnp.bfloat16)
    attended, log_total = attend_forward(mixed_low, images)
    branch, attended_half = second_product(attended, proj_low)
    middle = resid + branch
    h_two, normed_two, scaled_two = norm_forward(middle, norm_params[2], norm_params[3])
    hidden_pre, input_two = first_product(h_two, expand_low)
    gelu_value, gelu_pullback = jax.vjp(partial(jax.nn.gelu, approximate=False), hidden_pre)
    hidden = gelu_value.astype(jnp.bfloat16)
    feed, hidden_half = second_product(hidden, contract_low)
    output_tokens = middle + feed
    grad_hidden, contract_grad = second_backward(out_grad, hidden_half, contract_low)
    grad_pre = gelu_pullback(grad_hidden)[0].astype(jnp.bfloat16)
    grad_normed_two, expand_grad = first_backward(grad_pre, input_two, expand_low)
    middle_part, gain_two_grad, shift_two_grad = norm_backward(
        grad_normed_two, normed_two, scaled_two, norm_params[2]
    )
    grad_middle = out_grad.astype(jnp.float32) + middle_part
    grad_attended, proj_grad = second_backward(
        grad_middle.astype(jnp.bfloat16), attended_half, proj_low
    )
    grad_mixed = attend_backward(mixed_low, log_total, grad_attended.astype(jnp.bfloat16), images)
    grad_normed_one, qkv_grad = first_backward(grad_mixed, input_one, qkv_low)
    input_part, gain_one_grad, shift_one_grad = norm_backward(
        grad_normed_one, normed_one, scaled_one, norm_params[0]
    )
    input_grad = grad_middle + input_part
    norm_grad = jnp.stack((gain_one_grad, shift_one_grad, gain_two_grad, shift_two_grad))
    qkv_grad, proj_grad, expand_grad, contract_grad, norm_grad = lax.psum(
        (qkv_grad, proj_grad, expand_grad, contract_grad, norm_grad), "dp"
    )
    qkv_new, qkv_first_new, qkv_second_new = adamw_update(
        qkv_weight, qkv_grad, qkv_first, qkv_second, rate_matrix, decay_matrix
    )
    proj_new, proj_first_new, proj_second_new = adamw_update(
        proj_weight, proj_grad, proj_first, proj_second, rate_matrix, decay_matrix
    )
    expand_new, expand_first_new, expand_second_new = adamw_update(
        expand_weight, expand_grad, expand_first, expand_second, rate_matrix, decay_matrix
    )
    contract_new, contract_first_new, contract_second_new = adamw_update(
        contract_weight, contract_grad, contract_first, contract_second, rate_matrix, decay_matrix
    )
    norm_new, norm_first_new, norm_second_new = adamw_update(
        norm_params, norm_grad, norm_first, norm_second, rate_norm, 0.0
    )
    return (
        output_tokens,
        input_grad,
        qkv_new,
        qkv_first_new,
        qkv_second_new,
        proj_new,
        proj_first_new,
        proj_second_new,
        expand_new,
        expand_first_new,
        expand_second_new,
        contract_new,
        contract_first_new,
        contract_second_new,
        norm_new,
        norm_first_new,
        norm_second_new,
    )


def solution(mesh):
    in_specs = (
        P("dp", ("row", "col")),
        P("dp", ("row", "col")),
        P("row", "col"),
        P("col", "row"),
        P("row", "col"),
        P("col", "row"),
        P(None, ("row", "col")),
        P("row", "col"),
        P("row", "col"),
        P("col", "row"),
        P("col", "row"),
        P("row", "col"),
        P("row", "col"),
        P("col", "row"),
        P("col", "row"),
        P(None, ("row", "col")),
        P(None, ("row", "col")),
    )
    out_specs = (
        P("dp", ("row", "col")),
        P("dp", ("row", "col")),
        P("row", "col"),
        P("row", "col"),
        P("row", "col"),
        P("col", "row"),
        P("col", "row"),
        P("col", "row"),
        P("row", "col"),
        P("row", "col"),
        P("row", "col"),
        P("col", "row"),
        P("col", "row"),
        P("col", "row"),
        P(None, ("row", "col")),
        P(None, ("row", "col")),
        P(None, ("row", "col")),
    )
    return jax.shard_map(local, mesh=mesh, in_specs=in_specs, out_specs=out_specs, check_vma=False)
```

profile of v0, /device:TPU:0, one launch (start us, length us, event | category | flops | bytes accessed | tf_op | source)
XLA Modules:
  0.0 2135.3 jit_solution(6783659631551693573)
XLA Ops:
  10.3 13.2 all-reduce.4
  27.7 13.2 all-gather.9.cloned.1.call-done
  41.0 12.1 fusion.49
  53.4 244.5 %reduce-scatter.9.cloned.1.call-done = f32[4728,576]{0,1:T(8,128)} async-done(((f32[4728,1152]{0,1:T(8,128)}), f32[4728,576]{0,1:T(8,128)}) %reduce-scatter.9.cloned.1.call-update) | async-done | bytes 10893328 | tf_op jit(solution)/shard_map/reduce_scatter | solution.py:66
  304.9 24.2 %reshape.133 = bf16[8,3,197,3,3,64]{2,1,0,5,4,3:T(4,128)(2,1)} reshape(bf16[4728,576]{0,1:T(8,128)(2,1)} %convert_element_type.65) | data formatting | bytes 10893312 | tf_op jit(solution)/shard_map/reshape | solution.py:96
  329.1 11.8 copy.45
  340.9 21.1 while.22
  371.8 50.4 %all-gather.11.cloned.1.call-done = bf16[4728,384]{0,1:T(8,128)(2,1)} async-done(((bf16[4728,192]{0,1:T(8,128)(2,1)}), bf16[4728,384]{0,1:T(8,128)(2,1)}) %all-gather.11.cloned.1.call-update) | async-done | bytes 3631120 | tf_op jit(solution)/shard_map/all_gather | solution.py:78
  430.0 15.3 reduce-scatter.11.cloned.1.call-done
  449.7 12.1 all-reduce.3
  466.0 15.9 fusion.39
  483.6 15.1 fusion.45
  498.8 305.1 %reduce-scatter.17.cloned.1.call-done = f32[4728,768]{1,0:T(8,128)} async-done(((f32[4728,1536]{1,0:T(8,128)}), f32[4728,768]{1,0:T(8,128)}) %reduce-scatter.17.cloned.1.call-update) | async-done | bytes 14524432 | tf_op jit(solution)/shard_map/reduce_scatter | solution.py:89
  804.0 323.8 %reduce-scatter.13.cloned.1.call-done = f32[4728,768]{1,0:T(8,128)} async-done(((f32[4728,1536]{1,0:T(8,128)}), f32[4728,768]{1,0:T(8,128)}) %reduce-scatter.13.cloned.1.call-update) | async-done | bytes 14524432 | tf_op jit(solution)/shard_map/reduce_scatter | solution.py:66
  1127.8 37.0 %add_convert_fusion = (bf16[4728,768]{1,0:T(8,128)(2,1)}, f32[4728,768]{1,0:T(8,128)}) fusion(f32[4728,768]{1,0:T(8,128)} %reduce-scatter.17.cloned.1.call-done, f32[4728,768]{1,0:T(8,128)} %reduce-scatter.13.cloned.1.call-done), kind=kLoop, calls=%fused_computation.43 | loop fusion | flops 261439488 | bytes 50835456 | tf_op jit(solution)/shard_map/convert_element_type | solution.py:208
  1165.3 173.5 %all-gather.19.cloned.1.call-done = bf16[4728,1536]{1,0:T(8,128)(2,1)} async-done(((bf16[4728,768]{1,0:T(8,128)(2,1)}), bf16[4728,1536]{1,0:T(8,128)(2,1)}) %all-gather.19.cloned.1.call-update) | async-done | bytes 14524432 | tf_op jit(solution)/shard_map/all_gather | solution.py:71
  1338.8 16.7 fusion.43
  1355.5 15.9 reduce-scatter.19.cloned.1.call-done
  1376.2 12.1 all-reduce.2
  1394.6 13.0 all-gather.21.cloned.1.call-done
  1414.7 14.0 multiply_convert_fusion.1
  1428.9 74.8 %reduce-scatter.21.cloned.1.call-done = f32[4728,192]{0,1:T(8,128)} async-done(((f32[4728,384]{0,1:T(8,128)}), f32[4728,192]{0,1:T(8,128)}) %reduce-scatter.21.cloned.1.call-update) | async-done | bytes 3631120 | tf_op jit(solution)/shard_map/reduce_scatter | solution.py:89
  1518.8 56.4 %while.23 = (s32[]{:T(128)}, bf16[8,3,197,3,3,64]{2,5,3,1,4,0:T(8,128)(2,1)}, bf16[8,3,197,3,3,64]{2,5,3,1,4,0:T(8,128)(2,1)}, f32[8,3,3,197]{3,2,1,0:T(4,128)S(...) while((s32[]{:T(128)}, bf16[8,3,197,3,3,64]{2,5,3,1,4,0:T(8,128)(2,1)}, ...), condition=%wide.region_25.26_spmd, body=%wide.region_23.25_spmd.sunk | while | flops 228942160 | bytes 17083784 | solution.py:155
  1575.2 11.5 copy.49
  1586.7 17.0 reshape.136
  1615.3 63.8 %all-gather.15.cloned.1.call-done = bf16[4728,1536]{1,0:T(8,128)(2,1)} async-done(((bf16[4728,768]{1,0:T(8,128)(2,1)}), bf16[4728,1536]{1,0:T(8,128)(2,1)}) %all-gather.15.cloned.1.call-update) | async-done | bytes 14524432 | tf_op jit(solution)/shard_map/all_gather | solution.py:78
  1679.2 13.3 fusion.62
  1695.3 119.5 %all-gather.23.cloned.1.call-done = bf16[4728,1152]{0,1:T(8,128)(2,1)} async-done(((bf16[4728,576]{0,1:T(8,128)(2,1)}), bf16[4728,1152]{0,1:T(8,128)(2,1)}) %all-gather.23.cloned.1.call-update) | async-done | bytes 10893328 | tf_op jit(solution)/shard_map/all_gather | solution.py:71
  1814.9 12.6 fusion.59
  1841.7 12.1 fusion.41
  1853.8 209.6 %all-reduce.7.cloned.1.call-done = (f32[384,1152]{1,0:T(8,128)}, f32[384,384]{1,0:T(8,128)}, f32[384,1536]{1,0:T(8,128)}, f32[1536,384]{1,0:T(8,128)}) async-done(((f32[384,1152]{1,0:T(8,128)}, f32[384,384]{1,0:T(8,128)}, f32[384,1536]{1,0:T(8,128)}, f32[1536,384]{1,0:T(8,128)}), (f32[384,1152]{1,0:T(8,128)}, f32[384,384]{1,0:T(8,128)}, f32[384,1536]{1,0:T(8,128)}, ...) | async-done | bytes 7077904 | tf_op jit(solution)/shard_map/psum | solution.py:224
  2088.6 19.4 psum.103
  (269 shorter events, 227.6 us)
Async XLA Ops:
  7.2 33.8 %all-gather.9.cloned.1.call-start = ((), (), s32[]{:S(2)}) async-start(), calls=%async_computation.8 | async-start | bytes 5455872 | tf_op jit(solution)/shard_map/all_gather | solution.py:64
  8.1 32.9 %copy-start.8 = (f32[384,1152]{1,0:T(8,128)S(1)}, f32[384,1152]{1,0:T(8,128)}, u32[]{:S(2)}) copy-start(f32[384,1152]{1,0:T(8,128)} %param.23) | copy-start | bytes 5308420
  27.7 270.1 %reduce-scatter.9.cloned.1.call-start = ((), (), s32[]{:S(2)}) async-start(), calls=%async_computation.9 | async-start | bytes 32735232 | tf_op jit(solution)/shard_map/reduce_scatter | solution.py:66
  53.1 369.0 %all-gather.11.cloned.1.call-start = ((), (), s32[]{:S(2)}) async-start(), calls=%async_computation.10 | async-start | bytes 5455872 | tf_op jit(solution)/shard_map/all_gather | solution.py:78
  371.5 73.8 %reduce-scatter.11.cloned.1.call-start = ((), (), s32[]{:S(2)}) async-start(), calls=%async_computation.11 | async-start | bytes 10911744 | tf_op jit(solution)/shard_map/reduce_scatter | solution.py:82
  429.4 36.7 %all-gather.17.cloned.1.call-start = ((), (), s32[]{:S(2)}) async-start(), calls=%async_computation.16 | async-start | bytes 5455872 | tf_op jit(solution)/shard_map/all_gather | solution.py:86
  430.0 52.1 %all-gather.13.cloned.1.call-start = ((), (), s32[]{:S(2)}) async-start(), calls=%async_computation.12 | async-start | bytes 5455872 | tf_op jit(solution)/shard_map/all_gather | solution.py:64
  461.9 926.5 %copy-start.25 = (f32[4728]{0:T(1024)}, f32[4728]{0:T(1024)S(1)}, u32[]{:S(2)}) copy-start(f32[4728]{0:T(1024)S(1)} %get-tuple-element.154) | copy-start | bytes 56740
  461.9 926.5 %copy-start.27 = (f32[4728]{0:T(1024)}, f32[4728]{0:T(1024)S(1)}, u32[]{:S(2)}) copy-start(f32[4728]{0:T(1024)S(1)} %get-tuple-element.155) | copy-start | bytes 56740
  466.0 338.0 %reduce-scatter.17.cloned.1.call-start = ((), (), s32[]{:S(2)}) async-start(), calls=%async_computation.17 | async-start | bytes 43573248 | tf_op jit(solution)/shard_map/reduce_scatter | solution.py:89
  482.0 645.8 %reduce-scatter.13.cloned.1.call-start = ((), (), s32[]{:S(2)}) async-start(), calls=%async_computation.13 | async-start | bytes 43573248 | tf_op jit(solution)/shard_map/reduce_scatter | solution.py:66
  498.8 840.0 %all-gather.19.cloned.1.call-start = ((), (), s32[]{:S(2)}) async-start(), calls=%async_computation.18 | async-start | bytes 21786624 | tf_op jit(solution)/shard_map/all_gather | solution.py:71
  1164.8 206.6 %reduce-scatter.19.cloned.1.call-start = ((), (), s32[]{:S(2)}) async-start(), calls=%async_computation.19 | async-start | bytes 10911744 | tf_op jit(solution)/shard_map/reduce_scatter | solution.py:74
  1355.5 33.4 %copy-start.2 = (bf16[4728,192]{0,1:T(8,128)(2,1)S(1)}, bf16[4728,192]{0,1:T(8,128)(2,1)}, u32[]{:S(2)}) copy-start(bf16[4728,192]{0,1:T(8,128)(2,1)} %param.22) | copy-start | bytes 5446660
  1355.5 52.0 %all-gather.21.cloned.1.call-start = ((), (), s32[]{:S(2)}) async-start(), calls=%async_computation.20 | async-start | bytes 5455872 | tf_op jit(solution)/shard_map/all_gather | solution.py:86
  1394.5 109.1 %reduce-scatter.21.cloned.1.call-start = ((), (), s32[]{:S(2)}) async-start(), calls=%async_computation.21 | async-start | bytes 10911744 | tf_op jit(solution)/shard_map/reduce_scatter | solution.py:89
  1414.6 264.5 %all-gather.15.cloned.1.call-start = ((), (), s32[]{:S(2)}) async-start(), calls=%async_computation.14 | async-start | bytes 21786624 | tf_op jit(solution)/shard_map/all_gather | solution.py:78
  1428.7 386.2 %all-gather.23.cloned.1.call-start = ((), (), s32[]{:S(2)}) async-start(), calls=%async_computation.22 | async-start | bytes 16367616 | tf_op jit(solution)/shard_map/all_gather | solution.py:71
  1603.7 459.7 %all-reduce.7.cloned.1.call-start = ((), (), s32[]{:S(2)}) async-start(), calls=%async_computation.24 | async-start | bytes 14155776 | tf_op jit(solution)/shard_map/psum | solution.py:224
  1827.4 257.3 %reduce-scatter.23.cloned.1.call-start = ((), (), s32[]{:S(2)}) async-start(), calls=%async_computation.23 | async-start | bytes 10911744 | tf_op jit(solution)/shard_map/reduce_scatter | solution.py:74
  1840.0 279.2 %reduce-scatter.15.cloned.1.call-start = ((), (), s32[]{:S(2)}) async-start(), calls=%async_computation.15 | async-start | bytes 10911744 | tf_op jit(solution)/shard_map/reduce_scatter | solution.py:82
  1853.8 209.7 %copy-start.12 = (f32[384,384]{1,0:T(8,128)S(1)}, f32[384,384]{1,0:T(8,128)}, u32[]{:S(2)}) copy-start(f32[384,384]{1,0:T(8,128)} %param.24) | copy-start | bytes 1769476
  1853.8 209.7 %copy-start.23 = (f32[384,384]{1,0:T(8,128)S(1)}, f32[384,384]{1,0:T(8,128)}, u32[]{:S(2)}) copy-start(f32[384,384]{1,0:T(8,128)} %param.30) | copy-start | bytes 1769476
  1853.8 209.7 %copy-start.24 = (f32[384,384]{1,0:T(8,128)S(1)}, f32[384,384]{1,0:T(8,128)}, u32[]{:S(2)}) copy-start(f32[384,384]{1,0:T(8,128)} %param.31) | copy-start | bytes 1769476
  1853.8 212.3 %copy-start.10 = (f32[384,1152]{1,0:T(8,128)S(1)}, f32[384,1152]{1,0:T(8,128)}, u32[]{:S(2)}) copy-start(f32[384,1152]{1,0:T(8,128)} %param.23) | copy-start | bytes 5308420
  2084.6 33.8 %copy-start.37 = (f32[4,192]{1,0:T(4,128)S(1)}, f32[4,192]{1,0:T(4,128)}, u32[]{:S(2)}) copy-start(f32[4,192]{1,0:T(4,128)} %param.27) | copy-start | bytes 9220
  2084.6 33.8 %copy-start.40 = (f32[4,192]{1,0:T(4,128)S(1)}, f32[4,192]{1,0:T(4,128)}, u32[]{:S(2)}) copy-start(f32[4,192]{1,0:T(4,128)} %param.36) | copy-start | bytes 9220
  2084.6 33.8 %copy-start.41 = (f32[4,192]{1,0:T(4,128)S(1)}, f32[4,192]{1,0:T(4,128)}, u32[]{:S(2)}) copy-start(f32[4,192]{1,0:T(4,128)} %param.37) | copy-start | bytes 9220
  2084.7 34.5 %copy-start.26 = (f32[4728]{0:T(1024)S(1)}, f32[4728]{0:T(1024)}, u32[]{:S(2)}) copy-start(f32[4728]{0:T(1024)} %copy-done.25) | copy-start | bytes 56740
  2084.7 34.5 %copy-start.28 = (f32[4728]{0:T(1024)S(1)}, f32[4728]{0:T(1024)}, u32[]{:S(2)}) copy-start(f32[4728]{0:T(1024)} %copy-done.27) | copy-start | bytes 56740
  2084.7 34.5 %copy-start.34 = (f32[4728]{0:T(1024)S(1)}, f32[4728]{0:T(1024)}, u32[]{:S(2)}) copy-start(f32[4728]{0:T(1024)} %copy-done.33) | copy-start | bytes 56740
  2084.7 34.5 %copy-start.36 = (f32[4728]{0:T(1024)S(1)}, f32[4728]{0:T(1024)}, u32[]{:S(2)}) copy-start(f32[4728]{0:T(1024)} %copy-done.35) | copy-start | bytes 56740
  (27 other events, 160.9 us)
Sparse Core Ops, SparseCore 0:
  27.8 13.1 all-gather.8
  53.2 244.5 reduce-scatter.8
  371.7 50.4 all-gather.10
  429.5 15.7 reduce-scatter.10
  446.8 13.9 all-gather.16
  466.1 12.8 all-gather.12
  482.1 321.7 reduce-scatter.16
  806.4 321.3 reduce-scatter.12
  1164.9 173.8 all-gather.18
  1355.6 15.7 reduce-scatter.18
  1394.6 12.8 all-gather.20
  1414.7 88.8 reduce-scatter.20
  1505.3 173.8 all-gather.14
  1680.6 134.1 all-gather.22
  1827.6 235.8 all-reduce.6
  2065.6 14.7 reduce-scatter.22
  2082.6 16.9 reduce-scatter.14
where the time goes:
time: 2140 us
  waiting for transfers between devices  1620 us (76%)
  matrix products  179 us (8%)
  other arithmetic  132 us (6%)
  local copies, waits for them, and re-layouts  116 us (5%)
  blocking collectives  67.3 us (3%)
    reduce_scatter x2, waiting for transfers between devices, first_product(): lax.psum_scatter(partial_out, 'row', scatter_dimension=1, tiled=True)  568 us
    reduce_scatter x2, waiting for transfers between devices, second_backward(): lax.psum_scatter(partial_in, 'row', scatter_dimension=1, tiled=True)  380 us
    all_gather x2, waiting for transfers between devices, first_backward(): grad_half = lax.all_gather(grad_low, 'row', axis=1, tiled=True)  293 us
    psum x1, waiting for transfers between devices, local(): lax.psum((qkv_grad, proj_grad, expand_grad, contract_grad, norm_grad), 'dp')  210 us
    all_gather x2, waiting for transfers between devices, second_product(): lax.all_gather(for_sending(acts_low), 'row', axis=1, tiled=True)  114 us
    dot_general x4, matrix products, inner_cols(): lax.dot_general(left, right, (((1,), (1,)), ((), ())), preferred_element_...  50.7 us
  transfers between devices with their start and end apart: 17, of which 13 were waited for; matrix products, arithmetic and copies ran while one was open for 11% of the time, Pallas kernels for 0%

commit v1 on v0

v1 whole, which is shorter than its diff:
```python
import jax
import jax.numpy as jnp
from jax import lax
from jax.experimental import pallas as pl
from jax.experimental.pallas import tpu as pltpu
from jax.sharding import PartitionSpec as P

HEAD_DIM = 64
SEQ = 197
QROWS = 208
KROWS = 256
STEP = 10

norm_epsilon = 1e-06
beta_first = 0.9
beta_second = 0.999
adam_epsilon = 1e-08
rate_matrix = 0.1
rate_norm = 0.5
decay_matrix = 0.05

GROUP = ("row", "col")
bf16 = jnp.bfloat16
f32 = jnp.float32


def dot(left, right, dims=((1,), (0,))):
    return lax.dot_general(left, right, (dims, ((), ())), preferred_element_type=f32)


def swap_halves(block):
    return jnp.concatenate([block[:, HEAD_DIM:], block[:, :HEAD_DIM]], axis=1)


def attend_forward_kernel(mixed_ref, out_ref, probs_ref, wide, gathered):
    tokens = mixed_ref.shape[0]
    images = tokens // SEQ
    wide[tokens - tokens % 8 :, :] = jnp.zeros((wide.shape[0] - tokens + tokens % 8, 384), f32)
    wide[0:tokens, :] = mixed_ref[...].astype(f32)
    low_lane = lax.broadcasted_iota(jnp.int32, (1, 128), 1) < HEAD_DIM
    key_lane = lax.broadcasted_iota(jnp.int32, (1, KROWS), 1) < SEQ
    for image in range(images):
        start = image * SEQ
        block_a = wide[start : start + KROWS, 0:128]
        block_b = wide[start : start + KROWS, 128:256]
        block_c = wide[start : start + KROWS, 256:384]
        scale = HEAD_DIM ** (-0.5)
        query_0 = jnp.where(low_lane, block_a[:QROWS] * scale, 0.0).astype(bf16)
        query_1 = jnp.where(low_lane, 0.0, block_b[:QROWS] * scale).astype(bf16)
        keys_0 = swap_halves(block_a).astype(bf16)
        keys_1 = swap_halves(block_c).astype(bf16)
        outs = []
        for which, (query, keys, values) in enumerate(
            ((query_0, keys_0, block_b), (query_1, keys_1, block_c))
        ):
            scores = jnp.where(key_lane, dot(query, keys, ((1,), (1,))), -1e30)
            exponent = jnp.exp(scores - jnp.max(scores, axis=1, keepdims=True))
            total = jnp.sum(exponent, axis=1, keepdims=True)
            probs = (exponent * (1.0 / total)).astype(bf16)
            probs_ref[0, image * 2 + which] = probs
            outs.append(dot(probs, values.astype(bf16)))
        gathered[start : start + QROWS, :] = jnp.where(low_lane, outs[0], outs[1])
    out_ref[...] = gathered[0:tokens, :].astype(bf16)


def attend_forward(mixed):
    tokens, width = mixed.shape
    images = tokens // SEQ
    pairs = width // 384
    padded = -(-((images - 1) * SEQ + KROWS) // 16) * 16
    return pl.pallas_call(
        attend_forward_kernel,
        grid=(pairs,),
        in_specs=[pl.BlockSpec((tokens, 384), lambda i: (0, i))],
        out_specs=[
            pl.BlockSpec((tokens, 128), lambda i: (0, i)),
            pl.BlockSpec((1, 2 * images, QROWS, KROWS), lambda i: (i, 0, 0, 0)),
        ],
        out_shape=[
            jax.ShapeDtypeStruct((tokens, pairs * 128), bf16),
            jax.ShapeDtypeStruct((pairs, 2 * images, QROWS, KROWS), bf16),
        ],
        scratch_shapes=[pltpu.VMEM((padded, 384), f32), pltpu.VMEM((padded, 128), f32)],
        compiler_params=pltpu.CompilerParams(vmem_limit_bytes=40 * 2**20),
        cost_estimate=pl.CostEstimate(
            flops=pairs * images * 4 * 2 * QROWS * KROWS * 128,
            bytes_accessed=tokens * width * 3,
            transcendentals=pairs * images * 2 * QROWS * KROWS,
        ),
        name="attend_forward",
    )(mixed)


def attend_backward_kernel(mixed_ref, probs_ref, grad_ref, out_ref, wide, grad_wide, gathered):
    tokens = mixed_ref.shape[0]
    images = tokens // SEQ
    wide[tokens - tokens % 8 :, :] = jnp.zeros((wide.shape[0] - tokens + tokens % 8, 384), f32)
    wide[0:tokens, :] = mixed_ref[...].astype(f32)
    grad_wide[0:tokens, :] = grad_ref[...].astype(f32)
    low_lane = lax.broadcasted_iota(jnp.int32, (1, 128), 1) < HEAD_DIM
    query_row = lax.broadcasted_iota(jnp.int32, (QROWS, 128), 0) < SEQ
    scale = HEAD_DIM ** (-0.5)
    for image in range(images):
        start = image * SEQ
        block_a = wide[start : start + KROWS, 0:128]
        block_b = wide[start : start + KROWS, 128:256]
        block_c = wide[start : start + KROWS, 256:384]
        grad = jnp.where(query_row, grad_wide[start : start + QROWS, :], 0.0)
        grad_low = grad.astype(bf16)
        swapped_a = (swap_halves(block_a) * scale).astype(bf16)
        swapped_b = (swap_halves(block_b) * scale).astype(bf16)
        swapped_c = (swap_halves(block_c) * scale).astype(bf16)
        probs_0 = probs_ref[0, 2 * image]
        probs_1 = probs_ref[0, 2 * image + 1]
        grad_v0 = dot(probs_0, grad_low, ((0,), (0,)))
        grad_v1 = dot(probs_1, grad_low, ((0,), (0,)))
        score_grads = []
        for probs, part, values in (
            (probs_0, jnp.where(low_lane, grad, 0.0), block_b),
            (probs_1, jnp.where(low_lane, 0.0, grad), block_c),
        ):
            grad_probs = dot(part.astype(bf16), values.astype(bf16), ((1,), (1,)))
            wide_probs = probs.astype(f32)
            inner = jnp.sum(wide_probs * grad_probs, axis=1, keepdims=True)
            score_grads.append((wide_probs * (grad_probs - inner)).astype(bf16))
        score_0, score_1 = score_grads
        grad_q0 = dot(score_0, swapped_a)
        grad_k0 = dot(score_0, swapped_a[:QROWS], ((0,), (0,)))
        grad_q1 = dot(score_1, swapped_c)
        grad_k1 = dot(score_1, swapped_b[:QROWS], ((0,), (0,)))
        rows = slice(start, start + QROWS)
        gathered[rows, 0:128] = jnp.where(low_lane, grad_q0, grad_k0[:QROWS])
        gathered[rows, 128:256] = jnp.where(low_lane, grad_v0[:QROWS], grad_q1)
        gathered[rows, 256:384] = jnp.where(low_lane, grad_k1[:QROWS], grad_v1[:QROWS])
    out_ref[...] = gathered[0:tokens, :].astype(bf16)


def attend_backward(mixed, probs, grad_attended):
    tokens, width = mixed.shape
    images = tokens // SEQ
    pairs = width // 384
    padded = -(-((images - 1) * SEQ + KROWS) // 16) * 16
    return pl.pallas_call(
        attend_backward_kernel,
        grid=(pairs,),
        in_specs=[
            pl.BlockSpec((tokens, 384), lambda i: (0, i)),
            pl.BlockSpec((1, 2 * images, QROWS, KROWS), lambda i: (i, 0, 0, 0)),
            pl.BlockSpec((tokens, 128), lambda i: (0, i)),
        ],
        out_specs=pl.BlockSpec((tokens, 384), lambda i: (0, i)),
        out_shape=jax.ShapeDtypeStruct((tokens, width), bf16),
        scratch_shapes=[
            pltpu.VMEM((padded, 384), f32),
            pltpu.VMEM((padded, 128), f32),
            pltpu.VMEM((padded, 384), f32),
        ],
        compiler_params=pltpu.CompilerParams(vmem_limit_bytes=40 * 2**20),
        cost_estimate=pl.CostEstimate(
            flops=pairs * images * 8 * 2 * QROWS * KROWS * 128,
            bytes_accessed=tokens * width * 4,
            transcendentals=0,
        ),
        name="attend_backward",
    )(mixed, probs, grad_attended)


def gelu_and_slope(value):
    size = jnp.abs(value)
    density = jnp.exp(value * value * -0.5)
    t = 1.0 / (1.0 + (0.3275911 * 0.5**0.5) * size)
    series = t * (
        0.254829592
        + t * (-0.284496736 + t * (1.421413741 + t * (-1.453152027 + t * 1.061405429)))
    )
    tail = 0.5 * series * density
    phi = jnp.where(value >= 0, 1.0 - tail, tail)
    return (value * phi, phi + value * density * 0.3989422804014327)


def norm_forward(values, gain_row, shift_row):
    center = jnp.mean(values, axis=1, keepdims=True)
    spread = jnp.mean(values * values, axis=1, keepdims=True) - center * center
    scaled = lax.rsqrt(spread + norm_epsilon)
    normed = (values - center) * scaled
    return ((normed * gain_row + shift_row).astype(bf16), normed, scaled)


def norm_backward(grad_normed, normed, scaled, gain_row):
    local_grad = grad_normed * gain_row
    first = jnp.mean(local_grad, axis=1, keepdims=True)
    second = jnp.mean(local_grad * normed, axis=1, keepdims=True)
    grad_values = scaled * (local_grad - first - normed * second)
    return (grad_values, jnp.sum(grad_normed * normed, axis=0), jnp.sum(grad_normed, axis=0))


def adamw_update(weight, gradient, first_old, second_old, rate_value, decay_value):
    first_new = beta_first * first_old + (1.0 - beta_first) * gradient
    second_new = beta_second * second_old + (1.0 - beta_second) * (gradient * gradient)
    first_hat = first_new / (1.0 - beta_first**STEP)
    second_hat = second_new / (1.0 - beta_second**STEP)
    moved = weight - rate_value * (
        first_hat / (jnp.sqrt(second_hat) + adam_epsilon) + decay_value * weight
    )
    return (moved, first_new, second_new)


def local(
    tokens_in,
    out_grad,
    qkv_weight,
    proj_weight,
    expand_weight,
    contract_weight,
    norm_params,
    qkv_first,
    qkv_second,
    proj_first,
    proj_second,
    expand_first,
    expand_second,
    contract_first,
    contract_second,
    norm_first,
    norm_second,
):
    row = lax.axis_index("row")
    col = lax.axis_index("col")
    me = 2 * row + col
    tokens = tokens_in.shape[0] // 4
    part = tokens_in.shape[1]

    def swap(array, distance):
        if distance == 0:
            return array
        return lax.ppermute(array, GROUP, [(i, i ^ distance) for i in range(4)])

    def swap_row(array):
        return swap(array, 2)

    def swap_col(array):
        return swap(array, 1)

    def in_order(first, second):
        return jnp.where(col == 0, jnp.concatenate([first, second], -1), jnp.concatenate([second, first], -1))

    def join_features(parts):
        return jnp.concatenate([in_order(parts[0], parts[1]), in_order(parts[2], parts[3])], -1)

    def tokens_together(array):
        blocks = [
            lax.dynamic_slice(array, ((me ^ d) * tokens, 0), (tokens, part)) for d in range(4)
        ]
        return join_features([swap(block, d) for d, block in enumerate(blocks)])

    def split_features(array):
        quarters = [array[..., i * part : (i + 1) * part] for i in range(4)]
        own = [jnp.where(col == 0, quarters[2 * i], quarters[2 * i + 1]) for i in range(2)]
        other = [jnp.where(col == 0, quarters[2 * i + 1], quarters[2 * i]) for i in range(2)]
        return [own[0], other[0], own[1], other[1]]

    def features_together(array):
        pieces = split_features(array)
        result = jnp.zeros((4 * tokens, part), f32)
        for d in range(4):
            received = swap(pieces[d].astype(bf16), d).astype(f32)
            result = lax.dynamic_update_slice(result, received, ((me ^ d) * tokens, 0))
        return result

    def gather_row_col(weight):
        mine = weight.astype(bf16)
        stacked = jnp.concatenate([mine, swap_row(mine)], axis=0)
        return jnp.concatenate([stacked, swap_col(stacked)], axis=1)

    def gather_col_row(weight):
        mine = weight.astype(bf16)
        stacked = jnp.concatenate([mine, swap_row(mine)], axis=1)
        return jnp.concatenate([stacked, swap_col(stacked)], axis=0)

    def reduce_row_col(left, right):
        half = right.shape[1] // 2
        rows = left.shape[1] // 2
        away = dot(left, right[:, half:], ((0,), (0,))).astype(bf16)
        kept = dot(left, right[:, :half], ((0,), (0,)))
        total = kept + swap_col(away).astype(f32)
        return total[:rows] + swap_row(total[rows:].astype(bf16)).astype(f32)

    def reduce_col_row(left, right):
        half = left.shape[1] // 2
        columns = right.shape[1] // 2
        away = dot(left[:, half:], right, ((0,), (0,))).astype(bf16)
        kept = dot(left[:, :half], right, ((0,), (0,)))
        total = kept + swap_col(away).astype(f32)
        return total[:, :columns] + swap_row(total[:, columns:].astype(bf16)).astype(f32)

    resid_low = tokens_together(tokens_in)
    params = join_features([swap(norm_params, d) for d in range(4)])
    qkv_low = gather_row_col(qkv_weight)
    proj_low = gather_col_row(proj_weight)
    expand_low = gather_row_col(expand_weight)
    contract_low = gather_col_row(contract_weight)
    grad_low = tokens_together(out_grad)

    resid = resid_low.astype(f32)
    h_one, normed_one, scaled_one = norm_forward(resid, params[0], params[1])
    mixed = dot(h_one, qkv_low).astype(bf16)
    attended, probs = attend_forward(mixed)
    middle = resid + dot(attended, proj_low)
    h_two, normed_two, scaled_two = norm_forward(middle, params[2], params[3])
    gelu_value, gelu_slope = gelu_and_slope(dot(h_two, expand_low))
    hidden = gelu_value.astype(bf16)
    gelu_slope = gelu_slope.astype(bf16)
    output_tokens = features_together(middle + dot(hidden, contract_low))

    contract_grad = reduce_col_row(hidden, grad_low)
    grad_pre = (dot(grad_low, contract_low, ((1,), (1,))) * gelu_slope.astype(f32)).astype(bf16)
    expand_grad = reduce_row_col(h_two, grad_pre)
    grad_two = dot(grad_pre, expand_low, ((1,), (1,)))
    middle_part, gain_two, shift_two = norm_backward(grad_two, normed_two, scaled_two, params[2])
    grad_middle = grad_low.astype(f32) + middle_part
    grad_branch = grad_middle.astype(bf16)
    proj_grad = reduce_col_row(attended, grad_branch)
    grad_attended = dot(grad_branch, proj_low, ((1,), (1,))).astype(bf16)
    grad_mixed = attend_backward(mixed, probs, grad_attended)
    qkv_grad = reduce_row_col(h_one, grad_mixed)
    grad_one = dot(grad_mixed, qkv_low, ((1,), (1,)))
    input_part, gain_one, shift_one = norm_backward(grad_one, normed_one, scaled_one, params[0])
    input_grad = features_together(grad_middle + input_part)

    def over_dp(gradient, after):
        gradient = gradient.astype(bf16)
        if after is not None:
            gradient, after = lax.optimization_barrier((gradient, after))
        return lax.psum(gradient, "dp")

    contract_sum = over_dp(contract_grad, None)
    expand_sum = over_dp(expand_grad, contract_sum)
    proj_sum = over_dp(proj_grad, expand_sum)
    qkv_sum = over_dp(qkv_grad, proj_sum)
    norm_parts = jnp.stack(
        split_features(jnp.stack((gain_one, shift_one, gain_two, shift_two)))
    )
    norm_mine = norm_parts[0] + sum(swap(norm_parts[d], d) for d in range(1, 4))
    norm_sum = lax.psum(norm_mine, "dp")

    results = (output_tokens, input_grad)
    for weight, gradient, first, second in (
        (qkv_weight, qkv_sum, qkv_first, qkv_second),
        (proj_weight, proj_sum, proj_first, proj_second),
        (expand_weight, expand_sum, expand_first, expand_second),
        (contract_weight, contract_sum, contract_first, contract_second),
    ):
        results += adamw_update(
            weight, gradient.astype(f32), first, second, rate_matrix, decay_matrix
        )
    return results + adamw_update(norm_params, norm_sum, norm_first, norm_second, rate_norm, 0.0)


def solution(mesh):
    tokens = P("dp", ("row", "col"))
    one = P("row", "col")
    two = P("col", "row")
    norm = P(None, ("row", "col"))
    in_specs = (tokens, tokens, one, two, one, two, norm)
    in_specs += (one, one, two, two, one, one, two, two, norm, norm)
    out_specs = (tokens, tokens) + (one,) * 3 + (two,) * 3 + (one,) * 3 + (two,) * 3 + (norm,) * 3
    return jax.shard_map(local, mesh=mesh, in_specs=in_specs, out_specs=out_specs, check_vma=False)
```

time: 2140 us -> 751 us (0.35)
  waiting for transfers between devices: 1620 us -> 362 us
  other arithmetic: 132 us -> 65 us
  matrix products: 179 us -> 129 us
  blocking collectives: 67.3 us -> 19.9 us
  Pallas kernels: 0 us -> 43.1 us
  local copies, waits for them, and re-layouts: 116 us -> 80.6 us
  starting transfers between devices: 2.13 us -> 25.9 us
    reduce_scatter x8 -> x0, waiting for transfers between devices: 979 us -> none  [the longest x2 568 us: first_product(): lax.psum_scatter(partial_out, 'row', scatter_dimension=1, tiled=True)]
    all_gather x8 -> x0, waiting for transfers between devices: 433 us -> none  [the longest x2 293 us: first_backward(): grad_half = lax.all_gather(grad_low, 'row', axis=1, tiled=True)]
    ppermute x0 -> x34, waiting for transfers between devices: none -> 146 us  [swap(): return lax.ppermute(array, GROUP, [(i, i ^ distance) for i in range(4)])]
    convert_element_type x15 -> x16, other arithmetic: 78.2 us -> 20.4 us  [the longest x4 9.49 us: over_dp(): gradient = gradient.astype(bf16)]
    reshape x4 -> x0, local copies, waits for them, and re-layouts: 54 us -> none  [the longest x1 24.2 us: attend_forward(): mixed_low.reshape(images // IMG_BLOCK, IMG_BLOCK, SEQ, heads_here, 3, HEA...]
    dot_general x68 -> x16, matrix products: 179 us -> 129 us  [dot(): lax.dot_general(left, right, (dims, ((), ())), preferred_element_type=f32)]
    dynamic_update_slice x0 -> x8, local copies, waits for them, and re-layouts: none -> 48.8 us  [features_together(): result = lax.dynamic_update_slice(result, received, ((me ^ d) * tokens, 0))]
    psum x5 -> x1, blocking collectives: 67.3 us -> 19.9 us  [local(): norm_sum = lax.psum(norm_mine, 'dp')]
  transfers between devices with their start and end apart: 17 -> 38, of which waited for: 13 -> 14; matrix products, arithmetic and copies ran while one was open for 11% -> 19% of each run, Pallas kernels for 0% -> 2%
where the time goes in v1:
time: 751 us; the launch traced here: 741 us
  waiting for transfers between devices  362 us (48%)
  matrix products  129 us (17%)
  local copies, waits for them, and re-layouts  80.6 us (11%)
  other arithmetic  65 us (9%)
  Pallas kernels  43.1 us (6%)
  starting transfers between devices  25.9 us (3%)
  blocking collectives  19.9 us (3%)
  between operations  15.1 us (2%)
    psum x4, waiting for transfers between devices, over_dp(): return lax.psum(gradient, 'dp')  216 us
    ppermute x34, waiting for transfers between devices, swap(): return lax.ppermute(array, GROUP, [(i, i ^ distance) for i in range(4)])  146 us
    dot_general x16, matrix products, dot(): lax.dot_general(left, right, (dims, ((), ())), preferred_element_type=f32)  129 us
    dynamic_update_slice x8, local copies, waits for them, and re-layouts, features_together(): result = lax.dynamic_update_slice(result, received, ((me ^ d) * tokens, 0))  48.8 us
    pallas_call x1, Pallas kernels, attend_backward(): pl.pallas_call(attend_backward_kernel, grid=(pairs,), in_specs=[pl.BlockS...  26.1 us
    ppermute x34, starting transfers between devices, swap(): return lax.ppermute(array, GROUP, [(i, i ^ distance) for i in range(4)])  25.6 us
    sub x5, other arithmetic, adamw_update(): weight - rate_value * (first_hat / (jnp.sqrt(second_hat) + adam_epsilon)...  22.1 us
    psum x1, blocking collectives, local(): norm_sum = lax.psum(norm_mine, 'dp')  19.9 us
  transfers between devices with their start and end apart: 38, of which 14 were waited for; matrix products, arithmetic and copies ran while one was open for 19% of the time, Pallas kernels for 2%

profile of v1, /device:TPU:0, one launch (start us, length us, event | category | flops | bytes accessed | tf_op | source)
XLA Modules:
  0.0 741.2 jit_solution(6633585917124640552)
XLA Ops:
  24.1 9.4 %collective-permute-done.4 = f32[4,192]{1,0:T(4,128)S(1)} collective-permute-done((f32[4,192]{1,0:T(4,128)}, f32[4,192]{1,0:T(4,128)S(1)}, u32[]{:S(2)}, u32[]{:S(2)}) %collective-permute-start.4) | collective-permute-done | bytes 3104 | tf_op jit(solution)/shard_map/ppermute | solution.py:236
  37.4 23.6 %collective-permute-done.8 = bf16[384,384]{1,0:T(8,128)(2,1)S(1)} collective-permute-done((bf16[384,384]{1,0:T(8,128)(2,1)S(1)}, bf16[384,384]{1,0:T(8,128)(2,1)S(1)}, u32[]{:S(2)}, u32[]{:S(2)}) %collective-permute-start.8) | collective-permute-done | bytes 294944 | tf_op jit(solution)/shard_map/ppermute | solution.py:236
  66.2 30.6 %collective-permute-done.18 = bf16[1182,192]{0,1:T(8,128)(2,1)S(1)} collective-permute-done((bf16[1182,192]{0,1:T(8,128)(2,1)S(1)}, bf16[1182,192]{0,1:T(8,128)(2,1)S(1)}, u32[]{:S(2)}, u32[]{:S(2)}) %collective-permute-start.18) | collective-permute-done | bytes 453920 | tf_op jit(solution)/shard_map/ppermute | solution.py:236
  96.8 9.0 %collective-permute-done.19 = bf16[1182,192]{0,1:T(8,128)(2,1)S(1)} collective-permute-done((bf16[1182,192]{0,1:T(8,128)(2,1)S(1)}, bf16[1182,192]{0,1:T(8,128)(2,1)S(1)}, u32[]{:S(2)}, u32[]{:S(2)}) %collective-permute-start.19) | collective-permute-done | bytes 453920 | tf_op jit(solution)/shard_map/ppermute | solution.py:236
  107.2 6.8 convolution_convert_fusion.mixed_ref
  114.0 16.9 %attend_forward.1 = (bf16[1182,768]{1,0:T(8,128)(2,1)S(1)}, bf16[6,12,208,256]{3,2,1,0:T(8,128)(2,1)}) custom-call(bf16[1182,2304]{1,0:T(8,128)(2,1)S(1)} %convolution_convert_fusion.mixed_ref), custom_call_target="tpu_custom_call" | custom-call | flops 1962934272 | bytes 8169984 | tf_op jit(solution)/shard_map/attend_forward/pallas_call | solution.py:71
  135.6 25.1 %multiply_convert_fusion.1 = (bf16[1182,3072]{1,0:T(8,128)(2,1)S(1)}, f32[1182,3072]{1,0:T(8,128)}) fusion(bf16[1182,768]{0,1:T(8,128)(2,1)S(1)} %add_convert_fusion.1, bf16[768,1536]{1,0:T(8,128)(2,1)S(1)} %collective-permute-done.11, bf16[384,1536]{1,0:T(8,128)(2,1)S(1)} %collective-permute-done.10, bf16[384,1536]{1,0:T(8,128)(2,1)S(1)} %convert_element_type.163), kind=kOutput, calls=%fused_computation.3 | convolution fusion | flops 5671415808 | bytes 28320768 | tf_op jit(solution)/shard_map/dot_general | solution.py:28
  174.5 26.3 %collective-permute-done.30 = bf16[1536,384]{1,0:T(8,128)(2,1)S(1)} collective-permute-done((bf16[1536,384]{1,0:T(8,128)(2,1)S(1)}, bf16[1536,384]{1,0:T(8,128)(2,1)S(1)}, u32[]{:S(2)}, u32[]{:S(2)}) %collective-permute-start.30) | collective-permute-done | bytes 1179680 | tf_op jit(solution)/shard_map/ppermute | solution.py:236
  202.2 81.6 %all-reduce.5.cloned.1.call-done = bf16[1536,384]{1,0:T(8,128)(2,1)} async-done(((bf16[1536,384]{1,0:T(8,128)(2,1)}), bf16[1536,384]{1,0:T(8,128)(2,1)}) %all-reduce.5.cloned.1.call-update) | async-done | bytes 1179664 | tf_op jit(solution)/shard_map/psum | solution.py:334
  283.8 8.3 %multiply_subtract_fusion = (f32[1536,384]{1,0:T(8,128)}, f32[1536,384]{1,0:T(8,128)}, f32[1536,384]{1,0:T(8,128)}, bf16[1536,384]{1,0:T(8,128)(2,1)S(1)}) fusion(f32[1536,384]{1,0:T(8,128)} %param.22, bf16[1536,384]{1,0:T(8,128)(2,1)} %all-reduce.5.cloned.1.call-done, f32[1536,384]{1,0:T(8,128)} %param.30, f32[1536,384]{1,0:T(8,128)} %param.31), kind=kLoop, calls=%fused_computation.72 | loop fusion | flops 10027008 | bytes 16515072 | tf_op jit(solution)/shard_map/sub | solution.py:202
  293.6 25.7 %collective-permute-done.12 = bf16[1536,384]{1,0:T(8,128)(2,1)S(1)} collective-permute-done((bf16[1536,384]{1,0:T(8,128)(2,1)S(1)}, bf16[1536,384]{1,0:T(8,128)(2,1)S(1)}, u32[]{:S(2)}, u32[]{:S(2)}) %collective-permute-start.12) | collective-permute-done | bytes 1179680 | tf_op jit(solution)/shard_map/ppermute | solution.py:236
  324.0 26.4 %multiply_convert_fusion = bf16[1182,3072]{1,0:T(8,128)(2,1)S(1)} fusion(f32[1182,3072]{1,0:T(8,128)} %get-tuple-element.82, bf16[1536,768]{1,0:T(8,128)(2,1)S(1)} %collective-permute-done.13, bf16[1536,384]{1,0:T(8,128)(2,1)S(1)} %collective-permute-done.12, bf16[1536,384]{1,0:T(8,128)(2,1)S(1)} %get-tuple-element.56, ...), kind=kOutput, calls=%fused_computation.1 | convolution fusion | flops 5693202432 | bytes 28320768 | tf_op jit(solution)/shard_map/dot_general | solution.py:28
  355.1 7.7 %fusion.92 = (f32[768]{0:T(1024)S(1)}, f32[1182,768]{1,0:T(8,128)}) fusion(bf16[1182,3072]{1,0:T(8,128)(2,1)S(1)} %multiply_convert_fusion, bf16[768,1536]{1,0:T(8,128)(2,1)S(1)} %copy-done.64, bf16[384,1536]{1,0:T(8,128)(2,1)S(1)} %copy-done.33, bf16[384,1536]{1,0:T(8,128)(2,1)S(1)} %convert_element_type.163), kind=kOutput, calls=%fused_computation.171 | convolution fusion | flops 5592438784 | bytes 15614976 | tf_op jit(solution)/shard_map/dot_general | solution.py:28
  362.9 5.3 copy.74
  378.9 26.1 %attend_backward.1 = bf16[1182,2304]{1,0:T(8,128)(2,1)S(1)} custom-call(bf16[1182,2304]{1,0:T(8,128)(2,1)S(1)} %bitcast.8, bf16[6,12,208,256]{3,2,1,0:T(8,128)(2,1)} %get-tuple-element.23.probs_ref, bf16[1182,768]{1,0:T(8,128)(2,1)S(1)} %convolution_convert_fusion.2.grad_ref), custom_call_target="tpu_custom_call" | custom-call | flops 3925868544 | bytes 10893312 | tf_op jit(solution)/shard_map/attend_backward/pallas_call | solution.py:143
  410.2 7.7 %fusion.93 = (f32[768]{0:T(1024)S(1)}, f32[1182,768]{1,0:T(8,128)}) fusion(bf16[1182,2304]{1,0:T(8,128)(2,1)S(1)} %attend_backward.1, bf16[768,1152]{1,0:T(8,128)(2,1)S(1)} %copy-done.66, bf16[384,1152]{1,0:T(8,128)(2,1)} %collective-permute-done.6, bf16[384,1152]{1,0:T(8,128)(2,1)} %convert_element_type.159), kind=kOutput, calls=%fused_computation.172 | convolution fusion | flops 4194555648 | bytes 12619776 | tf_op jit(solution)/shard_map/dot_general | solution.py:28
  417.9 5.3 copy.75
  435.2 17.7 %convolution_add_fusion = bf16[1182,768]{0,1:T(8,128)(2,1)} fusion(f32[1182,768]{0,1:T(8,128)S(1)} %copy-done.9, bf16[1182,3072]{1,0:T(8,128)(2,1)} %copy-done.70, bf16[1536,768]{1,0:T(8,128)(2,1)} %copy-done.62, bf16[1536,384]{1,0:T(8,128)(2,1)S(1)} %copy-done.35, bf16[1536,384]{1,0:T(8,128)(2,1)S(1)} %copy-done.19), kind=kOutput, calls=%fused_computation.34 | convolution fusion | flops 5593347072 | bytes 17427456 | tf_op jit(solution)/shard_map/dot_general | solution.py:28
  453.0 6.5 convert_add_fusion.2
  466.8 5.7 dynamic_update_slice.28
  477.5 6.1 dynamic_update_slice.24
  496.2 5.6 convert_add_fusion.3
  520.1 19.9 %psum.39 = f32[4,192]{1,0:T(4,128)S(1)} all-reduce(f32[4,192]{1,0:T(4,128)S(1)} %add_add_fusion), channel_id=1, replica_groups=mesh['dp'=8,'row'=2,'col'=2] {'dp'}, use_global_device_ids=true, to_apply=%region_16.17 | all-reduce | flops 768 | bytes 6144 | tf_op jit(solution)/shard_map/psum | solution.py:344
  541.8 6.4 dynamic_update_slice.29
  548.3 6.4 dynamic_update_slice.30
  554.7 5.6 dynamic_update_slice.31
  561.5 6.4 dynamic_update_slice.25
  568.0 6.4 dynamic_update_slice.26
  575.5 5.7 dynamic_update_slice.27
  586.3 63.8 %all-reduce.9.cloned.1.call-done = bf16[384,384]{1,0:T(8,128)(2,1)} async-done(((bf16[384,384]{1,0:T(8,128)(2,1)}), bf16[384,384]{1,0:T(8,128)(2,1)}) %all-reduce.9.cloned.1.call-update) | async-done | bytes 294928 | tf_op jit(solution)/shard_map/psum | solution.py:334
  650.2 6.7 multiply_subtract_fusion.1
  658.5 70.9 %all-reduce.11.cloned.1.call-done = bf16[384,1152]{1,0:T(8,128)(2,1)} async-done(((bf16[384,1152]{1,0:T(8,128)(2,1)}), bf16[384,1152]{1,0:T(8,128)(2,1)}) %all-reduce.11.cloned.1.call-update) | async-done | bytes 884752 | tf_op jit(solution)/shard_map/psum | solution.py:334
  (281 shorter events, 144.2 us)
Async XLA Ops:
  7.2 276.6 %all-reduce.5.cloned.1.call-start = ((), (), s32[]{:S(2)}) async-start(), calls=%async_computation | async-start | bytes 2359296 | tf_op jit(solution)/shard_map/psum | solution.py:334
  9.7 26.0 %collective-permute-start.6 = (bf16[384,1152]{1,0:T(8,128)(2,1)}, bf16[384,1152]{1,0:T(8,128)(2,1)}, u32[]{:S(2)}, u32[]{:S(2)}) collective-permute-start(bf16[384,1152]{1,0:T(8,128)(2,1)} %convert_element_type.159), channel_id=1, source_target_pairs={{0,2},{1,3},{2,0},{3,1},{4,6},{5,7},{6,4},{7,5},{8,10},{9,11},{10,... | collective-permute-start | bytes 2654216 | tf_op jit(solution)/shard_map/ppermute | solution.py:236
  12.7 20.8 %collective-permute-start.4 = (f32[4,192]{1,0:T(4,128)}, f32[4,192]{1,0:T(4,128)S(1)}, u32[]{:S(2)}, u32[]{:S(2)}) collective-permute-start(f32[4,192]{1,0:T(4,128)} %param.23), channel_id=1, source_target_pairs={{0,2},{1,3},{2,0},{3,1},{4,6},{5,7},{6,4},{7,5},{8,10},{9,11},{10,... | collective-permute-start | bytes 9224 | tf_op jit(solution)/shard_map/ppermute | solution.py:236
  12.7 20.8 %collective-permute-start.5 = (f32[4,192]{1,0:T(4,128)}, f32[4,192]{1,0:T(4,128)S(1)}, u32[]{:S(2)}, u32[]{:S(2)}) collective-permute-start(f32[4,192]{1,0:T(4,128)} %param.23), channel_id=1, source_target_pairs={{0,3},{1,2},{2,1},{3,0},{4,7},{5,6},{6,5},{7,4},{8,11},{9,10},{10,... | collective-permute-start | bytes 9224 | tf_op jit(solution)/shard_map/ppermute | solution.py:236
  18.7 42.3 %collective-permute-start.1 = (bf16[1182,192]{0,1:T(8,128)(2,1)}, bf16[1182,192]{0,1:T(8,128)(2,1)}, u32[]{:S(2)}, u32[]{:S(2)}) collective-permute-start(bf16[1182,192]{0,1:T(8,128)(2,1)} %get-tuple-element.72), channel_id=1, source_target_pairs={{0,2},{1,3},{2,0},{3,1},{4,6},{5,7},{6,4},{7,5},{8,10},{9,11},{10,... | collective-permute-start | bytes 1361672 | tf_op jit(solution)/shard_map/ppermute | solution.py:236
  22.6 40.5 %collective-permute-start.2 = (bf16[1182,192]{0,1:T(8,128)(2,1)}, bf16[1182,192]{0,1:T(8,128)(2,1)S(1)}, u32[]{:S(2)}, u32[]{:S(2)}) collective-permute-start(bf16[1182,192]{0,1:T(8,128)(2,1)} %get-tuple-element.71), channel_id=1, source_target_pairs={{0,3},{1,2},{2,1},{3,0},{4,7},{5,6},{6,5},{7,4},{8,11},{9,10},{10,... | collective-permute-start | bytes 1361672 | tf_op jit(solution)/shard_map/ppermute | solution.py:236
  33.5 31.4 %collective-permute-start = (bf16[1182,192]{0,1:T(8,128)(2,1)}, bf16[1182,192]{0,1:T(8,128)(2,1)S(1)}, u32[]{:S(2)}, u32[]{:S(2)}) collective-permute-start(bf16[1182,192]{0,1:T(8,128)(2,1)} %get-tuple-element.70), channel_id=1, source_target_pairs={{0,1},{1,0},{2,3},{3,2},{4,5},{5,4},{6,7},{7,6},{8,9},{9,8},{10,11... | collective-permute-start | bytes 1361672 | tf_op jit(solution)/shard_map/ppermute | solution.py:236
  33.5 27.4 %collective-permute-start.8 = (bf16[384,384]{1,0:T(8,128)(2,1)S(1)}, bf16[384,384]{1,0:T(8,128)(2,1)S(1)}, u32[]{:S(2)}, u32[]{:S(2)}) collective-permute-start(bf16[384,384]{1,0:T(8,128)(2,1)S(1)} %convert_element_type.161), channel_id=1, source_target_pairs={{0,2},{1,3},{2,0},{3,1},{4,6},{5,7},{6,4},{7,5},{8,10},{9,11},{10,... | collective-permute-start | bytes 884744 | tf_op jit(solution)/shard_map/ppermute | solution.py:236
  35.7 70.6 %collective-permute-start.10 = (bf16[384,1536]{1,0:T(8,128)(2,1)S(1)}, bf16[384,1536]{1,0:T(8,128)(2,1)S(1)}, u32[]{:S(2)}, u32[]{:S(2)}) collective-permute-start(bf16[384,1536]{1,0:T(8,128)(2,1)S(1)} %convert_element_type.163), channel_id=1, source_target_pairs={{0,2},{1,3},{2,0},{3,1},{4,6},{5,7},{6,4},{7,5},{8,10},{9,11},{10,... | collective-permute-start | bytes 3538952 | tf_op jit(solution)/shard_map/ppermute | solution.py:236
  61.0 46.2 %collective-permute-start.7 = (bf16[768,1152]{1,0:T(8,128)(2,1)S(1)}, bf16[768,1152]{1,0:T(8,128)(2,1)S(1)}, u32[]{:S(2)}, u32[]{:S(2)}) collective-permute-start(bf16[768,1152]{1,0:T(8,128)(2,1)S(1)} %pad_maximum_fusion.11), channel_id=1, source_target_pairs={{0,1},{1,0},{2,3},{3,2},{4,5},{5,4},{6,7},{7,6},{8,9},{9,8},{10,11... | collective-permute-start | bytes 5308424 | tf_op jit(solution)/shard_map/ppermute | solution.py:236
  61.0 35.7 %collective-permute-start.18 = (bf16[1182,192]{0,1:T(8,128)(2,1)S(1)}, bf16[1182,192]{0,1:T(8,128)(2,1)S(1)}, u32[]{:S(2)}, u32[]{:S(2)}) collective-permute-start(bf16[1182,192]{0,1:T(8,128)(2,1)S(1)} %copy-done.41), channel_id=1, source_target_pairs={{0,2},{1,3},{2,0},{3,1},{4,6},{5,7},{6,4},{7,5},{8,10},{9,11},{10,... | collective-permute-start | bytes 1361672 | tf_op jit(solution)/shard_map/ppermute | solution.py:236
  63.2 42.6 %collective-permute-start.19 = (bf16[1182,192]{0,1:T(8,128)(2,1)S(1)}, bf16[1182,192]{0,1:T(8,128)(2,1)S(1)}, u32[]{:S(2)}, u32[]{:S(2)}) collective-permute-start(bf16[1182,192]{0,1:T(8,128)(2,1)S(1)} %copy-done.40), channel_id=1, source_target_pairs={{0,3},{1,2},{2,1},{3,0},{4,7},{5,6},{6,5},{7,4},{8,11},{9,10},{10,... | collective-permute-start | bytes 1361672 | tf_op jit(solution)/shard_map/ppermute | solution.py:236
  64.9 41.1 %collective-permute-start.17 = (bf16[1182,192]{0,1:T(8,128)(2,1)S(1)}, bf16[1182,192]{0,1:T(8,128)(2,1)S(1)}, u32[]{:S(2)}, u32[]{:S(2)}) collective-permute-start(bf16[1182,192]{0,1:T(8,128)(2,1)S(1)} %copy-done.39), channel_id=1, source_target_pairs={{0,1},{1,0},{2,3},{3,2},{4,5},{5,4},{6,7},{7,6},{8,9},{9,8},{10,11... | collective-permute-start | bytes 1361672 | tf_op jit(solution)/shard_map/ppermute | solution.py:236
  96.8 34.2 %collective-permute-start.9 = (bf16[384,768]{1,0:T(8,128)(2,1)S(1)}, bf16[384,768]{1,0:T(8,128)(2,1)S(1)}, u32[]{:S(2)}, u32[]{:S(2)}) collective-permute-start(bf16[384,768]{1,0:T(8,128)(2,1)S(1)} %pad_maximum_fusion.15), channel_id=1, source_target_pairs={{0,1},{1,0},{2,3},{3,2},{4,5},{5,4},{6,7},{7,6},{8,9},{9,8},{10,11... | collective-permute-start | bytes 1769480 | tf_op jit(solution)/shard_map/ppermute | solution.py:236
  106.5 29.0 %collective-permute-start.11 = (bf16[768,1536]{1,0:T(8,128)(2,1)S(1)}, bf16[768,1536]{1,0:T(8,128)(2,1)S(1)}, u32[]{:S(2)}, u32[]{:S(2)}) collective-permute-start(bf16[768,1536]{1,0:T(8,128)(2,1)S(1)} %pad_maximum_fusion.3), channel_id=1, source_target_pairs={{0,1},{1,0},{2,3},{3,2},{4,5},{5,4},{6,7},{7,6},{8,9},{9,8},{10,11... | collective-permute-start | bytes 7077896 | tf_op jit(solution)/shard_map/ppermute | solution.py:236
  172.7 28.1 %collective-permute-start.30 = (bf16[1536,384]{1,0:T(8,128)(2,1)S(1)}, bf16[1536,384]{1,0:T(8,128)(2,1)S(1)}, u32[]{:S(2)}, u32[]{:S(2)}) collective-permute-start(bf16[1536,384]{1,0:T(8,128)(2,1)S(1)} %slice.272), channel_id=1, source_target_pairs={{0,2},{1,3},{2,0},{3,1},{4,6},{5,7},{6,4},{7,5},{8,10},{9,11},{10,... | collective-permute-start | bytes 3538952 | tf_op jit(solution)/shard_map/ppermute | solution.py:236
  202.2 381.0 %all-reduce.7.cloned.1.call-start = ((), (), s32[]{:S(2)}) async-start(), calls=%async_computation.1 | async-start | bytes 2359296 | tf_op jit(solution)/shard_map/psum | solution.py:334
  292.1 27.1 %collective-permute-start.12 = (bf16[1536,384]{1,0:T(8,128)(2,1)S(1)}, bf16[1536,384]{1,0:T(8,128)(2,1)S(1)}, u32[]{:S(2)}, u32[]{:S(2)}) collective-permute-start(bf16[1536,384]{1,0:T(8,128)(2,1)S(1)} %get-tuple-element.56), channel_id=1, source_target_pairs={{0,2},{1,3},{2,0},{3,1},{4,6},{5,7},{6,4},{7,5},{8,10},{9,11},{10,... | collective-permute-start | bytes 3538952 | tf_op jit(solution)/shard_map/ppermute | solution.py:236
  427.5 66.6 %collective-permute-start.31 = (f32[4,192]{1,0:T(4,128)S(1)}, f32[4,192]{1,0:T(4,128)S(1)}, u32[]{:S(2)}, u32[]{:S(2)}) collective-permute-start(f32[4,192]{1,0:T(4,128)S(1)} %get-tuple-element.75), channel_id=1, source_target_pairs={{0,1},{1,0},{2,3},{3,2},{4,5},{5,4},{6,7},{7,6},{8,9},{9,8},{10,11... | collective-permute-start | bytes 9224 | tf_op jit(solution)/shard_map/ppermute | solution.py:236
  427.6 67.1 %collective-permute-start.32 = (f32[4,192]{1,0:T(4,128)S(1)}, f32[4,192]{1,0:T(4,128)S(1)}, u32[]{:S(2)}, u32[]{:S(2)}) collective-permute-start(f32[4,192]{1,0:T(4,128)S(1)} %get-tuple-element.73), channel_id=1, source_target_pairs={{0,2},{1,3},{2,0},{3,1},{4,6},{5,7},{6,4},{7,5},{8,10},{9,11},{10,... | collective-permute-start | bytes 9224 | tf_op jit(solution)/shard_map/ppermute | solution.py:236
  429.1 73.8 %collective-permute-start.33 = (f32[4,192]{1,0:T(4,128)S(1)}, f32[4,192]{1,0:T(4,128)S(1)}, u32[]{:S(2)}, u32[]{:S(2)}) collective-permute-start(f32[4,192]{1,0:T(4,128)S(1)} %get-tuple-element.74), channel_id=1, source_target_pairs={{0,3},{1,2},{2,1},{3,0},{4,7},{5,6},{6,5},{7,4},{8,11},{9,10},{10,... | collective-permute-start | bytes 9224 | tf_op jit(solution)/shard_map/ppermute | solution.py:236
  429.3 23.6 %collective-permute-start.27 = (bf16[768,1536]{1,0:T(8,128)(2,1)}, bf16[768,1536]{1,0:T(8,128)(2,1)}, u32[]{:S(2)}, u32[]{:S(2)}) collective-permute-start(bf16[768,1536]{1,0:T(8,128)(2,1)} %fusion.25), channel_id=1, source_target_pairs={{0,1},{1,0},{2,3},{3,2},{4,5},{5,4},{6,7},{7,6},{8,9},{9,8},{10,11... | collective-permute-start | bytes 7077896 | tf_op jit(solution)/shard_map/ppermute | solution.py:236
  429.8 66.4 %collective-permute-start.23 = (bf16[768,1152]{1,0:T(8,128)(2,1)}, bf16[768,1152]{1,0:T(8,128)(2,1)}, u32[]{:S(2)}, u32[]{:S(2)}) collective-permute-start(bf16[768,1152]{1,0:T(8,128)(2,1)} %convolution_convert_fusion.1), channel_id=1, source_target_pairs={{0,1},{1,0},{2,3},{3,2},{4,5},{5,4},{6,7},{7,6},{8,9},{9,8},{10,11... | collective-permute-start | bytes 5308424 | tf_op jit(solution)/shard_map/ppermute | solution.py:236
  462.0 28.6 %collective-permute-start.28 = (bf16[384,1536]{1,0:T(8,128)(2,1)}, bf16[384,1536]{1,0:T(8,128)(2,1)}, u32[]{:S(2)}, u32[]{:S(2)}) collective-permute-start(bf16[384,1536]{1,0:T(8,128)(2,1)} %slice.273), channel_id=1, source_target_pairs={{0,2},{1,3},{2,0},{3,1},{4,6},{5,7},{6,4},{7,5},{8,10},{9,11},{10,... | collective-permute-start | bytes 3538952 | tf_op jit(solution)/shard_map/ppermute | solution.py:236
  494.0 156.1 %all-reduce.9.cloned.1.call-start = ((), (), s32[]{:S(2)}) async-start(), calls=%async_computation.2 | async-start | bytes 589824 | tf_op jit(solution)/shard_map/psum | solution.py:334
  496.2 22.4 %collective-permute-start.22 = (bf16[1182,192]{0,1:T(8,128)(2,1)}, bf16[1182,192]{0,1:T(8,128)(2,1)S(1)}, u32[]{:S(2)}, u32[]{:S(2)}) collective-permute-start(bf16[1182,192]{0,1:T(8,128)(2,1)} %get-tuple-element.57), channel_id=1, source_target_pairs={{0,3},{1,2},{2,1},{3,0},{4,7},{5,6},{6,5},{7,4},{8,11},{9,10},{10,... | collective-permute-start | bytes 1361672 | tf_op jit(solution)/shard_map/ppermute | solution.py:236
  502.9 57.4 %collective-permute-start.14 = (bf16[1182,192]{0,1:T(8,128)(2,1)}, bf16[1182,192]{0,1:T(8,128)(2,1)}, u32[]{:S(2)}, u32[]{:S(2)}) collective-permute-start(bf16[1182,192]{0,1:T(8,128)(2,1)} %get-tuple-element.64), channel_id=1, source_target_pairs={{0,1},{1,0},{2,3},{3,2},{4,5},{5,4},{6,7},{7,6},{8,9},{9,8},{10,11... | collective-permute-start | bytes 1361672 | tf_op jit(solution)/shard_map/ppermute | solution.py:236
  504.0 63.9 %collective-permute-start.15 = (bf16[1182,192]{0,1:T(8,128)(2,1)}, bf16[1182,192]{0,1:T(8,128)(2,1)S(1)}, u32[]{:S(2)}, u32[]{:S(2)}) collective-permute-start(bf16[1182,192]{0,1:T(8,128)(2,1)} %get-tuple-element.62), channel_id=1, source_target_pairs={{0,2},{1,3},{2,0},{3,1},{4,6},{5,7},{6,4},{7,5},{8,10},{9,11},{10,... | collective-permute-start | bytes 1361672 | tf_op jit(solution)/shard_map/ppermute | solution.py:236
  509.0 65.4 %collective-permute-start.16 = (bf16[1182,192]{0,1:T(8,128)(2,1)}, bf16[1182,192]{0,1:T(8,128)(2,1)}, u32[]{:S(2)}, u32[]{:S(2)}) collective-permute-start(bf16[1182,192]{0,1:T(8,128)(2,1)} %get-tuple-element.61), channel_id=1, source_target_pairs={{0,3},{1,2},{2,1},{3,0},{4,7},{5,6},{6,5},{7,4},{8,11},{9,10},{10,... | collective-permute-start | bytes 1361672 | tf_op jit(solution)/shard_map/ppermute | solution.py:236
  509.1 74.4 %collective-permute-start.24 = (bf16[384,1152]{1,0:T(8,128)(2,1)}, bf16[384,1152]{1,0:T(8,128)(2,1)}, u32[]{:S(2)}, u32[]{:S(2)}) collective-permute-start(bf16[384,1152]{1,0:T(8,128)(2,1)} %slice.274), channel_id=1, source_target_pairs={{0,2},{1,3},{2,0},{3,1},{4,6},{5,7},{6,4},{7,5},{8,10},{9,11},{10,... | collective-permute-start | bytes 2654216 | tf_op jit(solution)/shard_map/ppermute | solution.py:236
  519.4 61.8 %collective-permute-start.26 = (bf16[384,384]{1,0:T(8,128)(2,1)}, bf16[384,384]{1,0:T(8,128)(2,1)}, u32[]{:S(2)}, u32[]{:S(2)}) collective-permute-start(bf16[384,384]{1,0:T(8,128)(2,1)} %slice.275), channel_id=1, source_target_pairs={{0,2},{1,3},{2,0},{3,1},{4,6},{5,7},{6,4},{7,5},{8,10},{9,11},{10,... | collective-permute-start | bytes 884744 | tf_op jit(solution)/shard_map/ppermute | solution.py:236
  583.2 146.2 %all-reduce.11.cloned.1.call-start = ((), (), s32[]{:S(2)}) async-start(), calls=%async_computation.3 | async-start | bytes 1769472 | tf_op jit(solution)/shard_map/psum | solution.py:334
  (79 other events, 1841.1 us)
Sparse Core Ops, SparseCore 0:
  202.3 81.4 all-reduce.4
  494.2 79.6 all-reduce.6
  583.3 66.8 all-reduce.8
  654.4 74.9 all-reduce.10

commit v2 on v1

--- a/solution.py
+++ b/solution.py
@@ -10,6 +10,8 @@
 QROWS = 208
 KROWS = 256
 STEP = 10
+ROWS = 400
+CHUNK = 512
 
 norm_epsilon = 1e-06
 beta_first = 0.9
@@ -33,10 +35,11 @@
 
 
 def attend_forward_kernel(mixed_ref, out_ref, probs_ref, wide, gathered):
-    tokens = mixed_ref.shape[0]
-    images = tokens // SEQ
-    wide[tokens - tokens % 8 :, :] = jnp.zeros((wide.shape[0] - tokens + tokens % 8, 384), f32)
-    wide[0:tokens, :] = mixed_ref[...].astype(f32)
+    rows = mixed_ref.shape[0]
+    images = rows // SEQ
+    tokens = images * SEQ
+    wide[rows:, :] = jnp.zeros((wide.shape[0] - rows, 384), f32)
+    wide[0:rows, :] = mixed_ref[...].astype(f32)
     low_lane = lax.broadcasted_iota(jnp.int32, (1, 128), 1) < HEAD_DIM
     key_lane = lax.broadcasted_iota(jnp.int32, (1, KROWS), 1) < SEQ
     for image in range(images):
@@ -60,7 +63,8 @@
             probs_ref[0, image * 2 + which] = probs
             outs.append(dot(probs, values.astype(bf16)))
         gathered[start : start + QROWS, :] = jnp.where(low_lane, outs[0], outs[1])
-    out_ref[...] = gathered[0:tokens, :].astype(bf16)
+    gathered[tokens:, :] = jnp.zeros((gathered.shape[0] - tokens, 128), f32)
+    out_ref[...] = gathered[0:rows, :].astype(bf16)
 
 
 def attend_forward(mixed):
@@ -92,11 +96,12 @@
 
 
 def attend_backward_kernel(mixed_ref, probs_ref, grad_ref, out_ref, wide, grad_wide, gathered):
-    tokens = mixed_ref.shape[0]
-    images = tokens // SEQ
-    wide[tokens - tokens % 8 :, :] = jnp.zeros((wide.shape[0] - tokens + tokens % 8, 384), f32)
-    wide[0:tokens, :] = mixed_ref[...].astype(f32)
-    grad_wide[0:tokens, :] = grad_ref[...].astype(f32)
+    token_rows = mixed_ref.shape[0]
+    images = token_rows // SEQ
+    tokens = images * SEQ
+    wide[token_rows:, :] = jnp.zeros((wide.shape[0] - token_rows, 384), f32)
+    wide[0:token_rows, :] = mixed_ref[...].astype(f32)
+    grad_wide[0:token_rows, :] = grad_ref[...].astype(f32)
     low_lane = lax.broadcasted_iota(jnp.int32, (1, 128), 1) < HEAD_DIM
     query_row = lax.broadcasted_iota(jnp.int32, (QROWS, 128), 0) < SEQ
     scale = HEAD_DIM ** (-0.5)
@@ -132,7 +137,8 @@
         gathered[rows, 0:128] = jnp.where(low_lane, grad_q0, grad_k0[:QROWS])
         gathered[rows, 128:256] = jnp.where(low_lane, grad_v0[:QROWS], grad_q1)
         gathered[rows, 256:384] = jnp.where(low_lane, grad_k1[:QROWS], grad_v1[:QROWS])
-    out_ref[...] = gathered[0:tokens, :].astype(bf16)
+    gathered[tokens:, :] = jnp.zeros((gathered.shape[0] - tokens, 384), f32)
+    out_ref[...] = gathered[0:token_rows, :].astype(bf16)
 
 
 def attend_backward(mixed, probs, grad_attended):
@@ -178,22 +184,6 @@
     return (value * phi, phi + value * density * 0.3989422804014327)
 
 
-def norm_forward(values, gain_row, shift_row):
-    center = jnp.mean(values, axis=1, keepdims=True)
-    spread = jnp.mean(values * values, axis=1, keepdims=True) - center * center
-    scaled = lax.rsqrt(spread + norm_epsilon)
-    normed = (values - center) * scaled
-    return ((normed * gain_row + shift_row).astype(bf16), normed, scaled)
-
-
-def norm_backward(grad_normed, normed, scaled, gain_row):
-    local_grad = grad_normed * gain_row
-    first = jnp.mean(local_grad, axis=1, keepdims=True)
-    second = jnp.mean(local_grad * normed, axis=1, keepdims=True)
-    grad_values = scaled * (local_grad - first - normed * second)
-    return (grad_values, jnp.sum(grad_normed * normed, axis=0), jnp.sum(grad_normed, axis=0))
-
-
 def adamw_update(weight, gradient, first_old, second_old, rate_value, decay_value):
     first_new = beta_first * first_old + (1.0 - beta_first) * gradient
     second_new = beta_second * second_old + (1.0 - beta_second) * (gradient * gradient)
@@ -203,6 +193,284 @@
         first_hat / (jnp.sqrt(second_hat) + adam_epsilon) + decay_value * weight
     )
     return (moved, first_new, second_new)
+
+
+def norm_rows(values):
+    center = jnp.mean(values, axis=1, keepdims=True)
+    spread = jnp.mean(values * values, axis=1, keepdims=True) - center * center
+    scaled = lax.rsqrt(spread + norm_epsilon)
+    return ((values - center) * scaled, scaled)
+
+
+def norm_backward(grad_normed, normed, scaled, gain_row):
+    local_grad = grad_normed * gain_row
+    first = jnp.mean(local_grad, axis=1, keepdims=True)
+    second = jnp.mean(local_grad * normed, axis=1, keepdims=True)
+    return scaled * (local_grad - first - normed * second)
+
+
+def square(refs, rows, columns):
+    return jnp.concatenate(
+        [
+            jnp.concatenate([refs[0][rows, columns], refs[2][rows, columns]], axis=1),
+            jnp.concatenate([refs[1][rows, columns], refs[3][rows, columns]], axis=1),
+        ],
+        axis=0,
+    )
+
+
+def in_order(col, first, second):
+    return jnp.where(
+        col == 0,
+        jnp.concatenate([first, second], axis=-1),
+        jnp.concatenate([second, first], axis=-1),
+    )
+
+
+def split_features(col, array):
+    part = array.shape[-1] // 4
+    quarters = [array[..., i * part : (i + 1) * part] for i in range(4)]
+    own = [jnp.where(col == 0, quarters[2 * i], quarters[2 * i + 1]) for i in range(2)]
+    other = [jnp.where(col == 0, quarters[2 * i + 1], quarters[2 * i]) for i in range(2)]
+    return [own[0], other[0], own[1], other[1]]
+
+
+def row_block(rows, width):
+    return pl.BlockSpec((rows, width), lambda i, *_: (i, 0))
+
+
+def resident(array):
+    zeros = (0,) * array.ndim
+    return pl.BlockSpec(array.shape, lambda i, *_: zeros)
+
+
+def row_call(kernel, place, tokens, by_row, whole, by_row_out, whole_out, flops, exps, name):
+    steps = -(-tokens // ROWS)
+    out_specs = [row_block(ROWS, shape.shape[1]) for shape in by_row_out]
+    out_specs += [resident(shape) for shape in whole_out]
+    size = sum(a.size * a.dtype.itemsize for a in [*by_row, *whole, *by_row_out, *whole_out])
+    return pl.pallas_call(
+        kernel,
+        grid_spec=pltpu.PrefetchScalarGridSpec(
+            num_scalar_prefetch=1,
+            grid=(steps,),
+            in_specs=[row_block(ROWS, a.shape[1]) for a in by_row] + [resident(a) for a in whole],
+            out_specs=out_specs,
+        ),
+        out_shape=[*by_row_out, *whole_out],
+        compiler_params=pltpu.CompilerParams(vmem_limit_bytes=54 * 2**20),
+        cost_estimate=pl.CostEstimate(flops=flops, bytes_accessed=size, transcendentals=exps),
+        name=name,
+    )(place, *by_row, *whole)
+
+
+def qkv_kernel(tokens, place, *refs):
+    parts, params, weights = refs[:4], refs[4], refs[5:9]
+    resid_ref, h_ref, mixed_ref = refs[9:]
+    col = place[0]
+    row = lax.broadcasted_iota(jnp.int32, (ROWS, 1), 0) + pl.program_id(0) * ROWS
+    half = [in_order(col, parts[2 * i][...].astype(f32), parts[2 * i + 1][...].astype(f32)) for i in range(2)]
+    resid = jnp.where(row < tokens, jnp.concatenate(half, axis=1), 0.0)
+    resid_ref[...] = resid.astype(bf16)
+    normed, _ = norm_rows(resid)
+    h = (normed * params[0:1, :] + params[1:2, :]).astype(bf16)
+    h_ref[...] = h
+    width = weights[0].shape[1]
+    for side in range(2):
+        for start in range(0, width, 384):
+            columns = slice(start, start + 384)
+            block = jnp.concatenate(
+                [weights[2 * side][:, columns], weights[2 * side + 1][:, columns]], axis=0
+            )
+            at = side * width + start
+            mixed_ref[:, at : at + 384] = dot(h, block).astype(bf16)
+
+
+def qkv_forward(place, parts, params, weights):
+    tokens = parts[0].shape[0]
+    padded = -(-tokens // ROWS) * ROWS
+    width, mixed_width = 4 * parts[0].shape[1], 2 * weights[0].shape[1]
+    return row_call(
+        lambda *refs: qkv_kernel(tokens, *refs),
+        place,
+        tokens,
+        parts,
+        [params, *weights],
+        [jax.ShapeDtypeStruct((padded, w), bf16) for w in (width, width, mixed_width)],
+        [],
+        2 * padded * width * mixed_width,
+        0,
+        "norm_qkv",
+    )
+
+
+def block_kernel(place, *refs):
+    resid_ref, attended_ref, grad_ref, params = refs[:4]
+    proj, expand, contract = refs[4:8], refs[8:12], refs[12:16]
+    out_parts = refs[16:20]
+    h_ref, hidden_ref, pre_ref, middle_ref, branch_ref, attended_grad_ref, sums_ref = refs[20:]
+    col = place[0]
+    whole = slice(None)
+    proj_low = square([proj[0], proj[2], proj[1], proj[3]], whole, whole)
+    middle = resid_ref[...].astype(f32) + dot(attended_ref[...], proj_low)
+    normed, scaled = norm_rows(middle)
+    h = (normed * params[2:3, :] + params[3:4, :]).astype(bf16)
+    h_ref[...] = h
+    grad = grad_ref[...]
+    half = expand[0].shape[1]
+    output = middle
+    grad_two = jnp.zeros_like(middle)
+    for side in range(2):
+        for start in range(0, half, CHUNK):
+            chunk = slice(start, start + CHUNK)
+            expand_low = jnp.concatenate(
+                [expand[2 * side][:, chunk], expand[2 * side + 1][:, chunk]], axis=0
+            )
+            contract_low = jnp.concatenate(
+                [contract[2 * side][chunk, :], contract[2 * side + 1][chunk, :]], axis=1
+            )
+            value, slope = gelu_and_slope(dot(h, expand_low))
+            hidden = value.astype(bf16)
+            grad_pre = (dot(grad, contract_low, ((1,), (1,))) * slope).astype(bf16)
+            at = side * half + start
+            hidden_ref[:, at : at + CHUNK] = hidden
+            pre_ref[:, at : at + CHUNK] = grad_pre
+            output = output + dot(hidden, contract_low)
+            grad_two = grad_two + dot(grad_pre, expand_low, ((1,), (1,)))
+    for part_ref, part in zip(out_parts, split_features(col, output)):
+        part_ref[...] = part.astype(bf16)
+    grad_middle = grad.astype(f32) + norm_backward(grad_two, normed, scaled, params[2:3, :])
+    middle_ref[...] = grad_middle
+    branch = grad_middle.astype(bf16)
+    branch_ref[...] = branch
+    attended_grad_ref[...] = dot(branch, proj_low, ((1,), (1,))).astype(bf16)
+
+    @pl.when(pl.program_id(0) == 0)
+    def _():
+        sums_ref[...] = jnp.zeros_like(sums_ref)
+
+    sums_ref[0:1, :] += jnp.sum(grad_two * normed, axis=0, keepdims=True)
+    sums_ref[1:2, :] += jnp.sum(grad_two, axis=0, keepdims=True)
+
+
+def block_middle(place, tokens, resid, attended, grad, params, proj, expand, contract):
+    padded, width = resid.shape
+    ff = 2 * expand[0].shape[1]
+    part = jax.ShapeDtypeStruct((tokens, width // 4), bf16)
+    narrow = jax.ShapeDtypeStruct((padded, width), bf16)
+    broad = jax.ShapeDtypeStruct((padded, ff), bf16)
+    return row_call(
+        block_kernel,
+        place,
+        padded,
+        [resid, attended, grad],
+        [params, *proj, *expand, *contract],
+        [part] * 4
+        + [narrow, broad, broad, jax.ShapeDtypeStruct((padded, width), f32), narrow, narrow],
+        [jax.ShapeDtypeStruct((2, width), f32)],
+        2 * padded * width * (4 * ff + 2 * width),
+        padded * ff,
+        "block_middle",
+    )
+
+
+def input_kernel(place, *refs):
+    mixed_ref, middle_ref, resid_ref, params = refs[:4]
+    weights = refs[4:8]
+    out_parts, sums_ref = refs[8:12], refs[12]
+    col = place[0]
+    width = weights[0].shape[1]
+    grad_one = None
+    for side in range(2):
+        weight = jnp.concatenate([weights[2 * side][...], weights[2 * side + 1][...]], axis=0)
+        piece = dot(mixed_ref[:, side * width : (side + 1) * width], weight, ((1,), (1,)))
+        grad_one = piece if grad_one is None else grad_one + piece
+    normed, scaled = norm_rows(resid_ref[...].astype(f32))
+    result = middle_ref[...] + norm_backward(grad_one, normed, scaled, params[0:1, :])
+    for part_ref, part in zip(out_parts, split_features(col, result)):
+        part_ref[...] = part.astype(bf16)
+
+    @pl.when(pl.program_id(0) == 0)
+    def _():
+        sums_ref[...] = jnp.zeros_like(sums_ref)
+
+    sums_ref[0:1, :] += jnp.sum(grad_one * normed, axis=0, keepdims=True)
+    sums_ref[1:2, :] += jnp.sum(grad_one, axis=0, keepdims=True)
+
+
+def input_backward(place, tokens, grad_mixed, grad_middle, resid, params, weights):
+    padded, width = resid.shape
+    part = jax.ShapeDtypeStruct((tokens, width // 4), bf16)
+    return row_call(
+        input_kernel,
+        place,
+        padded,
+        [grad_mixed, grad_middle, resid],
+        [params, *weights],
+        [part] * 4,
+        [jax.ShapeDtypeStruct((2, width), f32)],
+        2 * padded * width * grad_mixed.shape[1],
+        0,
+        "qkv_backward",
+    )
+
+
+def tokens_kernel(place, *refs):
+    parts, out_ref = refs[:4], refs[4]
+    tokens = parts[0].shape[0]
+    for block in range(4):
+        for distance in range(4):
+
+            @pl.when((place[1] ^ block) == distance)
+            def _():
+                rows = slice(block * tokens, (block + 1) * tokens)
+                out_ref[rows, :] = parts[distance][...].astype(f32)
+
+
+def tokens_apart(place, parts):
+    tokens, part = parts[0].shape
+    return pl.pallas_call(
+        tokens_kernel,
+        in_specs=[pl.BlockSpec(memory_space=pltpu.SMEM)]
+        + [pl.BlockSpec(memory_space=pltpu.VMEM)] * 4,
+        out_specs=pl.BlockSpec(memory_space=pltpu.VMEM),
+        out_shape=jax.ShapeDtypeStruct((4 * tokens, part), f32),
+        compiler_params=pltpu.CompilerParams(vmem_limit_bytes=40 * 2**20),
+        cost_estimate=pl.CostEstimate(
+            flops=0, bytes_accessed=4 * tokens * part * 6, transcendentals=0
+        ),
+        name="tokens_apart",
+    )(place, *parts)
+
+
+def adamw_kernel(place, weight, first, second, here, there, weight_out, first_out, second_out):
+    x = place[2]
+    mine = jnp.where(pl.program_id(0) // 4 == x, here[0].astype(f32), there[0].astype(f32))
+    results = adamw_update(
+        weight[...], mine, first[...], second[...], rate_matrix, decay_matrix
+    )
+    weight_out[...], first_out[...], second_out[...] = results
+
+
+def adamw_pieces(place, weight, first, second, here, there):
+    rows, width = weight.shape
+    piece = pl.BlockSpec((rows // 8, width), lambda i, place: (i, 0))
+    part = pl.BlockSpec((1, rows // 8, width), lambda i, place: ((i % 4) ^ place[3], 0, 0))
+    return pl.pallas_call(
+        adamw_kernel,
+        grid_spec=pltpu.PrefetchScalarGridSpec(
+            num_scalar_prefetch=1,
+            grid=(8,),
+            in_specs=[piece, piece, piece, part, part],
+            out_specs=[piece] * 3,
+        ),
+        out_shape=[jax.ShapeDtypeStruct((rows, width), f32)] * 3,
+        compiler_params=pltpu.CompilerParams(vmem_limit_bytes=40 * 2**20),
+        cost_estimate=pl.CostEstimate(
+            flops=20 * rows * width, bytes_accessed=28 * rows * width, transcendentals=0
+        ),
+        name="adamw_pieces",
+    )(place, weight, first, second, here, there)
 
 
 def local(
@@ -226,56 +494,38 @@
 ):
     row = lax.axis_index("row")
     col = lax.axis_index("col")
+    dp = lax.axis_index("dp")
+    n_dp = lax.axis_size("dp")
     me = 2 * row + col
+    place = jnp.stack([col, me, dp % 2, dp // 2]).astype(jnp.int32)
     tokens = tokens_in.shape[0] // 4
     part = tokens_in.shape[1]
+    padded = -(-tokens // ROWS) * ROWS
 
     def swap(array, distance):
         if distance == 0:
             return array
         return lax.ppermute(array, GROUP, [(i, i ^ distance) for i in range(4)])
 
+    def swap_dp(array, distance):
+        return lax.ppermute(array, "dp", [(i, i ^ distance) for i in range(n_dp)])
+
     def swap_row(array):
         return swap(array, 2)
 
     def swap_col(array):
         return swap(array, 1)
 
-    def in_order(first, second):
-        return jnp.where(col == 0, jnp.concatenate([first, second], -1), jnp.concatenate([second, first], -1))
-
-    def join_features(parts):
-        return jnp.concatenate([in_order(parts[0], parts[1]), in_order(parts[2], parts[3])], -1)
-
-    def tokens_together(array):
-        blocks = [
-            lax.dynamic_slice(array, ((me ^ d) * tokens, 0), (tokens, part)) for d in range(4)
-        ]
-        return join_features([swap(block, d) for d, block in enumerate(blocks)])
-
-    def split_features(array):
-        quarters = [array[..., i * part : (i + 1) * part] for i in range(4)]
-        own = [jnp.where(col == 0, quarters[2 * i], quarters[2 * i + 1]) for i in range(2)]
-        other = [jnp.where(col == 0, quarters[2 * i + 1], quarters[2 * i]) for i in range(2)]
-        return [own[0], other[0], own[1], other[1]]
-
-    def features_together(array):
-        pieces = split_features(array)
-        result = jnp.zeros((4 * tokens, part), f32)
-        for d in range(4):
-            received = swap(pieces[d].astype(bf16), d).astype(f32)
-            result = lax.dynamic_update_slice(result, received, ((me ^ d) * tokens, 0))
-        return result
-
-    def gather_row_col(weight):
-        mine = weight.astype(bf16)
-        stacked = jnp.concatenate([mine, swap_row(mine)], axis=0)
-        return jnp.concatenate([stacked, swap_col(stacked)], axis=1)
-
-    def gather_col_row(weight):
-        mine = weight.astype(bf16)
-        stacked = jnp.concatenate([mine, swap_row(mine)], axis=1)
-        return jnp.concatenate([stacked, swap_col(stacked)], axis=0)
+    def token_blocks(array):
+        return [lax.dynamic_slice(array, ((me ^ d) * tokens, 0), (tokens, part)) for d in range(4)]
+
+    def swap_all(blocks):
+        return [swap(block, d) for d, block in enumerate(blocks)]
+
+    def row_partner(mine, weight):
+        rows = weight.shape[0] // n_dp
+        piece = lax.dynamic_slice(weight, (dp * rows, 0), (rows, weight.shape[1]))
+        return lax.all_gather(swap_row(piece.astype(bf16)), "dp", axis=0, tiled=True)
 
     def reduce_row_col(left, right):
         half = right.shape[1] // 2
@@ -283,7 +533,7 @@
         away = dot(left, right[:, half:], ((0,), (0,))).astype(bf16)
         kept = dot(left, right[:, :half], ((0,), (0,)))
         total = kept + swap_col(away).astype(f32)
-        return total[:rows] + swap_row(total[rows:].astype(bf16)).astype(f32)
+        return total[:rows], swap_row(total[rows:].astype(bf16))
 
     def reduce_col_row(left, right):
         half = left.shape[1] // 2
@@ -291,68 +541,98 @@
         away = dot(left[:, half:], right, ((0,), (0,))).astype(bf16)
         kept = dot(left[:, :half], right, ((0,), (0,)))
         total = kept + swap_col(away).astype(f32)
-        return total[:, :columns] + swap_row(total[:, columns:].astype(bf16)).astype(f32)
-
-    resid_low = tokens_together(tokens_in)
-    params = join_features([swap(norm_params, d) for d in range(4)])
-    qkv_low = gather_row_col(qkv_weight)
-    proj_low = gather_col_row(proj_weight)
-    expand_low = gather_row_col(expand_weight)
-    contract_low = gather_col_row(contract_weight)
-    grad_low = tokens_together(out_grad)
-
-    resid = resid_low.astype(f32)
-    h_one, normed_one, scaled_one = norm_forward(resid, params[0], params[1])
-    mixed = dot(h_one, qkv_low).astype(bf16)
+        return total[:, :columns], swap_row(total[:, columns:].astype(bf16))
+
+    resid_parts = swap_all(token_blocks(tokens_in))
+    params = [swap(norm_params, d) for d in range(4)]
+    params = jnp.concatenate(
+        [in_order(col, params[0], params[1]), in_order(col, params[2], params[3])], axis=1
+    )
+    qkv_mine = qkv_weight.astype(bf16)
+    qkv_row = row_partner(qkv_mine, qkv_weight)
+    qkv_low = [qkv_mine, qkv_row, swap_col(qkv_mine), swap_col(qkv_row)]
+    proj_mine = proj_weight.astype(bf16)
+    proj_row = row_partner(proj_mine, proj_weight)
+    proj_low = [proj_mine, proj_row, swap_col(proj_mine), swap_col(proj_row)]
+    expand_mine = expand_weight.astype(bf16)
+    expand_row = row_partner(expand_mine, expand_weight)
+    expand_low = [expand_mine, expand_row, swap_col(expand_mine), swap_col(expand_row)]
+
+    resid_parts, contract_low, grad_blocks = lax.optimization_barrier(
+        (resid_parts, contract_weight.astype(bf16), token_blocks(out_grad))
+    )
+    contract_mine = contract_low
+    contract_row = swap_row(contract_mine)
+    contract_low = [contract_mine, contract_row, swap_col(contract_mine), swap_col(contract_row)]
+    grad_parts = swap_all(grad_blocks)
+    grad_low = jnp.concatenate(
+        [in_order(col, grad_parts[0], grad_parts[1]), in_order(col, grad_parts[2], grad_parts[3])],
+        axis=1,
+    )
+    grad_low = jnp.pad(grad_low, ((0, padded - tokens), (0, 0)))
+
+    resid, h_one, mixed = qkv_forward(place, resid_parts, params, qkv_low)
     attended, probs = attend_forward(mixed)
-    middle = resid + dot(attended, proj_low)
-    h_two, normed_two, scaled_two = norm_forward(middle, params[2], params[3])
-    gelu_value, gelu_slope = gelu_and_slope(dot(h_two, expand_low))
-    hidden = gelu_value.astype(bf16)
-    gelu_slope = gelu_slope.astype(bf16)
-    output_tokens = features_together(middle + dot(hidden, contract_low))
-
+    outs = block_middle(
+        place, tokens, resid, attended, grad_low, params, proj_low, expand_low, contract_low
+    )
+    output_parts = outs[:4]
+    h_two, hidden, grad_pre, grad_middle, grad_branch, grad_attended, sums_two = outs[4:]
     contract_grad = reduce_col_row(hidden, grad_low)
-    grad_pre = (dot(grad_low, contract_low, ((1,), (1,))) * gelu_slope.astype(f32)).astype(bf16)
     expand_grad = reduce_row_col(h_two, grad_pre)
-    grad_two = dot(grad_pre, expand_low, ((1,), (1,)))
-    middle_part, gain_two, shift_two = norm_backward(grad_two, normed_two, scaled_two, params[2])
-    grad_middle = grad_low.astype(f32) + middle_part
-    grad_branch = grad_middle.astype(bf16)
     proj_grad = reduce_col_row(attended, grad_branch)
-    grad_attended = dot(grad_branch, proj_low, ((1,), (1,))).astype(bf16)
     grad_mixed = attend_backward(mixed, probs, grad_attended)
     qkv_grad = reduce_row_col(h_one, grad_mixed)
-    grad_one = dot(grad_mixed, qkv_low, ((1,), (1,)))
-    input_part, gain_one, shift_one = norm_backward(grad_one, normed_one, scaled_one, params[0])
-    input_grad = features_together(grad_middle + input_part)
-
-    def over_dp(gradient, after):
-        gradient = gradient.astype(bf16)
-        if after is not None:
-            gradient, after = lax.optimization_barrier((gradient, after))
-        return lax.psum(gradient, "dp")
-
-    contract_sum = over_dp(contract_grad, None)
-    expand_sum = over_dp(expand_grad, contract_sum)
-    proj_sum = over_dp(proj_grad, expand_sum)
-    qkv_sum = over_dp(qkv_grad, proj_sum)
-    norm_parts = jnp.stack(
-        split_features(jnp.stack((gain_one, shift_one, gain_two, shift_two)))
-    )
-    norm_mine = norm_parts[0] + sum(swap(norm_parts[d], d) for d in range(1, 4))
-    norm_sum = lax.psum(norm_mine, "dp")
-
-    results = (output_tokens, input_grad)
+    outs = input_backward(place, tokens, grad_mixed, grad_middle, resid, params, qkv_low)
+    input_parts, sums_one = outs[:4], outs[4]
+
+    qkv_grad, output_parts, input_parts = lax.optimization_barrier(
+        (qkv_grad, output_parts, input_parts)
+    )
+
+    def over_dp(kept, received):
+        gradient = (kept + received.astype(f32)).astype(bf16)
+        if n_dp != 8:
+            return lax.psum(gradient, "dp").astype(f32)
+        rows = gradient.shape[0] // 2
+        x, z = dp % 2, dp // 2
+        away = lax.dynamic_slice_in_dim(gradient, (1 - x) * rows, rows)
+        total = lax.dynamic_slice_in_dim(gradient, x * rows, rows).astype(f32)
+        total = (total + swap_dp(away, 1).astype(f32)).astype(bf16)
+        pieces = [lax.dynamic_slice_in_dim(total, (z ^ d) * (rows // 4), rows // 4) for d in range(4)]
+        mine = pieces[0].astype(f32)
+        for d in range(1, 4):
+            mine = mine + swap_dp(pieces[d], 2 * d).astype(f32)
+        mine = mine.astype(bf16)
+        here = jnp.stack([mine] + [swap_dp(mine, 2 * d) for d in range(1, 4)])
+        return here, swap_dp(here, 1)
+
+    contract_sum = over_dp(*contract_grad)
+    expand_sum = over_dp(*expand_grad)
+    proj_sum = over_dp(*proj_grad)
+    qkv_sum = over_dp(*qkv_grad)
+    norm_parts = split_features(col, jnp.concatenate([sums_one, sums_two], axis=0))
+    norm_sum = norm_parts[0] + sum(swap(norm_parts[d], d) for d in range(1, 4))
+    if n_dp == 8:
+        for d in (1, 2, 4):
+            norm_sum = norm_sum + swap_dp(norm_sum, d)
+    else:
+        norm_sum = lax.psum(norm_sum, "dp")
+
+    results = (
+        tokens_apart(place, swap_all(output_parts)),
+        tokens_apart(place, swap_all(input_parts)),
+    )
     for weight, gradient, first, second in (
         (qkv_weight, qkv_sum, qkv_first, qkv_second),
         (proj_weight, proj_sum, proj_first, proj_second),
         (expand_weight, expand_sum, expand_first, expand_second),
         (contract_weight, contract_sum, contract_first, contract_second),
     ):
-        results += adamw_update(
-            weight, gradient.astype(f32), first, second, rate_matrix, decay_matrix
-        )
+        if n_dp == 8:
+            results += tuple(adamw_pieces(place, weight, first, second, *gradient))
+        else:
+            results += adamw_update(weight, gradient, first, second, rate_matrix, decay_matrix)
     return results + adamw_update(norm_params, norm_sum, norm_first, norm_second, rate_norm, 0.0)
 
 

time: 751 us -> 581 us (0.77)
  waiting for transfers between devices: 362 us -> 115 us
  Pallas kernels: 43.1 us -> 149 us
  matrix products: 129 us -> 33.7 us
  starting transfers between devices: 25.9 us -> 77.8 us
  blocking collectives: 19.9 us -> 67.4 us
  other arithmetic: 65 us -> 25.1 us
  local copies, waits for them, and re-layouts: 80.6 us -> 91.6 us
    psum x4 -> x0, waiting for transfers between devices: 216 us -> none  [over_dp(): return lax.psum(gradient, 'dp')]
    pallas_call x0 -> x9, Pallas kernels: none -> 106 us  [the longest x3 75.4 us: row_call(): pl.pallas_call(kernel, grid_spec=pltpu.PrefetchScalarGridSpec(num_scalar_...]
    dot_general x16 -> x8, matrix products: 129 us -> 33.7 us  [dot(): lax.dot_general(left, right, (dims, ((), ())), preferred_element_type=f32)]
    all_gather x0 -> x2, blocking collectives: none -> 67.4 us  [row_partner(): lax.all_gather(swap_row(piece.astype(bf16)), 'dp', axis=0, tiled=True)]
    ppermute x34 -> x38, waiting for transfers between devices: 146 us -> 79.2 us  [swap(): return lax.ppermute(array, GROUP, [(i, i ^ distance) for i in range(4)])]
    ppermute x0 -> x35, starting transfers between devices: none -> 51.4 us  [swap_dp(): return lax.ppermute(array, 'dp', [(i, i ^ distance) for i in range(n_dp)])]
    dynamic_update_slice x8 -> x0, local copies, waits for them, and re-layouts: 48.8 us -> none  [features_together(): result = lax.dynamic_update_slice(result, received, ((me ^ d) * tokens, 0))]
    ppermute x0 -> x35, waiting for transfers between devices: none -> 35.7 us  [swap_dp(): return lax.ppermute(array, 'dp', [(i, i ^ distance) for i in range(n_dp)])]
  transfers between devices with their start and end apart: 38 -> 74, of which waited for: 14 -> 15; matrix products, arithmetic and copies ran while one was open for 19% -> 20% of each run, Pallas kernels for 2% -> 16%
where the time goes in v2:
time: 581 us; the launch traced here: 575 us
  Pallas kernels  149 us (26%)
  waiting for transfers between devices  115 us (20%)
  local copies, waits for them, and re-layouts  91.6 us (16%)
  starting transfers between devices  77.8 us (13%)
  blocking collectives  67.4 us (12%)
  matrix products  33.7 us (6%)
  other arithmetic  25.1 us (4%)
  between operations  15.3 us (3%)
    ppermute x38, waiting for transfers between devices, swap(): return lax.ppermute(array, GROUP, [(i, i ^ distance) for i in range(4)])  79.2 us
    pallas_call x3, Pallas kernels, row_call(): pl.pallas_call(kernel, grid_spec=pltpu.PrefetchScalarGridSpec(num_scalar_...  75.4 us
    all_gather x2, blocking collectives, row_partner(): lax.all_gather(swap_row(piece.astype(bf16)), 'dp', axis=0, tiled=True)  67.4 us
    ppermute x35, starting transfers between devices, swap_dp(): return lax.ppermute(array, 'dp', [(i, i ^ distance) for i in range(n_dp)])  51.4 us
    unnamed x134, local copies, waits for them, and re-layouts  40.2 us
    ppermute x35, waiting for transfers between devices, swap_dp(): return lax.ppermute(array, 'dp', [(i, i ^ distance) for i in range(n_dp)])  35.7 us
    dot_general x8, matrix products, dot(): lax.dot_general(left, right, (dims, ((), ())), preferred_element_type=f32)  33.7 us
    pallas_call x4, Pallas kernels, adamw_pieces(): pl.pallas_call(adamw_kernel, grid_spec=pltpu.PrefetchScalarGridSpec(num_s...  27.8 us
  transfers between devices with their start and end apart: 74, of which 15 were waited for; matrix products, arithmetic and copies ran while one was open for 20% of the time, Pallas kernels for 16%

profile of v2, /device:TPU:0, one launch (start us, length us, event | category | flops | bytes accessed | tf_op | source)
XLA Modules:
  0.0 575.0 jit_solution(15716085891677413853)
XLA Ops:
  11.3 3.8 collective-permute-done.15
  15.8 3.7 constant_dynamic-slice_fusion.20
  33.8 9.8 %collective-permute-done.2 = bf16[1182,192]{0,1:T(8,128)(2,1)} collective-permute-done((bf16[1182,192]{0,1:T(8,128)(2,1)}, bf16[1182,192]{0,1:T(8,128)(2,1)}, u32[]{:S(2)}, u32[]{:S(2)}) %collective-permute-start.2) | collective-permute-done | bytes 453920 | tf_op jit(solution)/shard_map/ppermute | solution.py:508
  52.9 30.3 %collective-permute-done.4 = f32[4,192]{1,0:T(4,128)S(1)} collective-permute-done((f32[4,192]{1,0:T(4,128)}, f32[4,192]{1,0:T(4,128)S(1)}, u32[]{:S(2)}, u32[]{:S(2)}) %collective-permute-start.4) | collective-permute-done | bytes 3104 | tf_op jit(solution)/shard_map/ppermute | solution.py:508
  90.2 34.4 %all_gather.9.refs_7_.refs_5_ = bf16[384,1152]{1,0:T(8,128)(2,1)} all-gather(bf16[48,1152]{1,0:T(8,128)(2,1)S(1)} %collective-permute-done.6), channel_id=1, replica_groups=mesh['dp'=8,'row'=2,'col'=2] {'dp'}, dimensions={0}, use_global_device_ids=true | all-gather | bytes 995328 | tf_op jit(solution)/shard_map/all_gather | solution.py:528
  124.7 33.0 %all_gather.10.refs_5_ = bf16[384,384]{1,0:T(8,128)(2,1)} all-gather(bf16[48,384]{1,0:T(8,128)(2,1)S(1)} %collective-permute-done.12), channel_id=1, replica_groups=mesh['dp'=8,'row'=2,'col'=2] {'dp'}, dimensions={0}, use_global_device_ids=true | all-gather | bytes 331776 | tf_op jit(solution)/shard_map/all_gather | solution.py:528
  179.1 13.9 %norm_qkv.1 = (bf16[1200,768]{1,0:T(8,128)(2,1)}, bf16[1200,768]{1,0:T(8,128)(2,1)}, bf16[1200,2304]{1,0:T(8,128)(2,1)}) custom-call(s32[4]{0:T(128)} %pad_add_fusion.refs_0_.place, bf16[1182,192]{1,0:T(8,128)(2,1)} %copy.69.refs_1_, bf16[1182,192]{1,0:T(8,128)(2,1)} %copy.46.refs_2_, bf16[1182,192]{1,0:T(8,128)(2,1)} %copy.47.refs_3_, ...), custom_call_target="tpu_custom_call" | custom-call | flops 4246732800 | bytes 14582784 | tf_op jit(solution)/shard_map/norm_qkv/pallas_call | solution.py:252
  195.5 17.7 %attend_forward.1 = (bf16[1200,768]{1,0:T(8,128)(2,1)S(1)}, bf16[6,12,208,256]{3,2,1,0:T(8,128)(2,1)}) custom-call(bf16[1200,2304]{1,0:T(8,128)(2,1)S(1)} %copy-done.7), custom_call_target="tpu_custom_call" | custom-call | flops 1962934272 | bytes 8294400 | tf_op jit(solution)/shard_map/attend_forward/pallas_call | solution.py:75
  215.2 48.2 %block_middle.1 = (bf16[1182,192]{1,0:T(8,128)(2,1)}, bf16[1182,192]{1,0:T(8,128)(2,1)}, bf16[1182,192]{1,0:T(8,128)(2,1)}, bf16[1182,192]{1,0:T(8,128)(2,1)}, b...) custom-call(s32[4]{0:T(128)} %pad_add_fusion.refs_0_.place, ...), custom_call_target="tpu_custom_call" | custom-call | flops 25480396800 | bytes 41942016 | tf_op jit(solution)/shard_map/block_middle/pallas_call | solution.py:252
  269.1 25.9 %attend_backward.1.refs_0_ = bf16[1200,2304]{1,0:T(8,128)(2,1)S(1)} custom-call(bf16[1200,2304]{1,0:T(8,128)(2,1)S(1)} %copy-done.8, bf16[6,12,208,256]{3,2,1,0:T(8,128)(2,1)} %get-tuple-element.75.probs_ref, bf16[1200,768]{1,0:T(8,128)(2,1)S(1)} %copy-done.21), custom_call_target="tpu_custom_call" | custom-call | flops 3925868544 | bytes 11059200 | tf_op jit(solution)/shard_map/attend_backward/pallas_call | solution.py:149
  295.0 3.9 convolution_convert_fusion
  301.2 13.4 %qkv_backward.1 = (bf16[1182,192]{1,0:T(8,128)(2,1)}, bf16[1182,192]{1,0:T(8,128)(2,1)}, bf16[1182,192]{1,0:T(8,128)(2,1)}, bf16[1182,192]{1,0:T(8,128)(2,1)}, f32[2,768]{1,0:T(2,128)}) custom-call(s32[4]{0:T(128)} %pad_add_fusion.refs_0_.place, bf16[1200,2304]{1,0:T(8,128)(2,1)} %copy-done.6, f32[1200,768]{1,0:T(8,128)} %get-tuple-element.88.refs_1_, ...), custom_call_target="tpu_custom_call" | custom-call | flops 4246732800 | bytes 16432128 | tf_op jit(solution)/shard_map/qkv_backward/pallas_call | solution.py:252
  328.2 5.8 %fusion.8 = bf16[768,1536]{1,0:T(8,128)(2,1)S(1)} fusion(bf16[1200,768]{1,0:T(8,128)(2,1)S(1)} %copy-done.41, bf16[1200,3072]{1,0:T(8,128)(2,1)} %get-tuple-element.111), kind=kOutput, calls=%fused_computation.12 | convolution fusion | flops 2832334848 | bytes 7888896 | tf_op jit(solution)/shard_map/dot_general | solution.py:30
  339.6 4.3 convolution_add_fusion
  345.6 5.5 fusion.11
  353.5 11.4 %collective-permute-done.22 = bf16[384,1152]{1,0:T(8,128)(2,1)S(1)} collective-permute-done((bf16[384,1152]{1,0:T(8,128)(2,1)S(1)}, bf16[384,1152]{1,0:T(8,128)(2,1)S(1)}, u32[]{:S(2)}, u32[]{:S(2)}) %collective-permute-start.22) | collective-permute-done | bytes 884768 | tf_op jit(solution)/shard_map/ppermute | solution.py:508
  367.0 5.2 convert_add_fusion.1
  381.8 5.4 convert_add_fusion
  409.3 18.9 %collective-permute-done.58 = bf16[1536,384]{1,0:T(8,128)(2,1)S(1)} collective-permute-done((bf16[1536,384]{1,0:T(8,128)(2,1)}, bf16[1536,384]{1,0:T(8,128)(2,1)S(1)}, u32[]{:S(2)}, u32[]{:S(2)}) %collective-permute-start.58) | collective-permute-done | bytes 1179680 | tf_op jit(solution)/shard_map/ppermute | solution.py:508
  433.4 6.0 %collective-permute-done.59 = bf16[768,384]{1,0:T(8,128)(2,1)S(1)} collective-permute-done((bf16[768,384]{1,0:T(8,128)(2,1)S(1)}, bf16[768,384]{1,0:T(8,128)(2,1)S(1)}, u32[]{:S(2)}, u32[]{:S(2)}) %collective-permute-start.59) | collective-permute-done | bytes 589856 | tf_op jit(solution)/shard_map/ppermute | solution.py:511
  447.7 4.0 collective-permute-done.62
  454.0 8.6 %collective-permute-done.61 = bf16[192,384]{1,0:T(8,128)(2,1)S(1)} collective-permute-done((bf16[192,384]{1,0:T(8,128)(2,1)S(1)}, bf16[192,384]{1,0:T(8,128)(2,1)S(1)}, u32[]{:S(2)}, u32[]{:S(2)}) %collective-permute-start.61) | collective-permute-done | bytes 147488 | tf_op jit(solution)/shard_map/ppermute | solution.py:511
  467.3 7.7 %collective-permute-done.54 = bf16[48,1536]{1,0:T(8,128)(2,1)S(1)} collective-permute-done((bf16[48,1536]{1,0:T(8,128)(2,1)S(1)}, bf16[48,1536]{1,0:T(8,128)(2,1)S(1)}, u32[]{:S(2)}, u32[]{:S(2)}) %collective-permute-start.54) | collective-permute-done | bytes 147488 | tf_op jit(solution)/shard_map/ppermute | solution.py:511
  475.1 3.7 collective-permute-start.63
  479.6 7.3 %collective-permute-done.64 = bf16[192,384]{1,0:T(8,128)(2,1)S(1)} collective-permute-done((bf16[192,384]{1,0:T(8,128)(2,1)S(1)}, bf16[192,384]{1,0:T(8,128)(2,1)S(1)}, u32[]{:S(2)}, u32[]{:S(2)}) %collective-permute-start.64) | collective-permute-done | bytes 147488 | tf_op jit(solution)/shard_map/ppermute | solution.py:511
  487.0 3.7 collective-permute-start.33
  498.7 3.6 adamw_pieces.5
  515.1 5.7 copy.67
  533.4 5.7 copy.68
  543.5 7.7 %adamw_pieces.4 = (f32[384,1152]{1,0:T(8,128)}, f32[384,1152]{1,0:T(8,128)}, f32[384,1152]{1,0:T(8,128)}) custom-call(s32[4]{0:T(128)S(1)} %copy-done.33, f32[384,1152]{1,0:T(8,128)S(1)} %copy-done.5, f32[384,1152]{1,0:T(8,128)S(1)} %copy-done.22, f32[384,1152]{1,0:T(8,128)S(1)} %copy-done.23, bf16[4,48,1152]{2,1,0:T(8,128)(2,1)} %pad_maximum_fusion.2.here, ...), custom_call_target="tpu_custom_call" | custom-call | flops 8847360 | bytes 12386304 | tf_op jit(solution)/shard_map/adamw_pieces/pallas_call | solution.py:459
  551.3 8.4 %adamw_pieces.6 = (f32[384,1536]{1,0:T(8,128)}, f32[384,1536]{1,0:T(8,128)}, f32[384,1536]{1,0:T(8,128)}) custom-call(s32[4]{0:T(128)S(1)} %copy-done.33, f32[384,1536]{1,0:T(8,128)S(1)} %copy-done.2, f32[384,1536]{1,0:T(8,128)S(1)} %copy-done.14, f32[384,1536]{1,0:T(8,128)S(1)} %copy-done.15, bf16[4,48,1536]{2,1,0:T(8,128)(2,1)S(1)} %pad_maximum_fusion.here, ...), custom_call_target="tpu_custom_call" | custom-call | flops 11796480 | bytes 16515072 | tf_op jit(solution)/shard_map/adamw_pieces/pallas_call | solution.py:459
  559.7 8.2 %adamw_pieces.7 = (f32[1536,384]{1,0:T(8,128)}, f32[1536,384]{1,0:T(8,128)}, f32[1536,384]{1,0:T(8,128)}) custom-call(s32[4]{0:T(128)S(1)} %copy-done.33, f32[1536,384]{1,0:T(8,128)S(1)} %copy-done.4, f32[1536,384]{1,0:T(8,128)S(1)} %copy-done.16, f32[1536,384]{1,0:T(8,128)S(1)} %copy-done.17, bf16[4,192,384]{2,1,0:T(8,128)(2,1)} %pad_maximum_fusion.1.here, ...), custom_call_target="tpu_custom_call" | custom-call | flops 11796480 | bytes 16515072 | tf_op jit(solution)/shard_map/adamw_pieces/pallas_call | solution.py:459
  (344 shorter events, 184.9 us)
Async XLA Ops:
  7.2 161.5 %all-gather.2.cloned.1.call-start = ((), (), s32[]{:S(2)}) async-start(), calls=%async_computation | async-start | bytes 1327104 | tf_op jit(solution)/shard_map/all_gather | solution.py:528
  21.4 31.1 %collective-permute-start.5 = (f32[4,192]{1,0:T(4,128)}, f32[4,192]{1,0:T(4,128)}, u32[]{:S(2)}, u32[]{:S(2)}) collective-permute-start(f32[4,192]{1,0:T(4,128)} %param.23), channel_id=1, source_target_pairs={{0,3},{1,2},{2,1},{3,0},{4,7},{5,6},{6,5},{7,4},{8,11},{9,10},{10,... | collective-permute-start | bytes 9224 | tf_op jit(solution)/shard_map/ppermute | solution.py:508
  23.0 27.0 %collective-permute-start.3 = (f32[4,192]{1,0:T(4,128)}, f32[4,192]{1,0:T(4,128)}, u32[]{:S(2)}, u32[]{:S(2)}) collective-permute-start(f32[4,192]{1,0:T(4,128)} %param.23), channel_id=1, source_target_pairs={{0,1},{1,0},{2,3},{3,2},{4,5},{5,4},{6,7},{7,6},{8,9},{9,8},{10,11... | collective-permute-start | bytes 9224 | tf_op jit(solution)/shard_map/ppermute | solution.py:508
  31.3 136.8 %collective-permute-start.7 = (bf16[384,1152]{1,0:T(8,128)(2,1)}, bf16[384,1152]{1,0:T(8,128)(2,1)}, u32[]{:S(2)}, u32[]{:S(2)}) collective-permute-start(bf16[384,1152]{1,0:T(8,128)(2,1)} %convert_element_type.172.refs_6_.refs_4_), channel_id=1, source_target_pairs={{0,1},{1,0},{2,3},{3,2},{4,5},{5,4},{6,7},{7,6},{8,9},{9,8},{10,11... | collective-permute-start | bytes 2654216 | tf_op jit(solution)/shard_map/ppermute | solution.py:508
  43.6 125.0 %collective-permute-start.18 = (bf16[1536,384]{1,0:T(8,128)(2,1)}, bf16[1536,384]{1,0:T(8,128)(2,1)}, u32[]{:S(2)}, u32[]{:S(2)}) collective-permute-start(bf16[1536,384]{1,0:T(8,128)(2,1)} %convert_element_type.171.refs_12_), channel_id=1, source_target_pairs={{0,2},{1,3},{2,0},{3,1},{4,6},{5,7},{6,4},{7,5},{8,10},{9,11},{10,... | collective-permute-start | bytes 3538952 | tf_op jit(solution)/shard_map/ppermute | solution.py:508
  46.9 42.8 %collective-permute-start.11 = (bf16[1182,192]{0,1:T(8,128)(2,1)}, bf16[1182,192]{0,1:T(8,128)(2,1)}, u32[]{:S(2)}, u32[]{:S(2)}) collective-permute-start(bf16[1182,192]{0,1:T(8,128)(2,1)} %get-tuple-element.81), channel_id=1, source_target_pairs={{0,3},{1,2},{2,1},{3,0},{4,7},{5,6},{6,5},{7,4},{8,11},{9,10},{10,... | collective-permute-start | bytes 1361672 | tf_op jit(solution)/shard_map/ppermute | solution.py:508
  50.0 33.2 %collective-permute-start.4 = (f32[4,192]{1,0:T(4,128)}, f32[4,192]{1,0:T(4,128)S(1)}, u32[]{:S(2)}, u32[]{:S(2)}) collective-permute-start(f32[4,192]{1,0:T(4,128)} %param.23), channel_id=1, source_target_pairs={{0,2},{1,3},{2,0},{3,1},{4,6},{5,7},{6,4},{7,5},{8,10},{9,11},{10,... | collective-permute-start | bytes 9224 | tf_op jit(solution)/shard_map/ppermute | solution.py:508
  52.4 37.3 %collective-permute-start.6 = (bf16[48,1152]{1,0:T(8,128)(2,1)}, bf16[48,1152]{1,0:T(8,128)(2,1)S(1)}, u32[]{:S(2)}, u32[]{:S(2)}) collective-permute-start(bf16[48,1152]{1,0:T(8,128)(2,1)} %dynamic-slice_convert_fusion.1), channel_id=1, source_target_pairs={{0,2},{1,3},{2,0},{3,1},{4,6},{5,7},{6,4},{7,5},{8,10},{9,11},{10,... | collective-permute-start | bytes 331784 | tf_op jit(solution)/shard_map/ppermute | solution.py:508
  87.4 37.3 %collective-permute-start.10 = (bf16[1182,192]{0,1:T(8,128)(2,1)}, bf16[1182,192]{0,1:T(8,128)(2,1)}, u32[]{:S(2)}, u32[]{:S(2)}) collective-permute-start(bf16[1182,192]{0,1:T(8,128)(2,1)} %get-tuple-element.80), channel_id=1, source_target_pairs={{0,2},{1,3},{2,0},{3,1},{4,6},{5,7},{6,4},{7,5},{8,10},{9,11},{10,... | collective-permute-start | bytes 1361672 | tf_op jit(solution)/shard_map/ppermute | solution.py:508
  89.7 78.4 %collective-permute-start.13 = (bf16[384,384]{1,0:T(8,128)(2,1)}, bf16[384,384]{1,0:T(8,128)(2,1)}, u32[]{:S(2)}, u32[]{:S(2)}) collective-permute-start(bf16[384,384]{1,0:T(8,128)(2,1)} %convert_element_type.174.refs_4_), channel_id=1, source_target_pairs={{0,1},{1,0},{2,3},{3,2},{4,5},{5,4},{6,7},{7,6},{8,9},{9,8},{10,11... | collective-permute-start | bytes 884744 | tf_op jit(solution)/shard_map/ppermute | solution.py:508
  89.7 79.0 %collective-permute-start.9 = (bf16[1182,192]{0,1:T(8,128)(2,1)}, bf16[1182,192]{0,1:T(8,128)(2,1)}, u32[]{:S(2)}, u32[]{:S(2)}) collective-permute-start(bf16[1182,192]{0,1:T(8,128)(2,1)} %get-tuple-element.79), channel_id=1, source_target_pairs={{0,1},{1,0},{2,3},{3,2},{4,5},{5,4},{6,7},{7,6},{8,9},{9,8},{10,11... | collective-permute-start | bytes 1361672 | tf_op jit(solution)/shard_map/ppermute | solution.py:508
  124.7 54.3 %collective-permute-start.8 = (bf16[384,1152]{1,0:T(8,128)(2,1)}, bf16[384,1152]{1,0:T(8,128)(2,1)}, u32[]{:S(2)}, u32[]{:S(2)}) collective-permute-start(bf16[384,1152]{1,0:T(8,128)(2,1)} %all_gather.9.refs_7_.refs_5_), channel_id=1, source_target_pairs={{0,1},{1,0},{2,3},{3,2},{4,5},{5,4},{6,7},{7,6},{8,9},{9,8},{10,11... | collective-permute-start | bytes 2654216 | tf_op jit(solution)/shard_map/ppermute | solution.py:508
  168.1 46.4 %collective-permute-start.16 = (bf16[384,1536]{1,0:T(8,128)(2,1)}, bf16[384,1536]{1,0:T(8,128)(2,1)}, u32[]{:S(2)}, u32[]{:S(2)}) collective-permute-start(bf16[384,1536]{1,0:T(8,128)(2,1)} %convert_element_type.176.refs_8_), channel_id=1, source_target_pairs={{0,1},{1,0},{2,3},{3,2},{4,5},{5,4},{6,7},{7,6},{8,9},{9,8},{10,11... | collective-permute-start | bytes 3538952 | tf_op jit(solution)/shard_map/ppermute | solution.py:508
  168.1 46.4 %collective-permute-start.19 = (bf16[1536,384]{1,0:T(8,128)(2,1)}, bf16[1536,384]{1,0:T(8,128)(2,1)}, u32[]{:S(2)}, u32[]{:S(2)}) collective-permute-start(bf16[1536,384]{1,0:T(8,128)(2,1)} %convert_element_type.171.refs_12_), channel_id=1, source_target_pairs={{0,1},{1,0},{2,3},{3,2},{4,5},{5,4},{6,7},{7,6},{8,9},{9,8},{10,11... | collective-permute-start | bytes 3538952 | tf_op jit(solution)/shard_map/ppermute | solution.py:508
  168.6 45.9 %collective-permute-start.20 = (bf16[1536,384]{1,0:T(8,128)(2,1)}, bf16[1536,384]{1,0:T(8,128)(2,1)}, u32[]{:S(2)}, u32[]{:S(2)}) collective-permute-start(bf16[1536,384]{1,0:T(8,128)(2,1)} %collective-permute-done.18.refs_13_), channel_id=1, source_target_pairs={{0,1},{1,0},{2,3},{3,2},{4,5},{5,4},{6,7},{7,6},{8,9},{9,8},{10,11... | collective-permute-start | bytes 3538952 | tf_op jit(solution)/shard_map/ppermute | solution.py:508
  168.7 45.8 %collective-permute-start.17 = (bf16[384,1536]{1,0:T(8,128)(2,1)}, bf16[384,1536]{1,0:T(8,128)(2,1)}, u32[]{:S(2)}, u32[]{:S(2)}) collective-permute-start(bf16[384,1536]{1,0:T(8,128)(2,1)} %all-gather.2.cloned.1.call-done.refs_9_), channel_id=1, source_target_pairs={{0,1},{1,0},{2,3},{3,2},{4,5},{5,4},{6,7},{7,6},{8,9},{9,8},{10,11... | collective-permute-start | bytes 3538952 | tf_op jit(solution)/shard_map/ppermute | solution.py:508
  179.0 35.5 %collective-permute-start.14 = (bf16[384,384]{1,0:T(8,128)(2,1)S(1)}, bf16[384,384]{1,0:T(8,128)(2,1)S(1)}, u32[]{:S(2)}, u32[]{:S(2)}) collective-permute-start(bf16[384,384]{1,0:T(8,128)(2,1)S(1)} %copy-done.50), channel_id=1, source_target_pairs={{0,1},{1,0},{2,3},{3,2},{4,5},{5,4},{6,7},{7,6},{8,9},{9,8},{10,11... | collective-permute-start | bytes 884744 | tf_op jit(solution)/shard_map/ppermute | solution.py:508
  266.0 33.0 %collective-permute-start.37 = (bf16[384,768]{1,0:T(8,128)(2,1)S(1)}, bf16[384,768]{1,0:T(8,128)(2,1)S(1)}, u32[]{:S(2)}, u32[]{:S(2)}) collective-permute-start(bf16[384,768]{1,0:T(8,128)(2,1)S(1)} %convolution_convert_fusion.1), channel_id=1, source_target_pairs={{0,1},{1,0},{2,3},{3,2},{4,5},{5,4},{6,7},{7,6},{8,9},{9,8},{10,11... | collective-permute-start | bytes 1769480 | tf_op jit(solution)/shard_map/ppermute | solution.py:508
  298.9 39.3 %collective-permute-start.21 = (bf16[768,1152]{1,0:T(8,128)(2,1)}, bf16[768,1152]{1,0:T(8,128)(2,1)}, u32[]{:S(2)}, u32[]{:S(2)}) collective-permute-start(bf16[768,1152]{1,0:T(8,128)(2,1)} %convolution_convert_fusion), channel_id=1, source_target_pairs={{0,1},{1,0},{2,3},{3,2},{4,5},{5,4},{6,7},{7,6},{8,9},{9,8},{10,11... | collective-permute-start | bytes 5308424 | tf_op jit(solution)/shard_map/ppermute | solution.py:508
  334.0 33.0 %collective-permute-start.47 = (bf16[768,1536]{1,0:T(8,128)(2,1)S(1)}, bf16[768,1536]{1,0:T(8,128)(2,1)S(1)}, u32[]{:S(2)}, u32[]{:S(2)}) collective-permute-start(bf16[768,1536]{1,0:T(8,128)(2,1)S(1)} %fusion.8), channel_id=1, source_target_pairs={{0,1},{1,0},{2,3},{3,2},{4,5},{5,4},{6,7},{7,6},{8,9},{9,8},{10,11... | collective-permute-start | bytes 7077896 | tf_op jit(solution)/shard_map/ppermute | solution.py:508
  351.1 28.9 %collective-permute-start.57 = (bf16[1536,768]{1,0:T(8,128)(2,1)S(1)}, bf16[1536,768]{1,0:T(8,128)(2,1)S(1)}, u32[]{:S(2)}, u32[]{:S(2)}) collective-permute-start(bf16[1536,768]{1,0:T(8,128)(2,1)S(1)} %fusion.11), channel_id=1, source_target_pairs={{0,1},{1,0},{2,3},{3,2},{4,5},{5,4},{6,7},{7,6},{8,9},{9,8},{10,11... | collective-permute-start | bytes 7077896 | tf_op jit(solution)/shard_map/ppermute | solution.py:508
  351.2 90.1 %collective-permute-start.72 = (f32[4,192]{1,0:T(4,128)S(1)}, f32[4,192]{1,0:T(4,128)S(1)}, u32[]{:S(2)}, u32[]{:S(2)}) collective-permute-start(f32[4,192]{1,0:T(4,128)S(1)} %add.235), channel_id=1, source_target_pairs={{0,16},{4,20},{8,24},{12,28},{16,0},{20,4},{24,8},{28,12},{1,17},{... | collective-permute-start | bytes 9224 | tf_op jit(solution)/shard_map/ppermute | solution.py:511
  375.1 31.4 %collective-permute-start.48 = (bf16[384,1536]{1,0:T(8,128)(2,1)}, bf16[384,1536]{1,0:T(8,128)(2,1)}, u32[]{:S(2)}, u32[]{:S(2)}) collective-permute-start(bf16[384,1536]{1,0:T(8,128)(2,1)} %slice.176), channel_id=1, source_target_pairs={{0,2},{1,3},{2,0},{3,1},{4,6},{5,7},{6,4},{7,5},{8,10},{9,11},{10,... | collective-permute-start | bytes 3538952 | tf_op jit(solution)/shard_map/ppermute | solution.py:508
  377.4 25.5 %collective-permute-start.32 = (bf16[48,1152]{1,0:T(8,128)(2,1)}, bf16[48,1152]{1,0:T(8,128)(2,1)}, u32[]{:S(2)}, u32[]{:S(2)}) collective-permute-start(bf16[48,1152]{1,0:T(8,128)(2,1)} %get-tuple-element.173), channel_id=1, source_target_pairs={{0,24},{4,28},{8,16},{12,20},{16,8},{20,12},{24,0},{28,4},{1,25},{... | collective-permute-start | bytes 331784 | tf_op jit(solution)/shard_map/ppermute | solution.py:511
  402.9 38.5 %collective-permute-start.46 = (bf16[4,48,384]{2,1,0:T(8,128)(2,1)S(1)}, bf16[4,48,384]{2,1,0:T(8,128)(2,1)S(1)}, u32[]{:S(2)}, u32[]{:S(2)}) collective-permute-start(bf16[4,48,384]{2,1,0:T(8,128)(2,1)S(1)} %pad_maximum_fusion.3.here), channel_id=1, source_target_pairs={{0,4},{4,0},{8,12},{12,8},{16,20},{20,16},{24,28},{28,24},{1,5},{5... | collective-permute-start | bytes 442376 | tf_op jit(solution)/shard_map/ppermute | solution.py:511
  447.6 44.0 %collective-permute-start.25 = (bf16[1182,192]{0,1:T(8,128)(2,1)S(1)}, bf16[1182,192]{0,1:T(8,128)(2,1)S(1)}, u32[]{:S(2)}, u32[]{:S(2)}) collective-permute-start(bf16[1182,192]{0,1:T(8,128)(2,1)S(1)} %copy-done.43), channel_id=1, source_target_pairs={{0,3},{1,2},{2,1},{3,0},{4,7},{5,6},{6,5},{7,4},{8,11},{9,10},{10,... | collective-permute-start | bytes 1361672 | tf_op jit(solution)/shard_map/ppermute | solution.py:508
  466.3 30.5 %collective-permute-start.26 = (bf16[1182,192]{0,1:T(8,128)(2,1)S(1)}, bf16[1182,192]{0,1:T(8,128)(2,1)S(1)}, u32[]{:S(2)}, u32[]{:S(2)}) collective-permute-start(bf16[1182,192]{0,1:T(8,128)(2,1)S(1)} %copy-done.42), channel_id=1, source_target_pairs={{0,1},{1,0},{2,3},{3,2},{4,5},{5,4},{6,7},{7,6},{8,9},{9,8},{10,11... | collective-permute-start | bytes 1361672 | tf_op jit(solution)/shard_map/ppermute | solution.py:508
  491.6 30.5 %collective-permute-start.27 = (bf16[1182,192]{0,1:T(8,128)(2,1)}, bf16[1182,192]{0,1:T(8,128)(2,1)}, u32[]{:S(2)}, u32[]{:S(2)}) collective-permute-start(bf16[1182,192]{0,1:T(8,128)(2,1)} %copy.62), channel_id=1, source_target_pairs={{0,2},{1,3},{2,0},{3,1},{4,6},{5,7},{6,4},{7,5},{8,10},{9,11},{10,... | collective-permute-start | bytes 1361672 | tf_op jit(solution)/shard_map/ppermute | solution.py:508
  492.1 32.1 %collective-permute-start.28 = (bf16[1182,192]{0,1:T(8,128)(2,1)}, bf16[1182,192]{0,1:T(8,128)(2,1)}, u32[]{:S(2)}, u32[]{:S(2)}) collective-permute-start(bf16[1182,192]{0,1:T(8,128)(2,1)} %copy.63), channel_id=1, source_target_pairs={{0,3},{1,2},{2,1},{3,0},{4,7},{5,6},{6,5},{7,4},{8,11},{9,10},{10,... | collective-permute-start | bytes 1361672 | tf_op jit(solution)/shard_map/ppermute | solution.py:508
  494.0 57.3 %collective-permute-start.56 = (bf16[4,48,1536]{2,1,0:T(8,128)(2,1)S(1)}, bf16[4,48,1536]{2,1,0:T(8,128)(2,1)}, u32[]{:S(2)}, u32[]{:S(2)}) collective-permute-start(bf16[4,48,1536]{2,1,0:T(8,128)(2,1)S(1)} %pad_maximum_fusion.here), channel_id=1, source_target_pairs={{0,4},{4,0},{8,12},{12,8},{16,20},{20,16},{24,28},{28,24},{1,5},{5... | collective-permute-start | bytes 1769480 | tf_op jit(solution)/shard_map/ppermute | solution.py:511
  494.4 65.2 %collective-permute-start.66 = (bf16[4,192,384]{2,1,0:T(8,128)(2,1)}, bf16[4,192,384]{2,1,0:T(8,128)(2,1)}, u32[]{:S(2)}, u32[]{:S(2)}) collective-permute-start(bf16[4,192,384]{2,1,0:T(8,128)(2,1)} %pad_maximum_fusion.1.here), channel_id=1, source_target_pairs={{0,4},{4,0},{8,12},{12,8},{16,20},{20,16},{24,28},{28,24},{1,5},{5... | collective-permute-start | bytes 1769480 | tf_op jit(solution)/shard_map/ppermute | solution.py:511
  496.8 42.3 %collective-permute-start.36 = (bf16[4,48,1152]{2,1,0:T(8,128)(2,1)}, bf16[4,48,1152]{2,1,0:T(8,128)(2,1)}, u32[]{:S(2)}, u32[]{:S(2)}) collective-permute-start(bf16[4,48,1152]{2,1,0:T(8,128)(2,1)} %pad_maximum_fusion.2.here), channel_id=1, source_target_pairs={{0,4},{4,0},{8,12},{12,8},{16,20},{20,16},{24,28},{28,24},{1,5},{5... | collective-permute-start | bytes 1327112 | tf_op jit(solution)/shard_map/ppermute | solution.py:511
  (108 other events, 1511.6 us)
Sparse Core Ops, SparseCore 0:
  15.9 42.5 all-gather.1

commit v3 on v1

v3 whole, which is shorter than its diff:
```python
import jax
import jax.numpy as jnp
from jax import lax
from jax.experimental import pallas as pl
from jax.experimental.pallas import tpu as pltpu
from jax.sharding import PartitionSpec as P

HEAD_DIM = 64
SEQ = 197
QROWS = 208
KROWS = 256
STEP = 10
ROWS = 1200
BLOCK = 240
STEPS = 6
GROUPED = 2

norm_epsilon = 1e-06
beta_first = 0.9
beta_second = 0.999
adam_epsilon = 1e-08
rate_matrix = 0.1
rate_norm = 0.5
decay_matrix = 0.05

GROUP = ("row", "col")
bf16 = jnp.bfloat16
f32 = jnp.float32


def dot(left, right, dims=((1,), (0,))):
    return lax.dot_general(left, right, (dims, ((), ())), preferred_element_type=f32)


def swap_halves(block):
    return jnp.concatenate([block[:, HEAD_DIM:], block[:, :HEAD_DIM]], axis=1)


def gelu_and_slope(value):
    size = jnp.abs(value)
    density = jnp.exp(value * value * -0.5)
    t = 1.0 / (1.0 + (0.3275911 * 0.5**0.5) * size)
    series = t * (
        0.254829592
        + t * (-0.284496736 + t * (1.421413741 + t * (-1.453152027 + t * 1.061405429)))
    )
    tail = 0.5 * series * density
    phi = jnp.where(value >= 0, 1.0 - tail, tail)
    return (value * phi, phi + value * density * 0.3989422804014327)


def adamw_update(weight, gradient, first_old, second_old, rate_value, decay_value):
    first_new = beta_first * first_old + (1.0 - beta_first) * gradient
    second_new = beta_second * second_old + (1.0 - beta_second) * (gradient * gradient)
    first_hat = first_new / (1.0 - beta_first**STEP)
    second_hat = second_new / (1.0 - beta_second**STEP)
    moved = weight - rate_value * (
        first_hat / (jnp.sqrt(second_hat) + adam_epsilon) + decay_value * weight
    )
    return (moved, first_new, second_new)


def norm_rows(values):
    center = jnp.mean(values, axis=1, keepdims=True)
    spread = jnp.mean(values * values, axis=1, keepdims=True) - center * center
    scaled = lax.rsqrt(spread + norm_epsilon)
    return ((values - center) * scaled, scaled)


def norm_backward(grad_normed, normed, scaled, gain_row):
    local_grad = grad_normed * gain_row
    first = jnp.mean(local_grad, axis=1, keepdims=True)
    second = jnp.mean(local_grad * normed, axis=1, keepdims=True)
    return scaled * (local_grad - first - normed * second)


def in_order(col, first, second):
    return jnp.where(
        col == 0,
        jnp.concatenate([first, second], axis=-1),
        jnp.concatenate([second, first], axis=-1),
    )


def split_features(col, array):
    part = array.shape[-1] // 4
    quarters = [array[..., i * part : (i + 1) * part] for i in range(4)]
    own = [jnp.where(col == 0, quarters[2 * i], quarters[2 * i + 1]) for i in range(2)]
    other = [jnp.where(col == 0, quarters[2 * i + 1], quarters[2 * i]) for i in range(2)]
    return [own[0], other[0], own[1], other[1]]


def resident(array):
    zeros = (0,) * array.ndim
    return pl.BlockSpec(array.shape, lambda i, *_: zeros, pipeline_mode=pl.Buffered(1))


def column_block(rows, width):
    return pl.BlockSpec((rows, width), lambda i, *_: (0, i))


def side_blocks(rows, width, along, steps):
    def first(i, *_):
        at = jnp.minimum(i, steps // 2 - 1)
        return (0, at) if along == 1 else (at, 0)

    def second(i, *_):
        at = jnp.maximum(i - steps // 2, 0)
        return (0, at) if along == 1 else (at, 0)

    block = (rows, width)
    return [pl.BlockSpec(block, first)] * 2 + [pl.BlockSpec(block, second)] * 2


def side_weight(refs, steps, axis):
    own = jnp.concatenate([refs[0][...], refs[1][...]], axis=axis)
    other = jnp.concatenate([refs[2][...], refs[3][...]], axis=axis)
    return jnp.where(pl.program_id(0) < steps // 2, own, other)


def split_parts(col, array):
    part = array.shape[0] // 4
    quarters = [array[i * part : (i + 1) * part] for i in range(4)]
    own = [jnp.where(col == 0, quarters[2 * i], quarters[2 * i + 1]) for i in range(2)]
    other = [jnp.where(col == 0, quarters[2 * i + 1], quarters[2 * i]) for i in range(2)]
    return [own[0], other[0], own[1], other[1]]


def together_kernel(place, *refs):
    parts, out_ref = refs[:4], refs[4]
    part, tokens = parts[0].shape
    wide = [ref[...].astype(f32) for ref in parts]
    for half in range(2):
        first, second = wide[2 * half], wide[2 * half + 1]
        both = [jnp.where(place[0] == 0, first, second), jnp.where(place[0] == 0, second, first)]
        block = jnp.concatenate(both, axis=0)
        at = 2 * part * half
        out_ref[0:tokens, at : at + 2 * part] = block.T.astype(bf16)
    low = tokens - tokens % 16
    row = lax.broadcasted_iota(jnp.int32, (out_ref.shape[0] - low, 1), 0) + low
    out_ref[low:, :] = jnp.where(row < tokens, out_ref[low:, :].astype(f32), 0.0).astype(bf16)


def tokens_together(place, parts):
    part, tokens = parts[0].shape
    padded = -(-tokens // ROWS) * ROWS
    return pl.pallas_call(
        together_kernel,
        in_specs=[pl.BlockSpec(memory_space=pltpu.SMEM)]
        + [pl.BlockSpec(memory_space=pltpu.VMEM)] * 4,
        out_specs=pl.BlockSpec(memory_space=pltpu.VMEM),
        out_shape=jax.ShapeDtypeStruct((padded, 4 * part), bf16),
        compiler_params=pltpu.CompilerParams(vmem_limit_bytes=40 * 2**20),
        cost_estimate=pl.CostEstimate(
            flops=0, bytes_accessed=16 * tokens * part, transcendentals=0
        ),
        name="tokens_together",
    )(place, *parts)


def apart_kernel(place, *refs):
    parts, out_ref = refs[:4], refs[4]
    tokens = out_ref.shape[1] // 4
    for block in range(4):
        for distance in range(4):

            @pl.when((place[1] ^ block) == distance)
            def _():
                columns = slice(block * tokens, (block + 1) * tokens)
                out_ref[:, columns] = parts[distance][...].astype(f32)[:, :tokens]


def tokens_apart(place, tokens, parts):
    part = parts[0].shape[0]
    return pl.pallas_call(
        apart_kernel,
        in_specs=[pl.BlockSpec(memory_space=pltpu.SMEM)]
        + [pl.BlockSpec(memory_space=pltpu.VMEM)] * 4,
        out_specs=pl.BlockSpec(memory_space=pltpu.VMEM),
        out_shape=jax.ShapeDtypeStruct((part, 4 * tokens), f32),
        compiler_params=pltpu.CompilerParams(vmem_limit_bytes=40 * 2**20),
        cost_estimate=pl.CostEstimate(
            flops=0, bytes_accessed=4 * tokens * part * 6, transcendentals=0
        ),
        name="tokens_apart",
    )(place, *parts).T


def forward_kernel(*refs):
    resid_ref, params = refs[:2]
    weights = refs[2:6]
    h_ref, mixed_ref, out_ref, probs_ref, wide, gathered = refs[6:]
    rows = resid_ref.shape[0]
    images = rows // SEQ
    tokens = images * SEQ
    steps = pl.num_programs(0)

    @pl.when(pl.program_id(0) == 0)
    def _():
        for start in range(0, rows, BLOCK):
            block = slice(start, start + BLOCK)
            normed, _ = norm_rows(resid_ref[block, :].astype(f32))
            h_ref[block, :] = (normed * params[0:1, :] + params[1:2, :]).astype(bf16)

    weight = side_weight(weights, STEPS, 0)
    for start in range(0, rows, BLOCK):
        block = slice(start, start + BLOCK)
        mixed = dot(h_ref[block, :], weight).astype(bf16)
        mixed_ref[block, :] = mixed
        wide[block, :] = mixed.astype(f32)
    wide[rows:, :] = jnp.zeros((wide.shape[0] - rows, 384), f32)
    low_lane = lax.broadcasted_iota(jnp.int32, (1, 128), 1) < HEAD_DIM
    key_lane = lax.broadcasted_iota(jnp.int32, (1, KROWS), 1) < SEQ
    scale = HEAD_DIM ** (-0.5)
    for group in range(0, images, GROUPED):
        members = range(group, min(group + GROUPED, images))
        scores, values = [], []
        for image in members:
            start = image * SEQ
            block_a = wide[start : start + KROWS, 0:128]
            block_b = wide[start : start + KROWS, 128:256]
            block_c = wide[start : start + KROWS, 256:384]
            query_0 = jnp.where(low_lane, block_a[:QROWS] * scale, 0.0).astype(bf16)
            query_1 = jnp.where(low_lane, 0.0, block_b[:QROWS] * scale).astype(bf16)
            scores.append(dot(query_0, swap_halves(block_a).astype(bf16), ((1,), (1,))))
            scores.append(dot(query_1, swap_halves(block_c).astype(bf16), ((1,), (1,))))
            values += [block_b.astype(bf16), block_c.astype(bf16)]
        scores = [jnp.where(key_lane, score, -1e30) for score in scores]
        tops = [jnp.max(score, axis=1, keepdims=True) for score in scores]
        exponents = [jnp.exp(score - top) for score, top in zip(scores, tops)]
        totals = [jnp.sum(exponent, axis=1, keepdims=True) for exponent in exponents]
        probs = [(e * (1.0 / total)).astype(bf16) for e, total in zip(exponents, totals)]
        outs = [dot(prob, value) for prob, value in zip(probs, values)]
        for at, image in enumerate(members):
            start = image * SEQ
            probs_ref[0, image * 2] = probs[2 * at]
            probs_ref[0, image * 2 + 1] = probs[2 * at + 1]
            gathered[start : start + QROWS, :] = jnp.where(
                low_lane, outs[2 * at], outs[2 * at + 1]
            )
    gathered[tokens:, :] = jnp.zeros((gathered.shape[0] - tokens, 128), f32)
    out_ref[...] = gathered[0:rows, :].astype(bf16)


def attend_forward(resid, params, weights):
    rows, width = resid.shape
    images = rows // SEQ
    padded = -(-((images - 1) * SEQ + KROWS) // 16) * 16
    pair_probs = (STEPS, 2 * images, QROWS, KROWS)
    half_rows = weights[0].shape[0]
    return pl.pallas_call(
        forward_kernel,
        grid=(STEPS,),
        in_specs=[resident(resid), resident(params), *side_blocks(half_rows, 384, 1, STEPS)],
        out_specs=[
            pl.BlockSpec((rows, width), lambda i: (0, 0)),
            column_block(rows, 384),
            column_block(rows, 128),
            pl.BlockSpec((1, *pair_probs[1:]), lambda i: (i, 0, 0, 0)),
        ],
        out_shape=[
            jax.ShapeDtypeStruct((rows, width), bf16),
            jax.ShapeDtypeStruct((rows, STEPS * 384), bf16),
            jax.ShapeDtypeStruct((rows, STEPS * 128), bf16),
            jax.ShapeDtypeStruct(pair_probs, bf16),
        ],
        scratch_shapes=[pltpu.VMEM((padded, 384), f32), pltpu.VMEM((padded, 128), f32)],
        compiler_params=pltpu.CompilerParams(vmem_limit_bytes=54 * 2**20),
        cost_estimate=pl.CostEstimate(
            flops=20 * 10**9, bytes_accessed=rows * width * 20, transcendentals=10**6
        ),
        name="attend_forward",
    )(resid, params, *weights)


def backward_kernel(place, *refs):
    mixed_ref, probs_ref, grad_ref, middle_ref, resid_ref, params = refs[:6]
    weights = refs[6:10]
    out_ref, out_parts, sums_ref = refs[10], refs[11:15], refs[15]
    wide, grad_wide, gathered, total = refs[16:]
    rows = mixed_ref.shape[0]
    images = rows // SEQ
    tokens = images * SEQ
    wide[rows:, :] = jnp.zeros((wide.shape[0] - rows, 384), f32)
    wide[0:rows, :] = mixed_ref[...].astype(f32)
    grad_wide[0:rows, :] = grad_ref[...].astype(f32)
    low_lane = lax.broadcasted_iota(jnp.int32, (1, 128), 1) < HEAD_DIM
    query_row = lax.broadcasted_iota(jnp.int32, (QROWS, 128), 0) < SEQ
    scale = HEAD_DIM ** (-0.5)
    for group in range(0, images, GROUPED):
        members = range(group, min(group + GROUPED, images))
        grad_probs, grad_values, probs, swapped = [], [], [], []
        for image in members:
            start = image * SEQ
            block_a = wide[start : start + KROWS, 0:128]
            block_b = wide[start : start + KROWS, 128:256]
            block_c = wide[start : start + KROWS, 256:384]
            grad = jnp.where(query_row, grad_wide[start : start + QROWS, :], 0.0)
            grad_low = grad.astype(bf16)
            probs_0 = probs_ref[0, 2 * image]
            probs_1 = probs_ref[0, 2 * image + 1]
            probs += [probs_0, probs_1]
            part_0 = jnp.where(low_lane, grad, 0.0).astype(bf16)
            part_1 = jnp.where(low_lane, 0.0, grad).astype(bf16)
            grad_probs.append(dot(part_0, block_b.astype(bf16), ((1,), (1,))))
            grad_probs.append(dot(part_1, block_c.astype(bf16), ((1,), (1,))))
            grad_values.append(dot(probs_0, grad_low, ((0,), (0,))))
            grad_values.append(dot(probs_1, grad_low, ((0,), (0,))))
            swapped.append(
                [(swap_halves(block) * scale).astype(bf16) for block in (block_a, block_b, block_c)]
            )
        wide_probs = [prob.astype(f32) for prob in probs]
        inner = [
            jnp.sum(prob * grad, axis=1, keepdims=True)
            for prob, grad in zip(wide_probs, grad_probs)
        ]
        score_grads = [
            (prob * (grad - each)).astype(bf16)
            for prob, grad, each in zip(wide_probs, grad_probs, inner)
        ]
        for at, image in enumerate(members):
            start = image * SEQ
            swapped_a, swapped_b, swapped_c = swapped[at]
            score_0, score_1 = score_grads[2 * at : 2 * at + 2]
            grad_v0, grad_v1 = grad_values[2 * at : 2 * at + 2]
            grad_q0 = dot(score_0, swapped_a)
            grad_k0 = dot(score_0, swapped_a[:QROWS], ((0,), (0,)))
            grad_q1 = dot(score_1, swapped_c)
            grad_k1 = dot(score_1, swapped_b[:QROWS], ((0,), (0,)))
            block = slice(start, start + QROWS)
            gathered[block, 0:128] = jnp.where(low_lane, grad_q0, grad_k0[:QROWS])
            gathered[block, 128:256] = jnp.where(low_lane, grad_v0[:QROWS], grad_q1)
            gathered[block, 256:384] = jnp.where(low_lane, grad_k1[:QROWS], grad_v1[:QROWS])
    gathered[tokens:, :] = jnp.zeros((gathered.shape[0] - tokens, 384), f32)
    weight = side_weight(weights, STEPS, 0)
    step = pl.program_id(0)

    @pl.when(step == 0)
    def _():
        total[...] = jnp.zeros_like(total)

    for start in range(0, rows, BLOCK):
        block = slice(start, start + BLOCK)
        grad_mixed = gathered[block, :].astype(bf16)
        out_ref[block, :] = grad_mixed
        total[block, :] += dot(grad_mixed, weight, ((1,), (1,)))

    @pl.when(step == STEPS - 1)
    def _():
        gain = jnp.zeros((1, total.shape[1]), f32)
        shift = jnp.zeros((1, total.shape[1]), f32)
        for start in range(0, rows, BLOCK):
            block = slice(start, start + BLOCK)
            grad_one = total[block, :]
            normed, scaled = norm_rows(resid_ref[block, :].astype(f32))
            gain += jnp.sum(grad_one * normed, axis=0, keepdims=True)
            shift += jnp.sum(grad_one, axis=0, keepdims=True)
            total[block, :] = middle_ref[block, :] + norm_backward(
                grad_one, normed, scaled, params[0:1, :]
            )
        sums_ref[0:1, :] = gain
        sums_ref[1:2, :] = shift
        for part_ref, part in zip(out_parts, split_parts(place[0], total[...].T)):
            part_ref[...] = part.astype(bf16)


def attend_backward(place, mixed, probs, grad_attended, grad_middle, resid, params, weights):
    rows, width = resid.shape
    images = rows // SEQ
    padded = -(-((images - 1) * SEQ + KROWS) // 16) * 16
    part = jax.ShapeDtypeStruct((width // 4, rows), bf16)
    sums = jax.ShapeDtypeStruct((2, width), f32)
    whole = [pl.BlockSpec(each.shape, lambda i, *_: (0, 0)) for each in [part] * 4 + [sums]]
    return pl.pallas_call(
        backward_kernel,
        grid_spec=pltpu.PrefetchScalarGridSpec(
            num_scalar_prefetch=1,
            grid=(STEPS,),
            in_specs=[
                column_block(rows, 384),
                pl.BlockSpec((1, *probs.shape[1:]), lambda i, *_: (i, 0, 0, 0)),
                column_block(rows, 128),
                resident(grad_middle),
                resident(resid),
                resident(params),
                *side_blocks(weights[0].shape[0], 384, 1, STEPS),
            ],
            out_specs=[column_block(rows, 384), *whole],
            scratch_shapes=[
                pltpu.VMEM((padded, 384), f32),
                pltpu.VMEM((padded, 128), f32),
                pltpu.VMEM((padded, 384), f32),
                pltpu.VMEM((rows, width), f32),
            ],
        ),
        out_shape=[jax.ShapeDtypeStruct(mixed.shape, bf16), *[part] * 4, sums],
        compiler_params=pltpu.CompilerParams(vmem_limit_bytes=54 * 2**20),
        cost_estimate=pl.CostEstimate(
            flops=30 * 10**9, bytes_accessed=rows * width * 24, transcendentals=0
        ),
        name="attend_backward",
    )(place, mixed, probs, grad_attended, grad_middle, resid, params, *weights)


def block_kernel(place, *refs):
    resid_ref, attended_ref, grad_ref, params = refs[:4]
    proj, expand, contract = refs[4:8], refs[8:12], refs[12:16]
    out_parts = refs[16:20]
    h_ref, hidden_ref, pre_ref, middle_ref, attended_grad_ref, sums_ref = refs[20:26]
    middle, output, grad_two = refs[26:]
    rows = resid_ref.shape[0]
    step = pl.program_id(0)
    blocks = [slice(start, start + BLOCK) for start in range(0, rows, BLOCK)]

    def proj_low():
        own = jnp.concatenate([proj[0][...], proj[1][...]], axis=1)
        return jnp.concatenate([own, jnp.concatenate([proj[2][...], proj[3][...]], axis=1)], axis=0)

    @pl.when(step == 0)
    def _():
        weight = proj_low()
        for block in blocks:
            value = resid_ref[block, :].astype(f32) + dot(attended_ref[block, :], weight)
            middle[block, :] = value
            output[block, :] = value
            grad_two[block, :] = jnp.zeros_like(value)
            normed, _ = norm_rows(value)
            h_ref[block, :] = (normed * params[2:3, :] + params[3:4, :]).astype(bf16)

    expand_low = side_weight(expand, STEPS, 0)
    contract_low = side_weight(contract, STEPS, 1)

    def products(block):
        return (
            dot(h_ref[block, :], expand_low),
            dot(grad_ref[block, :], contract_low, ((1,), (1,))),
        )

    ahead = products(blocks[0])
    for at, block in enumerate(blocks):
        before, grad_hidden = ahead
        if at + 1 < len(blocks):
            ahead = products(blocks[at + 1])
        value, slope = gelu_and_slope(before)
        hidden = value.astype(bf16)
        grad_pre = (grad_hidden * slope).astype(bf16)
        hidden_ref[block, :] = hidden
        pre_ref[block, :] = grad_pre
        output[block, :] += dot(hidden, contract_low)
        grad_two[block, :] += dot(grad_pre, expand_low, ((1,), (1,)))

    @pl.when(step == STEPS - 1)
    def _():
        weight = proj_low()
        gain = jnp.zeros((1, middle.shape[1]), f32)
        shift = jnp.zeros((1, middle.shape[1]), f32)
        for block in blocks:
            grad = grad_two[block, :]
            normed, scaled = norm_rows(middle[block, :])
            gain += jnp.sum(grad * normed, axis=0, keepdims=True)
            shift += jnp.sum(grad, axis=0, keepdims=True)
            grad_middle = grad_ref[block, :].astype(f32) + norm_backward(
                grad, normed, scaled, params[2:3, :]
            )
            middle_ref[block, :] = grad_middle
            attended_grad_ref[block, :] = dot(
                grad_middle.astype(bf16), weight, ((1,), (1,))
            ).astype(bf16)
        sums_ref[0:1, :] = gain
        sums_ref[1:2, :] = shift
        for part_ref, part in zip(out_parts, split_parts(place[0], output[...].T)):
            part_ref[...] = part.astype(bf16)


def block_middle(place, resid, attended, grad, params, proj, expand, contract):
    rows, width = resid.shape
    ff = 2 * expand[0].shape[1]
    chunk = ff // STEPS
    part = jax.ShapeDtypeStruct((width // 4, rows), bf16)
    narrow = jax.ShapeDtypeStruct((rows, width), bf16)
    broad = jax.ShapeDtypeStruct((rows, ff), bf16)
    wide = jax.ShapeDtypeStruct((rows, width), f32)
    sums = jax.ShapeDtypeStruct((2, width), f32)

    def fixed(shape):
        return pl.BlockSpec(shape.shape, lambda i, *_: (0, 0))

    return pl.pallas_call(
        block_kernel,
        grid_spec=pltpu.PrefetchScalarGridSpec(
            num_scalar_prefetch=1,
            grid=(STEPS,),
            in_specs=[
                *[resident(each) for each in (resid, attended, grad, params, *proj)],
                *side_blocks(expand[0].shape[0], chunk, 1, STEPS),
                *side_blocks(chunk, contract[0].shape[1], 0, STEPS),
            ],
            out_specs=[
                *[fixed(part)] * 4,
                fixed(narrow),
                column_block(rows, chunk),
                column_block(rows, chunk),
                fixed(wide),
                fixed(narrow),
                fixed(sums),
            ],
            scratch_shapes=[pltpu.VMEM((rows, width), f32)] * 3,
        ),
        out_shape=[*[part] * 4, narrow, broad, broad, wide, narrow, sums],
        compiler_params=pltpu.CompilerParams(vmem_limit_bytes=58 * 2**20),
        cost_estimate=pl.CostEstimate(
            flops=2 * rows * width * (4 * ff + 2 * width),
            bytes_accessed=rows * ff * 8,
            transcendentals=2 * rows * ff,
        ),
        name="block_middle",
    )(place, resid, attended, grad, params, *proj, *expand, *contract)


def adamw_kernel(place, weight, first, second, here, there, weight_out, first_out, second_out):
    x = place[2]
    mine = jnp.where(pl.program_id(0) // 4 == x, here[0].astype(f32), there[0].astype(f32))
    results = adamw_update(
        weight[...], mine, first[...], second[...], rate_matrix, decay_matrix
    )
    weight_out[...], first_out[...], second_out[...] = results


def adamw_pieces(place, weight, first, second, here, there):
    rows, width = weight.shape
    piece = pl.BlockSpec((rows // 8, width), lambda i, place: (i, 0))
    part = pl.BlockSpec((1, rows // 8, width), lambda i, place: ((i % 4) ^ place[3], 0, 0))
    return pl.pallas_call(
        adamw_kernel,
        grid_spec=pltpu.PrefetchScalarGridSpec(
            num_scalar_prefetch=1,
            grid=(8,),
            in_specs=[piece, piece, piece, part, part],
            out_specs=[piece] * 3,
        ),
        out_shape=[jax.ShapeDtypeStruct((rows, width), f32)] * 3,
        compiler_params=pltpu.CompilerParams(vmem_limit_bytes=40 * 2**20),
        cost_estimate=pl.CostEstimate(
            flops=20 * rows * width, bytes_accessed=28 * rows * width, transcendentals=0
        ),
        name="adamw_pieces",
    )(place, weight, first, second, here, there)


def local(
    tokens_in,
    out_grad,
    qkv_weight,
    proj_weight,
    expand_weight,
    contract_weight,
    norm_params,
    qkv_first,
    qkv_second,
    proj_first,
    proj_second,
    expand_first,
    expand_second,
    contract_first,
    contract_second,
    norm_first,
    norm_second,
):
    row = lax.axis_index("row")
    col = lax.axis_index("col")
    dp = lax.axis_index("dp")
    n_dp = lax.axis_size("dp")
    me = 2 * row + col
    place = jnp.stack([col, me, dp % 2, dp // 2]).astype(jnp.int32)
    tokens = tokens_in.shape[0] // 4
    part = tokens_in.shape[1]

    def swap(array, distance):
        if distance == 0:
            return array
        return lax.ppermute(array, GROUP, [(i, i ^ distance) for i in range(4)])

    def swap_dp(array, distance):
        return lax.ppermute(array, "dp", [(i, i ^ distance) for i in range(n_dp)])

    def swap_row(array):
        return swap(array, 2)

    def swap_col(array):
        return swap(array, 1)

    def token_blocks(array):
        return [lax.dynamic_slice(array, ((me ^ d) * tokens, 0), (tokens, part)) for d in range(4)]

    def swap_all(blocks):
        return [swap(block, d) for d, block in enumerate(blocks)]

    def ordered(bit, mine, partner):
        return jnp.where(
            bit == 0,
            jnp.concatenate([mine, partner], axis=0),
            jnp.concatenate([partner, mine], axis=0),
        )

    def by_halves(mine):
        rows = mine.shape[0] // 2
        got = swap_row(lax.dynamic_slice_in_dim(mine, (dp % 2) * rows, rows))
        return ordered(dp % 2, got, swap_dp(got, 1))

    def by_quarters(mine):
        rows = mine.shape[0] // 4
        got = swap_row(lax.dynamic_slice_in_dim(mine, (dp % 4) * rows, rows))
        got = ordered(dp % 2, got, swap_dp(got, 1))
        return ordered(dp // 2 % 2, got, swap_dp(got, 2))

    def all_blocks(mine, partner):
        return [mine, partner, swap_col(mine), swap_col(partner)]

    def reduce_row_col(left, right):
        half = right.shape[1] // 2
        rows = left.shape[1] // 2
        away = dot(left, right[:, half:], ((0,), (0,))).astype(bf16)
        kept = dot(left, right[:, :half], ((0,), (0,)))
        total = kept + swap_col(away).astype(f32)
        return total[:rows], total[rows:].astype(bf16)

    def reduce_col_row(left, right):
        half = left.shape[1] // 2
        columns = right.shape[1] // 2
        away = dot(left[:, half:], right, ((0,), (0,))).astype(bf16)
        kept = dot(left[:, :half], right, ((0,), (0,)))
        total = kept + swap_col(away).astype(f32)
        return total[:, :columns], total[:, columns:].astype(bf16)

    resid_parts = swap_all(token_blocks(tokens_in))
    params = [swap(norm_params, d) for d in range(4)]
    params = jnp.concatenate(
        [in_order(col, params[0], params[1]), in_order(col, params[2], params[3])], axis=1
    )
    qkv_mine = qkv_weight.astype(bf16)
    qkv_low = all_blocks(qkv_mine, by_halves(qkv_mine))

    resid_parts, proj_mine, expand_mine, contract_mine, grad_blocks = lax.optimization_barrier(
        (
            resid_parts,
            proj_weight.astype(bf16),
            expand_weight.astype(bf16),
            contract_weight.astype(bf16),
            token_blocks(out_grad),
        )
    )
    proj_low = all_blocks(proj_mine, by_halves(proj_mine))
    expand_low = all_blocks(expand_mine, by_quarters(expand_mine))
    contract_low = all_blocks(contract_mine, by_quarters(contract_mine))
    grad_parts = swap_all(grad_blocks)
    resid = tokens_together(place, [each.T for each in resid_parts])
    h_one, mixed, attended, probs = attend_forward(resid, params, qkv_low)
    grad_low = tokens_together(place, [each.T for each in grad_parts])
    outs = block_middle(place, resid, attended, grad_low, params, proj_low, expand_low, contract_low)
    output_parts = outs[:4]
    h_two, hidden, grad_pre, grad_middle, grad_attended, sums_two = outs[4:]
    contract_grad = reduce_col_row(hidden, grad_low)
    expand_grad = reduce_row_col(h_two, grad_pre)
    proj_grad = reduce_col_row(attended, grad_middle.astype(bf16))
    contract_grad, expand_grad, proj_grad, grad_attended = lax.optimization_barrier(
        (contract_grad, expand_grad, proj_grad, grad_attended)
    )
    contract_grad, expand_grad, proj_grad = [
        (kept, swap_row(away)) for kept, away in (contract_grad, expand_grad, proj_grad)
    ]
    outs = attend_backward(
        place, mixed, probs, grad_attended, grad_middle, resid, params, qkv_low
    )
    grad_mixed, input_parts, sums_one = outs[0], outs[1:5], outs[5]
    kept, away = reduce_row_col(h_one, grad_mixed)
    qkv_grad = (kept, swap_row(away))

    qkv_grad, output_parts, input_parts = lax.optimization_barrier(
        (qkv_grad, output_parts, input_parts)
    )

    def over_dp(kept, received):
        gradient = (kept + received.astype(f32)).astype(bf16)
        if n_dp != 8:
            return lax.psum(gradient, "dp").astype(f32)
        rows = gradient.shape[0] // 2
        x, z = dp % 2, dp // 2
        away = lax.dynamic_slice_in_dim(gradient, (1 - x) * rows, rows)
        total = lax.dynamic_slice_in_dim(gradient, x * rows, rows).astype(f32)
        total = (total + swap_dp(away, 1).astype(f32)).astype(bf16)
        pieces = [lax.dynamic_slice_in_dim(total, (z ^ d) * (rows // 4), rows // 4) for d in range(4)]
        mine = pieces[0].astype(f32)
        for d in range(1, 4):
            mine = mine + swap_dp(pieces[d], 2 * d).astype(f32)
        mine = mine.astype(bf16)
        here = jnp.stack([mine] + [swap_dp(mine, 2 * d) for d in range(1, 4)])
        return here, swap_dp(here, 1)

    contract_sum = over_dp(*contract_grad)
    expand_sum = over_dp(*expand_grad)
    proj_sum = over_dp(*proj_grad)
    qkv_sum = over_dp(*qkv_grad)
    norm_parts = split_features(col, jnp.concatenate([sums_one, sums_two], axis=0))
    norm_sum = norm_parts[0] + sum(swap(norm_parts[d], d) for d in range(1, 4))
    if n_dp == 8:
        for d in (1, 2, 4):
            norm_sum = norm_sum + swap_dp(norm_sum, d)
    else:
        norm_sum = lax.psum(norm_sum, "dp")

    results = (
        tokens_apart(place, tokens, swap_all(output_parts)),
        tokens_apart(place, tokens, swap_all(input_parts)),
    )
    for weight, gradient, first, second in (
        (qkv_weight, qkv_sum, qkv_first, qkv_second),
        (proj_weight, proj_sum, proj_first, proj_second),
        (expand_weight, expand_sum, expand_first, expand_second),
        (contract_weight, contract_sum, contract_first, contract_second),
    ):
        if n_dp == 8:
            results += tuple(adamw_pieces(place, weight, first, second, *gradient))
        else:
            results += adamw_update(weight, gradient, first, second, rate_matrix, decay_matrix)
    return results + adamw_update(norm_params, norm_sum, norm_first, norm_second, rate_norm, 0.0)


def solution(mesh):
    tokens = P("dp", ("row", "col"))
    one = P("row", "col")
    two = P("col", "row")
    norm = P(None, ("row", "col"))
    in_specs = (tokens, tokens, one, two, one, two, norm)
    in_specs += (one, one, two, two, one, one, two, two, norm, norm)
    out_specs = (tokens, tokens) + (one,) * 3 + (two,) * 3 + (one,) * 3 + (two,) * 3 + (norm,) * 3
    return jax.shard_map(local, mesh=mesh, in_specs=in_specs, out_specs=out_specs, check_vma=False)
```

time: 751 us -> 452 us (0.60)
  waiting for transfers between devices: 362 us -> 145 us
  matrix products: 129 us -> 26.2 us
  Pallas kernels: 43.1 us -> 133 us
  starting transfers between devices: 25.9 us -> 92.2 us
  local copies, waits for them, and re-layouts: 80.6 us -> 28.3 us
  other arithmetic: 65 us -> 16.6 us
  blocking collectives: 19.9 us -> 0 us
  between operations: 15.1 us -> 1.82 us
    psum x4 -> x0, waiting for transfers between devices: 216 us -> none  [over_dp(): return lax.psum(gradient, 'dp')]
    dot_general x16 -> x8, matrix products: 129 us -> 26.2 us  [dot(): lax.dot_general(left, right, (dims, ((), ())), preferred_element_type=f32)]
    pallas_call x2 -> x11, Pallas kernels: 43.1 us -> 133 us  [the longest x1 44.6 us: block_middle(): pl.pallas_call(block_kernel, grid_spec=pltpu.PrefetchScalarGridSpec(num_s...]
    ppermute x34 -> x38, waiting for transfers between devices: 146 us -> 80.4 us  [swap(): return lax.ppermute(array, GROUP, [(i, i ^ distance) for i in range(4)])]
    ppermute x0 -> x41, starting transfers between devices: none -> 65 us  [swap_dp(): return lax.ppermute(array, 'dp', [(i, i ^ distance) for i in range(n_dp)])]
    ppermute x0 -> x41, waiting for transfers between devices: none -> 65 us  [swap_dp(): return lax.ppermute(array, 'dp', [(i, i ^ distance) for i in range(n_dp)])]
    dynamic_update_slice x8 -> x0, local copies, waits for them, and re-layouts: 48.8 us -> none  [features_together(): result = lax.dynamic_update_slice(result, received, ((me ^ d) * tokens, 0))]
    sub x5 -> x1, other arithmetic: 22.1 us -> 0.62 us  [adamw_update(): weight - rate_value * (first_hat / (jnp.sqrt(second_hat) + adam_epsilon)...]
  transfers between devices with their start and end apart: 38 -> 79, of which waited for: 14 -> 30; matrix products, arithmetic and copies ran while one was open for 19% -> 10% of each run, Pallas kernels for 2% -> 19%
where the time goes in v3:
time: 452 us; the launch traced here: 443 us
  waiting for transfers between devices  145 us (32%)
  Pallas kernels  133 us (29%)
  starting transfers between devices  92.2 us (20%)
  local copies, waits for them, and re-layouts  28.3 us (6%)
  matrix products  26.2 us (6%)
  other arithmetic  16.6 us (4%)
    ppermute x38, waiting for transfers between devices, swap(): return lax.ppermute(array, GROUP, [(i, i ^ distance) for i in range(4)])  80.4 us
    ppermute x41, starting transfers between devices, swap_dp(): return lax.ppermute(array, 'dp', [(i, i ^ distance) for i in range(n_dp)])  65 us
    ppermute x41, waiting for transfers between devices, swap_dp(): return lax.ppermute(array, 'dp', [(i, i ^ distance) for i in range(n_dp)])  65 us
    pallas_call x1, Pallas kernels, block_middle(): pl.pallas_call(block_kernel, grid_spec=pltpu.PrefetchScalarGridSpec(num_s...  44.6 us
    pallas_call x1, Pallas kernels, attend_backward(): pl.pallas_call(backward_kernel, grid_spec=pltpu.PrefetchScalarGridSpec(nu...  38.4 us
    ppermute x38, starting transfers between devices, swap(): return lax.ppermute(array, GROUP, [(i, i ^ distance) for i in range(4)])  27.1 us
    dot_general x8, matrix products, dot(): lax.dot_general(left, right, (dims, ((), ())), preferred_element_type=f32)  26.2 us
    pallas_call x1, Pallas kernels, attend_forward(): pl.pallas_call(forward_kernel, grid=(STEPS,), in_specs=[resident(resid),...  20.2 us
  transfers between devices with their start and end apart: 79, of which 30 were waited for; matrix products, arithmetic and copies ran while one was open for 10% of the time, Pallas kernels for 19%

profile of v3, /device:TPU:0, one launch (start us, length us, event | category | flops | bytes accessed | tf_op | source)
XLA Modules:
  0.0 443.1 jit_solution(5485175680795427132)
XLA Ops:
  0.7 3.5 constant_dynamic-slice_fusion.24
  17.5 3.7 constant_dynamic-slice_fusion.20
  21.1 8.5 %collective-permute-done.2 = bf16[1182,192]{0,1:T(8,128)(2,1)} collective-permute-done((bf16[1182,192]{0,1:T(8,128)(2,1)}, bf16[1182,192]{0,1:T(8,128)(2,1)}, u32[]{:S(2)}, u32[]{:S(2)}) %collective-permute-start.2) | collective-permute-done | bytes 453920 | tf_op jit(solution)/shard_map/ppermute | solution.py:581
  36.7 9.2 %collective-permute-done.17 = bf16[96,1536]{1,0:T(8,128)(2,1)} collective-permute-done((bf16[96,1536]{1,0:T(8,128)(2,1)}, bf16[96,1536]{1,0:T(8,128)(2,1)}, u32[]{:S(2)}, u32[]{:S(2)}) %collective-permute-start.17) | collective-permute-done | bytes 294944 | tf_op jit(solution)/shard_map/ppermute | solution.py:581
  59.5 9.0 %collective-permute-done.13 = bf16[192,384]{1,0:T(8,128)(2,1)S(1)} collective-permute-done((bf16[192,384]{1,0:T(8,128)(2,1)S(1)}, bf16[192,384]{1,0:T(8,128)(2,1)S(1)}, u32[]{:S(2)}, u32[]{:S(2)}) %collective-permute-start.13) | collective-permute-done | bytes 147488 | tf_op jit(solution)/shard_map/ppermute | solution.py:581
  82.5 4.2 collective-permute-done.12
  89.3 7.2 %collective-permute-done.24 = bf16[768,384]{1,0:T(8,128)(2,1)S(1)} collective-permute-done((bf16[768,384]{1,0:T(8,128)(2,1)S(1)}, bf16[768,384]{1,0:T(8,128)(2,1)S(1)}, u32[]{:S(2)}, u32[]{:S(2)}) %collective-permute-start.24) | collective-permute-done | bytes 589856 | tf_op jit(solution)/shard_map/ppermute | solution.py:584
  99.5 20.2 %attend_forward.1 = (bf16[1200,768]{1,0:T(8,128)(2,1)}, bf16[1200,2304]{1,0:T(8,128)(2,1)}, bf16[1200,768]{1,0:T(8,128)(2,1)}, bf16[6,12,208,256]{3,2,1,0:T(8,128)(2,1)}) custom-call(bf16[1200,768]{1,0:T(8,128)(2,1)} %copy-done.10, f32[4,768]{1,0:T(4,128)} %pad_maximum_fusion.4.refs_1_.refs_3_.refs_5_, ...), custom_call_target="tpu_custom_call" | custom-call | flops 20000000000 | bytes 18432000 | tf_op jit(solution)/shard_map/attend_forward/pallas_call | solution.py:251
  120.9 44.6 %block_middle.1 = (bf16[192,1200]{1,0:T(8,128)(2,1)}, bf16[192,1200]{1,0:T(8,128)(2,1)}, bf16[192,1200]{1,0:T(8,128)(2,1)}, bf16[192,1200]{1,0:T(8,128)(2,1)}, b...) custom-call(s32[4]{0:T(128)} %copy-done.19, ...), custom_call_target="tpu_custom_call" | custom-call | flops 25480396800 | bytes 29491200 | tf_op jit(solution)/shard_map/block_middle/pallas_call | solution.py:488
  165.5 5.5 %fusion.6 = bf16[1536,768]{1,0:T(8,128)(2,1)S(1)} fusion(bf16[1200,768]{1,0:T(8,128)(2,1)S(1)} %copy-done.12, bf16[1200,3072]{1,0:T(8,128)(2,1)} %get-tuple-element.92), kind=kOutput, calls=%fused_computation.9 | convolution fusion | flops 2832334848 | bytes 7888896 | tf_op jit(solution)/shard_map/dot_general | solution.py:32
  171.5 3.6 fusion.9
  176.7 3.8 collective-permute-done.29
  182.6 3.5 convert_add_fusion.1
  197.5 38.4 %attend_backward.1 = (bf16[1200,2304]{1,0:T(8,128)(2,1)}, bf16[192,1200]{1,0:T(8,128)(2,1)}, bf16[192,1200]{1,0:T(8,128)(2,1)}, bf16[192,1200]{1,0:T(8,128)(2,1)...) custom-call(s32[4]{0:T(128)} %copy-done.19, bf16[1200,2304]{1,0:T(8,128)(2,1)} %get-tuple-element.82.refs_0_, ...), custom_call_target="tpu_custom_call" | custom-call | flops 30000001024 | bytes 22118400 | tf_op jit(solution)/shard_map/attend_backward/pallas_call | solution.py:374
  248.7 5.5 %convolution_convert_fusion = bf16[768,1152]{1,0:T(8,128)(2,1)S(1)} fusion(bf16[1200,768]{1,0:T(8,128)(2,1)} %get-tuple-element.81, bf16[1200,2304]{1,0:T(8,128)(2,1)} %get-tuple-element.98), kind=kOutput, calls=%fused_computation.11 | convolution fusion | flops 2124251136 | bytes 6377472 | tf_op jit(solution)/shard_map/dot_general | solution.py:32
  258.6 13.1 %collective-permute-done.55 = bf16[384,1536]{1,0:T(8,128)(2,1)S(1)} collective-permute-done((bf16[384,1536]{1,0:T(8,128)(2,1)}, bf16[384,1536]{1,0:T(8,128)(2,1)S(1)}, u32[]{:S(2)}, u32[]{:S(2)}) %collective-permute-start.55) | collective-permute-done | bytes 1179680 | tf_op jit(solution)/shard_map/ppermute | solution.py:581
  273.5 21.1 %collective-permute-done.64 = bf16[1536,384]{1,0:T(8,128)(2,1)S(1)} collective-permute-done((bf16[1536,384]{1,0:T(8,128)(2,1)S(1)}, bf16[1536,384]{1,0:T(8,128)(2,1)S(1)}, u32[]{:S(2)}, u32[]{:S(2)}) %collective-permute-start.64) | collective-permute-done | bytes 1179680 | tf_op jit(solution)/shard_map/ppermute | solution.py:581
  302.4 5.5 %collective-permute-done.65 = bf16[768,384]{1,0:T(8,128)(2,1)S(1)} collective-permute-done((bf16[768,384]{1,0:T(8,128)(2,1)S(1)}, bf16[768,384]{1,0:T(8,128)(2,1)S(1)}, u32[]{:S(2)}, u32[]{:S(2)}) %collective-permute-start.65) | collective-permute-done | bytes 589856 | tf_op jit(solution)/shard_map/ppermute | solution.py:584
  308.2 3.6 collective-permute-start.68
  312.8 3.9 collective-permute-done.68
  319.7 7.3 %collective-permute-done.67 = bf16[192,384]{1,0:T(8,128)(2,1)S(1)} collective-permute-done((bf16[192,384]{1,0:T(8,128)(2,1)S(1)}, bf16[192,384]{1,0:T(8,128)(2,1)S(1)}, u32[]{:S(2)}, u32[]{:S(2)}) %collective-permute-start.67) | collective-permute-done | bytes 147488 | tf_op jit(solution)/shard_map/ppermute | solution.py:584
  327.0 4.0 collective-permute-start.57
  331.1 3.6 collective-permute-start.49
  341.3 4.4 %collective-permute-done.49 = bf16[48,384]{1,0:T(8,128)(2,1)S(1)} collective-permute-done((bf16[48,384]{1,0:T(8,128)(2,1)S(1)}, bf16[48,384]{1,0:T(8,128)(2,1)S(1)}, u32[]{:S(2)}, u32[]{:S(2)}) %collective-permute-start.49) | collective-permute-done | bytes 36896 | tf_op jit(solution)/shard_map/ppermute | solution.py:584
  345.7 7.8 %collective-permute-start.69 = (bf16[192,384]{1,0:T(8,128)(2,1)S(1)}, bf16[192,384]{1,0:T(8,128)(2,1)S(1)}, u32[]{:S(2)}, u32[]{:S(2)}) collective-permute-start(bf16[192,384]{1,0:T(8,128)(2,1)S(1)} %add_convert_fusion.7), channel_id=1, source_target_pairs={{0,8},{4,12},{8,0},{12,4},{16,24},{20,28},{24,16},{28,20},{1,9},{5... | collective-permute-start | bytes 442376 | tf_op jit(solution)/shard_map/ppermute | solution.py:584
  380.2 15.9 %collective-permute-done.54.there = bf16[4,48,384]{2,1,0:T(8,128)(2,1)S(1)} collective-permute-done((bf16[4,48,384]{2,1,0:T(8,128)(2,1)S(1)}, bf16[4,48,384]{2,1,0:T(8,128)(2,1)S(1)}, u32[]{:S(2)}, u32[]{:S(2)}) %collective-permute-start.54) | collective-permute-done | bytes 147488 | tf_op jit(solution)/shard_map/ppermute | solution.py:584
  397.2 3.4 collective-permute-start.42
  408.5 3.6 adamw_pieces.5
  412.2 5.7 %adamw_pieces.6 = (f32[384,1536]{1,0:T(8,128)}, f32[384,1536]{1,0:T(8,128)}, f32[384,1536]{1,0:T(8,128)}) custom-call(s32[4]{0:T(128)S(1)} %copy-done.20, f32[384,1536]{1,0:T(8,128)S(1)} %copy-done, f32[384,1536]{1,0:T(8,128)S(1)} %copy-done.5, f32[384,1536]{1,0:T(8,128)S(1)} %copy-done.6, bf16[4,48,1536]{2,1,0:T(8,128)(2,1)S(1)} %pad_maximum_fusion.here, ...), custom_call_target="tpu_custom_call" | custom-call | flops 11796480 | bytes 16515072 | tf_op jit(solution)/shard_map/adamw_pieces/pallas_call | solution.py:533
  417.9 5.6 %adamw_pieces.7 = (f32[1536,384]{1,0:T(8,128)}, f32[1536,384]{1,0:T(8,128)}, f32[1536,384]{1,0:T(8,128)}) custom-call(s32[4]{0:T(128)S(1)} %copy-done.20, f32[1536,384]{1,0:T(8,128)S(1)} %copy-done.2, f32[1536,384]{1,0:T(8,128)S(1)} %copy-done.7, f32[1536,384]{1,0:T(8,128)S(1)} %copy-done.8, bf16[4,192,384]{2,1,0:T(8,128)(2,1)S(1)} %pad_maximum_fusion.1.here, ...), custom_call_target="tpu_custom_call" | custom-call | flops 11796480 | bytes 16515072 | tf_op jit(solution)/shard_map/adamw_pieces/pallas_call | solution.py:533
  426.6 8.2 %collective-permute-done.37.refs_3_ = bf16[192,1200]{1,0:T(8,128)(2,1)S(1)} collective-permute-done((bf16[192,1200]{1,0:T(8,128)(2,1)S(1)}, bf16[192,1200]{1,0:T(8,128)(2,1)S(1)}, u32[]{:S(2)}, u32[]{:S(2)}) %collective-permute-start.37) | collective-permute-done | bytes 460832 | tf_op jit(solution)/shard_map/ppermute | solution.py:581
  438.0 4.9 %adamw_pieces.4 = (f32[384,1152]{1,0:T(8,128)}, f32[384,1152]{1,0:T(8,128)}, f32[384,1152]{1,0:T(8,128)}) custom-call(s32[4]{0:T(128)S(1)} %copy-done.20, f32[384,1152]{1,0:T(8,128)S(1)} %copy-done.3, f32[384,1152]{1,0:T(8,128)S(1)} %copy-done.13, f32[384,1152]{1,0:T(8,128)S(1)} %copy-done.14, bf16[4,48,1152]{2,1,0:T(8,128)(2,1)S(1)} %pad_maximum_fusion.2.here, ...), custom_call_target="tpu_custom_call" | custom-call | flops 8847360 | bytes 12386304 | tf_op jit(solution)/shard_map/adamw_pieces/pallas_call | solution.py:533
  (324 shorter events, 149.3 us)
Async XLA Ops:
  7.2 22.4 %collective-permute-start.2 = (bf16[1182,192]{0,1:T(8,128)(2,1)}, bf16[1182,192]{0,1:T(8,128)(2,1)}, u32[]{:S(2)}, u32[]{:S(2)}) collective-permute-start(bf16[1182,192]{0,1:T(8,128)(2,1)} %get-tuple-element.144), channel_id=1, source_target_pairs={{0,3},{1,2},{2,1},{3,0},{4,7},{5,6},{6,5},{7,4},{8,11},{9,10},{10,... | collective-permute-start | bytes 1361672 | tf_op jit(solution)/shard_map/ppermute | solution.py:581
  11.8 37.8 %collective-permute-start.6 = (bf16[192,1152]{1,0:T(8,128)(2,1)}, bf16[192,1152]{1,0:T(8,128)(2,1)}, u32[]{:S(2)}, u32[]{:S(2)}) collective-permute-start(bf16[192,1152]{1,0:T(8,128)(2,1)} %constant_dynamic-slice_fusion.19), channel_id=1, source_target_pairs={{0,2},{1,3},{2,0},{3,1},{4,6},{5,7},{6,4},{7,5},{8,10},{9,11},{10,... | collective-permute-start | bytes 1327112 | tf_op jit(solution)/shard_map/ppermute | solution.py:581
  49.6 20.5 %collective-permute-start.7 = (bf16[192,1152]{1,0:T(8,128)(2,1)}, bf16[192,1152]{1,0:T(8,128)(2,1)S(1)}, u32[]{:S(2)}, u32[]{:S(2)}) collective-permute-start(bf16[192,1152]{1,0:T(8,128)(2,1)} %collective-permute-done.6), channel_id=1, source_target_pairs={{0,4},{4,0},{8,12},{12,8},{16,20},{20,16},{24,28},{28,24},{1,5},{5... | collective-permute-start | bytes 1327112 | tf_op jit(solution)/shard_map/ppermute | solution.py:584
  51.1 22.6 %collective-permute-start.10 = (bf16[1182,192]{0,1:T(8,128)(2,1)}, bf16[1182,192]{0,1:T(8,128)(2,1)S(1)}, u32[]{:S(2)}, u32[]{:S(2)}) collective-permute-start(bf16[1182,192]{0,1:T(8,128)(2,1)} %get-tuple-element.86), channel_id=1, source_target_pairs={{0,1},{1,0},{2,3},{3,2},{4,5},{5,4},{6,7},{7,6},{8,9},{9,8},{10,11... | collective-permute-start | bytes 1361672 | tf_op jit(solution)/shard_map/ppermute | solution.py:581
  52.2 24.5 %collective-permute-start.11 = (bf16[1182,192]{0,1:T(8,128)(2,1)}, bf16[1182,192]{0,1:T(8,128)(2,1)S(1)}, u32[]{:S(2)}, u32[]{:S(2)}) collective-permute-start(bf16[1182,192]{0,1:T(8,128)(2,1)} %get-tuple-element.87), channel_id=1, source_target_pairs={{0,2},{1,3},{2,0},{3,1},{4,6},{5,7},{6,4},{7,5},{8,10},{9,11},{10,... | collective-permute-start | bytes 1361672 | tf_op jit(solution)/shard_map/ppermute | solution.py:581
  56.2 19.2 %collective-permute-start.23 = (bf16[384,384]{1,0:T(8,128)(2,1)}, bf16[384,384]{1,0:T(8,128)(2,1)S(1)}, u32[]{:S(2)}, u32[]{:S(2)}) collective-permute-start(bf16[384,384]{1,0:T(8,128)(2,1)} %collective-permute-done.22), channel_id=1, source_target_pairs={{0,4},{4,0},{8,12},{12,8},{16,20},{20,16},{24,28},{28,24},{1,5},{5... | collective-permute-start | bytes 884744 | tf_op jit(solution)/shard_map/ppermute | solution.py:584
  73.7 23.8 %collective-permute-start.8 = (bf16[384,1152]{1,0:T(8,128)(2,1)S(1)}, bf16[384,1152]{1,0:T(8,128)(2,1)S(1)}, u32[]{:S(2)}, u32[]{:S(2)}) collective-permute-start(bf16[384,1152]{1,0:T(8,128)(2,1)S(1)} %copy-done.25), channel_id=1, source_target_pairs={{0,1},{1,0},{2,3},{3,2},{4,5},{5,4},{6,7},{7,6},{8,9},{9,8},{10,11... | collective-permute-start | bytes 2654216 | tf_op jit(solution)/shard_map/ppermute | solution.py:581
  75.4 22.2 %collective-permute-start.9 = (bf16[384,1152]{1,0:T(8,128)(2,1)S(1)}, bf16[384,1152]{1,0:T(8,128)(2,1)S(1)}, u32[]{:S(2)}, u32[]{:S(2)}) collective-permute-start(bf16[384,1152]{1,0:T(8,128)(2,1)S(1)} %maximum_select_fusion.2.refs_3_.refs_7_), channel_id=1, source_target_pairs={{0,1},{1,0},{2,3},{3,2},{4,5},{5,4},{6,7},{7,6},{8,9},{9,8},{10,11... | collective-permute-start | bytes 2654216 | tf_op jit(solution)/shard_map/ppermute | solution.py:581
  76.7 19.8 %collective-permute-start.24 = (bf16[768,384]{1,0:T(8,128)(2,1)S(1)}, bf16[768,384]{1,0:T(8,128)(2,1)S(1)}, u32[]{:S(2)}, u32[]{:S(2)}) collective-permute-start(bf16[768,384]{1,0:T(8,128)(2,1)S(1)} %maximum_select_fusion.4), channel_id=1, source_target_pairs={{0,8},{4,12},{8,0},{12,4},{16,24},{20,28},{24,16},{28,20},{1,9},{5... | collective-permute-start | bytes 1769480 | tf_op jit(solution)/shard_map/ppermute | solution.py:584
  88.8 31.0 %collective-permute-start.20 = (bf16[384,1536]{1,0:T(8,128)(2,1)S(1)}, bf16[384,1536]{1,0:T(8,128)(2,1)}, u32[]{:S(2)}, u32[]{:S(2)}) collective-permute-start(bf16[384,1536]{1,0:T(8,128)(2,1)S(1)} %copy-done.27), channel_id=1, source_target_pairs={{0,1},{1,0},{2,3},{3,2},{4,5},{5,4},{6,7},{7,6},{8,9},{9,8},{10,11... | collective-permute-start | bytes 3538952 | tf_op jit(solution)/shard_map/ppermute | solution.py:581
  96.5 23.3 %collective-permute-start.25 = (bf16[1536,384]{1,0:T(8,128)(2,1)S(1)}, bf16[1536,384]{1,0:T(8,128)(2,1)}, u32[]{:S(2)}, u32[]{:S(2)}) collective-permute-start(bf16[1536,384]{1,0:T(8,128)(2,1)S(1)} %copy-done.28), channel_id=1, source_target_pairs={{0,1},{1,0},{2,3},{3,2},{4,5},{5,4},{6,7},{7,6},{8,9},{9,8},{10,11... | collective-permute-start | bytes 3538952 | tf_op jit(solution)/shard_map/ppermute | solution.py:581
  97.0 22.8 %collective-permute-start.16 = (bf16[384,384]{1,0:T(8,128)(2,1)S(1)}, bf16[384,384]{1,0:T(8,128)(2,1)S(1)}, u32[]{:S(2)}, u32[]{:S(2)}) collective-permute-start(bf16[384,384]{1,0:T(8,128)(2,1)S(1)} %maximum_select_fusion.5.refs_5_), channel_id=1, source_target_pairs={{0,1},{1,0},{2,3},{3,2},{4,5},{5,4},{6,7},{7,6},{8,9},{9,8},{10,11... | collective-permute-start | bytes 884744 | tf_op jit(solution)/shard_map/ppermute | solution.py:581
  97.5 22.3 %collective-permute-start.21 = (bf16[384,1536]{1,0:T(8,128)(2,1)S(1)}, bf16[384,1536]{1,0:T(8,128)(2,1)}, u32[]{:S(2)}, u32[]{:S(2)}) collective-permute-start(bf16[384,1536]{1,0:T(8,128)(2,1)S(1)} %maximum_select_fusion.refs_9_), channel_id=1, source_target_pairs={{0,1},{1,0},{2,3},{3,2},{4,5},{5,4},{6,7},{7,6},{8,9},{9,8},{10,11... | collective-permute-start | bytes 3538952 | tf_op jit(solution)/shard_map/ppermute | solution.py:581
  99.4 20.4 %collective-permute-start.26 = (bf16[1536,384]{1,0:T(8,128)(2,1)S(1)}, bf16[1536,384]{1,0:T(8,128)(2,1)S(1)}, u32[]{:S(2)}, u32[]{:S(2)}) collective-permute-start(bf16[1536,384]{1,0:T(8,128)(2,1)S(1)} %maximum_select_fusion.1.refs_13_), channel_id=1, source_target_pairs={{0,1},{1,0},{2,3},{3,2},{4,5},{5,4},{6,7},{7,6},{8,9},{9,8},{10,11... | collective-permute-start | bytes 3538952 | tf_op jit(solution)/shard_map/ppermute | solution.py:581
  195.9 51.1 %collective-permute-start.46 = (bf16[384,384]{1,0:T(8,128)(2,1)}, bf16[384,384]{1,0:T(8,128)(2,1)}, u32[]{:S(2)}, u32[]{:S(2)}) collective-permute-start(bf16[384,384]{1,0:T(8,128)(2,1)} %slice.167), channel_id=1, source_target_pairs={{0,2},{1,3},{2,0},{3,1},{4,6},{5,7},{6,4},{7,5},{8,10},{9,11},{10,... | collective-permute-start | bytes 884744 | tf_op jit(solution)/shard_map/ppermute | solution.py:581
  242.6 29.1 %collective-permute-start.55 = (bf16[384,1536]{1,0:T(8,128)(2,1)}, bf16[384,1536]{1,0:T(8,128)(2,1)S(1)}, u32[]{:S(2)}, u32[]{:S(2)}) collective-permute-start(bf16[384,1536]{1,0:T(8,128)(2,1)} %slice.164), channel_id=1, source_target_pairs={{0,2},{1,3},{2,0},{3,1},{4,6},{5,7},{6,4},{7,5},{8,10},{9,11},{10,... | collective-permute-start | bytes 3538952 | tf_op jit(solution)/shard_map/ppermute | solution.py:581
  254.3 42.1 %collective-permute-start.30 = (bf16[768,1152]{1,0:T(8,128)(2,1)S(1)}, bf16[768,1152]{1,0:T(8,128)(2,1)S(1)}, u32[]{:S(2)}, u32[]{:S(2)}) collective-permute-start(bf16[768,1152]{1,0:T(8,128)(2,1)S(1)} %convolution_convert_fusion), channel_id=1, source_target_pairs={{0,1},{1,0},{2,3},{3,2},{4,5},{5,4},{6,7},{7,6},{8,9},{9,8},{10,11... | collective-permute-start | bytes 5308424 | tf_op jit(solution)/shard_map/ppermute | solution.py:581
  254.4 40.2 %collective-permute-start.64 = (bf16[1536,384]{1,0:T(8,128)(2,1)S(1)}, bf16[1536,384]{1,0:T(8,128)(2,1)S(1)}, u32[]{:S(2)}, u32[]{:S(2)}) collective-permute-start(bf16[1536,384]{1,0:T(8,128)(2,1)S(1)} %copy-done.32), channel_id=1, source_target_pairs={{0,2},{1,3},{2,0},{3,1},{4,6},{5,7},{6,4},{7,5},{8,10},{9,11},{10,... | collective-permute-start | bytes 3538952 | tf_op jit(solution)/shard_map/ppermute | solution.py:581
  256.1 83.0 %collective-permute-start.50 = (bf16[48,384]{1,0:T(8,128)(2,1)S(1)}, bf16[48,384]{1,0:T(8,128)(2,1)S(1)}, u32[]{:S(2)}, u32[]{:S(2)}) collective-permute-start(bf16[48,384]{1,0:T(8,128)(2,1)S(1)} %get-tuple-element.158), channel_id=1, source_target_pairs={{0,24},{4,28},{8,16},{12,20},{16,8},{20,12},{24,0},{28,4},{1,25},{... | collective-permute-start | bytes 110600 | tf_op jit(solution)/shard_map/ppermute | solution.py:584
  272.2 39.6 %collective-permute-start.56 = (bf16[192,1536]{1,0:T(8,128)(2,1)S(1)}, bf16[192,1536]{1,0:T(8,128)(2,1)S(1)}, u32[]{:S(2)}, u32[]{:S(2)}) collective-permute-start(bf16[192,1536]{1,0:T(8,128)(2,1)S(1)} %constant_dynamic-slice_fusion.7), channel_id=1, source_target_pairs={{0,4},{4,0},{8,12},{12,8},{16,20},{20,16},{24,28},{28,24},{1,5},{5... | collective-permute-start | bytes 1769480 | tf_op jit(solution)/shard_map/ppermute | solution.py:584
  301.0 37.6 %collective-permute-start.31 = (bf16[384,1152]{1,0:T(8,128)(2,1)S(1)}, bf16[384,1152]{1,0:T(8,128)(2,1)S(1)}, u32[]{:S(2)}, u32[]{:S(2)}) collective-permute-start(bf16[384,1152]{1,0:T(8,128)(2,1)S(1)} %slice.166), channel_id=1, source_target_pairs={{0,2},{1,3},{2,0},{3,1},{4,6},{5,7},{6,4},{7,5},{8,10},{9,11},{10,... | collective-permute-start | bytes 2654216 | tf_op jit(solution)/shard_map/ppermute | solution.py:581
  339.1 21.0 %collective-permute-start.62 = (bf16[48,1536]{1,0:T(8,128)(2,1)S(1)}, bf16[48,1536]{1,0:T(8,128)(2,1)S(1)}, u32[]{:S(2)}, u32[]{:S(2)}) collective-permute-start(bf16[48,1536]{1,0:T(8,128)(2,1)S(1)} %add_convert_fusion.8), channel_id=1, source_target_pairs={{0,24},{4,28},{8,16},{12,20},{16,8},{20,12},{24,0},{28,4},{1,25},{... | collective-permute-start | bytes 442376 | tf_op jit(solution)/shard_map/ppermute | solution.py:584
  367.1 30.1 %collective-permute-start.63 = (bf16[4,48,1536]{2,1,0:T(8,128)(2,1)S(1)}, bf16[4,48,1536]{2,1,0:T(8,128)(2,1)S(1)}, u32[]{:S(2)}, u32[]{:S(2)}) collective-permute-start(bf16[4,48,1536]{2,1,0:T(8,128)(2,1)S(1)} %pad_maximum_fusion.here), channel_id=1, source_target_pairs={{0,4},{4,0},{8,12},{12,8},{16,20},{20,16},{24,28},{28,24},{1,5},{5... | collective-permute-start | bytes 1769480 | tf_op jit(solution)/shard_map/ppermute | solution.py:584
  368.7 28.5 %collective-permute-start.72 = (bf16[4,192,384]{2,1,0:T(8,128)(2,1)S(1)}, bf16[4,192,384]{2,1,0:T(8,128)(2,1)S(1)}, u32[]{:S(2)}, u32[]{:S(2)}) collective-permute-start(bf16[4,192,384]{2,1,0:T(8,128)(2,1)S(1)} %pad_maximum_fusion.1.here), channel_id=1, source_target_pairs={{0,4},{4,0},{8,12},{12,8},{16,20},{20,16},{24,28},{28,24},{1,5},{5... | collective-permute-start | bytes 1769480 | tf_op jit(solution)/shard_map/ppermute | solution.py:584
  376.3 19.9 %collective-permute-start.54 = (bf16[4,48,384]{2,1,0:T(8,128)(2,1)S(1)}, bf16[4,48,384]{2,1,0:T(8,128)(2,1)S(1)}, u32[]{:S(2)}, u32[]{:S(2)}) collective-permute-start(bf16[4,48,384]{2,1,0:T(8,128)(2,1)S(1)} %pad_maximum_fusion.3.here), channel_id=1, source_target_pairs={{0,4},{4,0},{8,12},{12,8},{16,20},{20,16},{24,28},{28,24},{1,5},{5... | collective-permute-start | bytes 442376 | tf_op jit(solution)/shard_map/ppermute | solution.py:584
  378.9 21.7 %collective-permute-start.32 = (bf16[192,1200]{1,0:T(8,128)(2,1)S(1)}, bf16[192,1200]{1,0:T(8,128)(2,1)S(1)}, u32[]{:S(2)}, u32[]{:S(2)}) collective-permute-start(bf16[192,1200]{1,0:T(8,128)(2,1)S(1)} %copy-done.48), channel_id=1, source_target_pairs={{0,1},{1,0},{2,3},{3,2},{4,5},{5,4},{6,7},{7,6},{8,9},{9,8},{10,11... | collective-permute-start | bytes 1382408 | tf_op jit(solution)/shard_map/ppermute | solution.py:581
  378.9 27.4 %collective-permute-start.33 = (bf16[192,1200]{1,0:T(8,128)(2,1)S(1)}, bf16[192,1200]{1,0:T(8,128)(2,1)S(1)}, u32[]{:S(2)}, u32[]{:S(2)}) collective-permute-start(bf16[192,1200]{1,0:T(8,128)(2,1)S(1)} %copy-done.45), channel_id=1, source_target_pairs={{0,2},{1,3},{2,0},{3,1},{4,6},{5,7},{6,4},{7,5},{8,10},{9,11},{10,... | collective-permute-start | bytes 1382408 | tf_op jit(solution)/shard_map/ppermute | solution.py:581
  400.6 22.9 %collective-permute-start.34 = (bf16[192,1200]{1,0:T(8,128)(2,1)S(1)}, bf16[192,1200]{1,0:T(8,128)(2,1)S(1)}, u32[]{:S(2)}, u32[]{:S(2)}) collective-permute-start(bf16[192,1200]{1,0:T(8,128)(2,1)S(1)} %copy-done.44), channel_id=1, source_target_pairs={{0,3},{1,2},{2,1},{3,0},{4,7},{5,6},{6,5},{7,4},{8,11},{9,10},{10,... | collective-permute-start | bytes 1382408 | tf_op jit(solution)/shard_map/ppermute | solution.py:581
  402.9 23.7 %collective-permute-start.35 = (bf16[192,1200]{1,0:T(8,128)(2,1)}, bf16[192,1200]{1,0:T(8,128)(2,1)S(1)}, u32[]{:S(2)}, u32[]{:S(2)}) collective-permute-start(bf16[192,1200]{1,0:T(8,128)(2,1)} %get-tuple-element.112), channel_id=1, source_target_pairs={{0,1},{1,0},{2,3},{3,2},{4,5},{5,4},{6,7},{7,6},{8,9},{9,8},{10,11... | collective-permute-start | bytes 1382408 | tf_op jit(solution)/shard_map/ppermute | solution.py:581
  405.1 21.6 %collective-permute-start.36 = (bf16[192,1200]{1,0:T(8,128)(2,1)S(1)}, bf16[192,1200]{1,0:T(8,128)(2,1)S(1)}, u32[]{:S(2)}, u32[]{:S(2)}) collective-permute-start(bf16[192,1200]{1,0:T(8,128)(2,1)S(1)} %copy-done.47), channel_id=1, source_target_pairs={{0,2},{1,3},{2,0},{3,1},{4,6},{5,7},{6,4},{7,5},{8,10},{9,11},{10,... | collective-permute-start | bytes 1382408 | tf_op jit(solution)/shard_map/ppermute | solution.py:581
  406.3 28.6 %collective-permute-start.37 = (bf16[192,1200]{1,0:T(8,128)(2,1)S(1)}, bf16[192,1200]{1,0:T(8,128)(2,1)S(1)}, u32[]{:S(2)}, u32[]{:S(2)}) collective-permute-start(bf16[192,1200]{1,0:T(8,128)(2,1)S(1)} %copy-done.46), channel_id=1, source_target_pairs={{0,3},{1,2},{2,1},{3,0},{4,7},{5,6},{6,5},{7,4},{8,11},{9,10},{10,... | collective-permute-start | bytes 1382408 | tf_op jit(solution)/shard_map/ppermute | solution.py:581
  406.4 31.7 %collective-permute-start.45 = (bf16[4,48,1152]{2,1,0:T(8,128)(2,1)S(1)}, bf16[4,48,1152]{2,1,0:T(8,128)(2,1)S(1)}, u32[]{:S(2)}, u32[]{:S(2)}) collective-permute-start(bf16[4,48,1152]{2,1,0:T(8,128)(2,1)S(1)} %pad_maximum_fusion.2.here), channel_id=1, source_target_pairs={{0,4},{4,0},{8,12},{12,8},{16,20},{20,16},{24,28},{28,24},{1,5},{5... | collective-permute-start | bytes 1327112 | tf_op jit(solution)/shard_map/ppermute | solution.py:584
  (109 other events, 1676.0 us)

commit v4 on v3

--- a/solution.py
+++ b/solution.py
@@ -273,11 +273,16 @@
     )(resid, params, *weights)
 
 
-def backward_kernel(place, *refs):
-    mixed_ref, probs_ref, grad_ref, middle_ref, resid_ref, params = refs[:6]
-    weights = refs[6:10]
-    out_ref, out_parts, sums_ref = refs[10], refs[11:15], refs[15]
-    wide, grad_wide, gathered, total = refs[16:]
+def backward_kernel(last, place, *refs):
+    mixed_ref, probs_ref, grad_ref = refs[:3]
+    weights = refs[3:5]
+    if last:
+        before_ref, middle_ref, resid_ref, params = refs[5:9]
+        out_ref, out_parts, sums_ref = refs[9], refs[10:14], refs[14]
+        wide, grad_wide, gathered, total = refs[15:]
+    else:
+        out_ref, total = refs[5:7]
+        wide, grad_wide, gathered = refs[7:]
     rows = mixed_ref.shape[0]
     images = rows // SEQ
     tokens = images * SEQ
@@ -332,12 +337,12 @@
             gathered[block, 128:256] = jnp.where(low_lane, grad_v0[:QROWS], grad_q1)
             gathered[block, 256:384] = jnp.where(low_lane, grad_k1[:QROWS], grad_v1[:QROWS])
     gathered[tokens:, :] = jnp.zeros((gathered.shape[0] - tokens, 384), f32)
-    weight = side_weight(weights, STEPS, 0)
+    weight = jnp.concatenate([weights[0][...], weights[1][...]], axis=0)
     step = pl.program_id(0)
 
     @pl.when(step == 0)
     def _():
-        total[...] = jnp.zeros_like(total)
+        total[...] = before_ref[...] if last else jnp.zeros_like(total)
 
     for start in range(0, rows, BLOCK):
         block = slice(start, start + BLOCK)
@@ -345,7 +350,10 @@
         out_ref[block, :] = grad_mixed
         total[block, :] += dot(grad_mixed, weight, ((1,), (1,)))
 
-    @pl.when(step == STEPS - 1)
+    if not last:
+        return
+
+    @pl.when(step == pl.num_programs(0) - 1)
     def _():
         gain = jnp.zeros((1, total.shape[1]), f32)
         shift = jnp.zeros((1, total.shape[1]), f32)
@@ -364,42 +372,49 @@
             part_ref[...] = part.astype(bf16)
 
 
-def attend_backward(place, mixed, probs, grad_attended, grad_middle, resid, params, weights):
-    rows, width = resid.shape
+def attend_backward(place, mixed, probs, grad_attended, weights, side, rest):
+    rows, width = grad_attended.shape
     images = rows // SEQ
+    steps = STEPS // 2
+    first = side * steps
     padded = -(-((images - 1) * SEQ + KROWS) // 16) * 16
     part = jax.ShapeDtypeStruct((width // 4, rows), bf16)
     sums = jax.ShapeDtypeStruct((2, width), f32)
-    whole = [pl.BlockSpec(each.shape, lambda i, *_: (0, 0)) for each in [part] * 4 + [sums]]
+    whole = jax.ShapeDtypeStruct((rows, width), f32)
+    extra = [part] * 4 + [sums] if rest else [whole]
+    scratch = [
+        pltpu.VMEM((padded, 384), f32),
+        pltpu.VMEM((padded, 128), f32),
+        pltpu.VMEM((padded, 384), f32),
+    ]
+    if rest:
+        scratch.append(pltpu.VMEM((rows, width), f32))
+    weight_rows = weights[0].shape[0]
     return pl.pallas_call(
-        backward_kernel,
+        lambda *refs: backward_kernel(bool(rest), *refs),
         grid_spec=pltpu.PrefetchScalarGridSpec(
             num_scalar_prefetch=1,
-            grid=(STEPS,),
+            grid=(steps,),
             in_specs=[
+                pl.BlockSpec((rows, 384), lambda i, *_: (0, i + first)),
+                pl.BlockSpec((1, *probs.shape[1:]), lambda i, *_: (i + first, 0, 0, 0)),
+                pl.BlockSpec((rows, 128), lambda i, *_: (0, i + first)),
+                *[pl.BlockSpec((weight_rows, 384), lambda i, *_: (0, i))] * 2,
+                *[resident(each) for each in rest],
+            ],
+            out_specs=[
                 column_block(rows, 384),
-                pl.BlockSpec((1, *probs.shape[1:]), lambda i, *_: (i, 0, 0, 0)),
-                column_block(rows, 128),
-                resident(grad_middle),
-                resident(resid),
-                resident(params),
-                *side_blocks(weights[0].shape[0], 384, 1, STEPS),
+                *[pl.BlockSpec(each.shape, lambda i, *_: (0, 0)) for each in extra],
             ],
-            out_specs=[column_block(rows, 384), *whole],
-            scratch_shapes=[
-                pltpu.VMEM((padded, 384), f32),
-                pltpu.VMEM((padded, 128), f32),
-                pltpu.VMEM((padded, 384), f32),
-                pltpu.VMEM((rows, width), f32),
-            ],
+            scratch_shapes=scratch,
         ),
-        out_shape=[jax.ShapeDtypeStruct(mixed.shape, bf16), *[part] * 4, sums],
+        out_shape=[jax.ShapeDtypeStruct((rows, steps * 384), bf16), *extra],
         compiler_params=pltpu.CompilerParams(vmem_limit_bytes=54 * 2**20),
         cost_estimate=pl.CostEstimate(
-            flops=30 * 10**9, bytes_accessed=rows * width * 24, transcendentals=0
+            flops=15 * 10**9, bytes_accessed=rows * width * 12, transcendentals=0
         ),
         name="attend_backward",
-    )(place, mixed, probs, grad_attended, grad_middle, resid, params, *weights)
+    )(place, mixed, probs, grad_attended, *weights[2 * side : 2 * side + 2], *rest)
 
 
 def block_kernel(place, *refs):
@@ -602,104 +617,181 @@
             jnp.concatenate([partner, mine], axis=0),
         )
 
-    def by_halves(mine):
-        rows = mine.shape[0] // 2
-        got = swap_row(lax.dynamic_slice_in_dim(mine, (dp % 2) * rows, rows))
-        return ordered(dp % 2, got, swap_dp(got, 1))
-
-    def by_quarters(mine):
-        rows = mine.shape[0] // 4
-        got = swap_row(lax.dynamic_slice_in_dim(mine, (dp % 4) * rows, rows))
-        got = ordered(dp % 2, got, swap_dp(got, 1))
-        return ordered(dp // 2 % 2, got, swap_dp(got, 2))
+    def dp_part(mine, count):
+        rows = mine.shape[0] // count
+        return lax.dynamic_slice_in_dim(mine, (dp % count) * rows, rows)
 
     def all_blocks(mine, partner):
         return [mine, partner, swap_col(mine), swap_col(partner)]
-
-    def reduce_row_col(left, right):
-        half = right.shape[1] // 2
-        rows = left.shape[1] // 2
-        away = dot(left, right[:, half:], ((0,), (0,))).astype(bf16)
-        kept = dot(left, right[:, :half], ((0,), (0,)))
-        total = kept + swap_col(away).astype(f32)
-        return total[:rows], total[rows:].astype(bf16)
-
-    def reduce_col_row(left, right):
-        half = left.shape[1] // 2
-        columns = right.shape[1] // 2
-        away = dot(left[:, half:], right, ((0,), (0,))).astype(bf16)
-        kept = dot(left[:, :half], right, ((0,), (0,)))
-        total = kept + swap_col(away).astype(f32)
-        return total[:, :columns], total[:, columns:].astype(bf16)
 
     resid_parts = swap_all(token_blocks(tokens_in))
     params = [swap(norm_params, d) for d in range(4)]
     params = jnp.concatenate(
         [in_order(col, params[0], params[1]), in_order(col, params[2], params[3])], axis=1
     )
+    x, z = dp % 2, dp // 2
     qkv_mine = qkv_weight.astype(bf16)
-    qkv_low = all_blocks(qkv_mine, by_halves(qkv_mine))
-
-    resid_parts, proj_mine, expand_mine, contract_mine, grad_blocks = lax.optimization_barrier(
+    qkv_got = swap_row(dp_part(qkv_mine, 2))
+    expand_mine = expand_weight.astype(bf16)
+    contract_mine = contract_weight.astype(bf16)
+    proj_mine = proj_weight.astype(bf16)
+
+    resid_parts, qkv_got, *sends = lax.optimization_barrier(
         (
             resid_parts,
-            proj_weight.astype(bf16),
-            expand_weight.astype(bf16),
-            contract_weight.astype(bf16),
-            token_blocks(out_grad),
+            qkv_got,
+            dp_part(expand_mine, 4),
+            dp_part(contract_mine, 4),
+            dp_part(proj_mine, 2),
         )
     )
-    proj_low = all_blocks(proj_mine, by_halves(proj_mine))
-    expand_low = all_blocks(expand_mine, by_quarters(expand_mine))
-    contract_low = all_blocks(contract_mine, by_quarters(contract_mine))
+    qkv_next = swap_dp(qkv_got, 1)
+    expand_got, contract_got, proj_got = [swap_row(each) for each in sends]
+    qkv_got, qkv_next, expand_got, contract_got, proj_got, grad_blocks = lax.optimization_barrier(
+        (qkv_got, qkv_next, expand_got, contract_got, proj_got, token_blocks(out_grad))
+    )
+    qkv_low = all_blocks(qkv_mine, ordered(x, qkv_got, qkv_next))
+    quarters = [[each, swap_dp(each, 1), swap_dp(each, 2)] for each in (expand_got, contract_got)]
+    proj_next = swap_dp(proj_got, 1)
     grad_parts = swap_all(grad_blocks)
     resid = tokens_together(place, [each.T for each in resid_parts])
     h_one, mixed, attended, probs = attend_forward(resid, params, qkv_low)
+    attended, quarters, proj_next, grad_parts = lax.optimization_barrier(
+        (attended, quarters, proj_next, grad_parts)
+    )
+    expand_row, contract_row = [
+        ordered(
+            z % 2,
+            ordered(x, each[0], each[1]),
+            ordered(x, each[2], swap_dp(each[2], 1)),
+        )
+        for each in quarters
+    ]
+    proj_low = all_blocks(proj_mine, ordered(x, proj_got, proj_next))
+    expand_low = all_blocks(expand_mine, expand_row)
+    contract_low = all_blocks(contract_mine, contract_row)
     grad_low = tokens_together(place, [each.T for each in grad_parts])
     outs = block_middle(place, resid, attended, grad_low, params, proj_low, expand_low, contract_low)
     output_parts = outs[:4]
     h_two, hidden, grad_pre, grad_middle, grad_attended, sums_two = outs[4:]
-    contract_grad = reduce_col_row(hidden, grad_low)
-    expand_grad = reduce_row_col(h_two, grad_pre)
-    proj_grad = reduce_col_row(attended, grad_middle.astype(bf16))
-    contract_grad, expand_grad, proj_grad, grad_attended = lax.optimization_barrier(
-        (contract_grad, expand_grad, proj_grad, grad_attended)
-    )
-    contract_grad, expand_grad, proj_grad = [
-        (kept, swap_row(away)) for kept, away in (contract_grad, expand_grad, proj_grad)
-    ]
+
+    def halves(array, axis):
+        size = array.shape[axis] // 2
+        return (
+            lax.slice_in_dim(array, 0, size, axis=axis),
+            lax.slice_in_dim(array, size, 2 * size, axis=axis),
+        )
+
+    def over_col(left, right, received):
+        total = dot(left, right, ((0,), (0,))) + received.astype(f32)
+        return total.astype(bf16)
+
+    def split_x(array, axis):
+        size = array.shape[axis] // 2
+        kept = lax.dynamic_slice_in_dim(array, x * size, size, axis)
+        return kept, lax.dynamic_slice_in_dim(array, (1 - x) * size, size, axis)
+
+    def add(kept, received):
+        return (kept.astype(f32) + received.astype(f32)).astype(bf16)
+
+    def over_z(total):
+        rows = total.shape[0] // 4
+        pieces = [lax.dynamic_slice_in_dim(total, (z ^ d) * rows, rows) for d in range(4)]
+        return [pieces[0]] + [swap_dp(pieces[d], 2 * d) for d in range(1, 4)]
+
+    def sum_z(pieces):
+        return sum(piece.astype(f32) for piece in pieces).astype(bf16)
+
+    def gather_z(mine):
+        return [mine] + [swap_dp(mine, 2 * d) for d in range(1, 4)]
+
+    def gather_x(pieces):
+        here = jnp.stack(pieces)
+        return here, swap_dp(here, 1)
+
+    hidden_own, hidden_other = halves(hidden, 1)
+    pre_own, pre_other = halves(grad_pre, 1)
+    attended_own, attended_other = halves(attended, 1)
+    branch = grad_middle.astype(bf16)
+    contract_away = swap_col(dot(hidden_other, grad_low, ((0,), (0,))).astype(bf16))
+    expand_away = swap_col(dot(h_two, pre_other, ((0,), (0,))).astype(bf16))
+    proj_away = swap_col(dot(attended_other, branch, ((0,), (0,))).astype(bf16))
+    contract_sum = over_col(hidden_own, grad_low, contract_away)
+    expand_sum = over_col(h_two, pre_own, expand_away)
+    proj_sum = over_col(attended_own, branch, proj_away)
+    contract_sum, expand_sum, proj_sum, grad_attended = lax.optimization_barrier(
+        (contract_sum, expand_sum, proj_sum, grad_attended)
+    )
+    contract_kept, contract_away = halves(contract_sum, 1)
+    proj_kept, proj_away = halves(proj_sum, 1)
+    expand_sum = expand_sum.reshape(2, expand_sum.shape[0] // 2, expand_sum.shape[1])
+    expand_kept, expand_away = split_x(expand_sum, 1)
+    contract_got, expand_got, proj_got = (
+        swap_row(contract_away),
+        swap_dp(expand_away, 1),
+        swap_row(proj_away),
+    )
+    mixed_other, grad_other = attend_backward(
+        place, mixed, probs, grad_attended, qkv_low, 1, []
+    )
+    contract_got, expand_got, proj_got, mixed_other, grad_other = lax.optimization_barrier(
+        (contract_got, expand_got, proj_got, mixed_other, grad_other)
+    )
+    contract_kept, contract_away = split_x(add(contract_kept, contract_got), 0)
+    proj_kept, proj_away = split_x(add(proj_kept, proj_got), 0)
+    expand_kept, expand_away = add(expand_kept, expand_got)
+    qkv_away = dot(h_one, mixed_other, ((0,), (0,))).astype(bf16)
+    contract_away, proj_away, expand_away, qkv_away, grad_other = lax.optimization_barrier(
+        (contract_away, proj_away, expand_away, qkv_away, grad_other)
+    )
+    contract_got, expand_got, proj_got, qkv_got = (
+        swap_dp(contract_away, 1),
+        swap_row(expand_away),
+        swap_dp(proj_away, 1),
+        swap_col(qkv_away),
+    )
     outs = attend_backward(
-        place, mixed, probs, grad_attended, grad_middle, resid, params, qkv_low
-    )
-    grad_mixed, input_parts, sums_one = outs[0], outs[1:5], outs[5]
-    kept, away = reduce_row_col(h_one, grad_mixed)
-    qkv_grad = (kept, swap_row(away))
-
-    qkv_grad, output_parts, input_parts = lax.optimization_barrier(
-        (qkv_grad, output_parts, input_parts)
-    )
-
-    def over_dp(kept, received):
-        gradient = (kept + received.astype(f32)).astype(bf16)
-        if n_dp != 8:
-            return lax.psum(gradient, "dp").astype(f32)
-        rows = gradient.shape[0] // 2
-        x, z = dp % 2, dp // 2
-        away = lax.dynamic_slice_in_dim(gradient, (1 - x) * rows, rows)
-        total = lax.dynamic_slice_in_dim(gradient, x * rows, rows).astype(f32)
-        total = (total + swap_dp(away, 1).astype(f32)).astype(bf16)
-        pieces = [lax.dynamic_slice_in_dim(total, (z ^ d) * (rows // 4), rows // 4) for d in range(4)]
-        mine = pieces[0].astype(f32)
-        for d in range(1, 4):
-            mine = mine + swap_dp(pieces[d], 2 * d).astype(f32)
-        mine = mine.astype(bf16)
-        here = jnp.stack([mine] + [swap_dp(mine, 2 * d) for d in range(1, 4)])
-        return here, swap_dp(here, 1)
-
-    contract_sum = over_dp(*contract_grad)
-    expand_sum = over_dp(*expand_grad)
-    proj_sum = over_dp(*proj_grad)
-    qkv_sum = over_dp(*qkv_grad)
+        place, mixed, probs, grad_attended, qkv_low, 0, [grad_other, grad_middle, resid, params]
+    )
+    mixed_own, input_parts, sums_one = outs[0], outs[1:5], outs[5]
+    contract_got, expand_got, proj_got, qkv_got, mixed_own = lax.optimization_barrier(
+        (contract_got, expand_got, proj_got, qkv_got, mixed_own)
+    )
+    qkv_kept, qkv_away = halves(over_col(h_one, mixed_own, qkv_got), 0)
+    contract_sum = add(contract_kept, contract_got)
+    expand_sum = add(expand_kept, expand_got)
+    proj_sum = add(proj_kept, proj_got)
+    qkv_away, contract_sum, expand_sum, proj_sum = lax.optimization_barrier(
+        (qkv_away, contract_sum, expand_sum, proj_sum)
+    )
+    qkv_got = swap_row(qkv_away)
+    if n_dp == 8:
+        first_pieces = [over_z(each) for each in (contract_sum, expand_sum, proj_sum)]
+        first_pieces, qkv_got, output_parts, input_parts = lax.optimization_barrier(
+            (first_pieces, qkv_got, output_parts, input_parts)
+        )
+        qkv_kept, qkv_away = split_x(add(qkv_kept, qkv_got), 0)
+        qkv_got = swap_dp(qkv_away, 1)
+        mine = [sum_z(each) for each in first_pieces]
+        mine, qkv_away = lax.optimization_barrier((mine, qkv_away))
+        gathered = [gather_z(each) for each in mine]
+        qkv_pieces = over_z(add(qkv_kept, qkv_got))
+        gathered, qkv_pieces = lax.optimization_barrier((gathered, qkv_pieces))
+        contract_sum, expand_sum, proj_sum = [gather_x(each) for each in gathered]
+        qkv_sum = gather_x(gather_z(sum_z(qkv_pieces)))
+    else:
+        def whole(total):
+            total = lax.psum(total, tuple(["dp"]), axis_index_groups=same_x)
+            other = swap_dp(total, 1)
+            return ordered(x, total, other).astype(f32)
+
+        same_x = [[i for i in range(n_dp) if i % 2 == bit] for bit in range(2)]
+        contract_sum, expand_sum, proj_sum = [
+            whole(each) for each in (contract_sum, expand_sum, proj_sum)
+        ]
+        qkv_kept, qkv_away = split_x(add(qkv_kept, qkv_got), 0)
+        qkv_sum = whole(add(qkv_kept, swap_dp(qkv_away, 1)))
+
     norm_parts = split_features(col, jnp.concatenate([sums_one, sums_two], axis=0))
     norm_sum = norm_parts[0] + sum(swap(norm_parts[d], d) for d in range(1, 4))
     if n_dp == 8:

time: 452 us -> 476 us (1.053)
  waiting for transfers between devices: 145 us -> 131 us
  starting transfers between devices: 92.2 us -> 106 us
  matrix products: 26.2 us -> 37.5 us
  local copies, waits for them, and re-layouts: 28.3 us -> 33.5 us
    ppermute x41 -> x43, waiting for transfers between devices: 65 us -> 47.5 us  [swap_dp(): return lax.ppermute(array, 'dp', [(i, i ^ distance) for i in range(n_dp)])]
    ppermute x41 -> x43, starting transfers between devices: 65 us -> 81.5 us  [swap_dp(): return lax.ppermute(array, 'dp', [(i, i ^ distance) for i in range(n_dp)])]
    dot_general x8, matrix products: 26.2 us -> 37.5 us  [dot(): lax.dot_general(left, right, (dims, ((), ())), preferred_element_type=f32)]
    pallas_call x1 -> x2, Pallas kernels: 38.4 us -> 43.3 us  [attend_backward(): pl.pallas_call(lambda *refs: backward_kernel(bool(rest), *refs), grid_spe...]
    unnamed x116 -> x132, local copies, waits for them, and re-layouts: 11.4 us -> 13.6 us
  transfers between devices with their start and end apart: 79 -> 81, of which waited for: 30 -> 26; matrix products, arithmetic and copies ran while one was open for 10% -> 10% of each run, Pallas kernels for 19% -> 19%
where the time goes in v4:
time: 476 us; the launch traced here: 467 us
  Pallas kernels  137 us (29%)
  waiting for transfers between devices  131 us (28%)
  starting transfers between devices  106 us (22%)
  matrix products  37.5 us (8%)
  local copies, waits for them, and re-layouts  33.5 us (7%)
  other arithmetic  19.9 us (4%)
    ppermute x38, waiting for transfers between devices, swap(): return lax.ppermute(array, GROUP, [(i, i ^ distance) for i in range(4)])  84 us
    ppermute x43, starting transfers between devices, swap_dp(): return lax.ppermute(array, 'dp', [(i, i ^ distance) for i in range(n_dp)])  81.5 us
    ppermute x43, waiting for transfers between devices, swap_dp(): return lax.ppermute(array, 'dp', [(i, i ^ distance) for i in range(n_dp)])  47.5 us
    pallas_call x1, Pallas kernels, block_middle(): pl.pallas_call(block_kernel, grid_spec=pltpu.PrefetchScalarGridSpec(num_s...  44.2 us
    pallas_call x2, Pallas kernels, attend_backward(): pl.pallas_call(lambda *refs: backward_kernel(bool(rest), *refs), grid_spe...  43.3 us
    dot_general x8, matrix products, dot(): lax.dot_general(left, right, (dims, ((), ())), preferred_element_type=f32)  37.5 us
    ppermute x38, starting transfers between devices, swap(): return lax.ppermute(array, GROUP, [(i, i ^ distance) for i in range(4)])  24.1 us
    pallas_call x1, Pallas kernels, attend_forward(): pl.pallas_call(forward_kernel, grid=(STEPS,), in_specs=[resident(resid),...  20.7 us
  transfers between devices with their start and end apart: 81, of which 26 were waited for; matrix products, arithmetic and copies ran while one was open for 10% of the time, Pallas kernels for 19%

profile of v4, /device:TPU:0, one launch (start us, length us, event | category | flops | bytes accessed | tf_op | source)
XLA Modules:
  0.0 467.0 jit_solution(12599548860452408621)
XLA Ops:
  6.1 3.8 constant_dynamic-slice_fusion.28
  21.5 6.4 %collective-permute-done.1 = bf16[1182,192]{0,1:T(8,128)(2,1)} collective-permute-done((bf16[1182,192]{0,1:T(8,128)(2,1)}, bf16[1182,192]{0,1:T(8,128)(2,1)}, u32[]{:S(2)}, u32[]{:S(2)}) %collective-permute-start.1) | collective-permute-done | bytes 453920 | tf_op jit(solution)/shard_map/ppermute | solution.py:596
  27.9 9.0 %collective-permute-done.2 = bf16[1182,192]{0,1:T(8,128)(2,1)} collective-permute-done((bf16[1182,192]{0,1:T(8,128)(2,1)}, bf16[1182,192]{0,1:T(8,128)(2,1)}, u32[]{:S(2)}, u32[]{:S(2)}) %collective-permute-start.2) | collective-permute-done | bytes 453920 | tf_op jit(solution)/shard_map/ppermute | solution.py:596
  46.0 11.7 %collective-permute-done.10 = bf16[192,384]{1,0:T(8,128)(2,1)} collective-permute-done((bf16[192,384]{1,0:T(8,128)(2,1)}, bf16[192,384]{1,0:T(8,128)(2,1)}, u32[]{:S(2)}, u32[]{:S(2)}) %collective-permute-start.10) | collective-permute-done | bytes 147488 | tf_op jit(solution)/shard_map/ppermute | solution.py:596
  80.6 20.7 %attend_forward.1 = (bf16[1200,768]{1,0:T(8,128)(2,1)}, bf16[1200,2304]{1,0:T(8,128)(2,1)}, bf16[1200,768]{1,0:T(8,128)(2,1)}, bf16[6,12,208,256]{3,2,1,0:T(8,128)(2,1)}) custom-call(bf16[1200,768]{1,0:T(8,128)(2,1)} %copy-done.10, f32[4,768]{1,0:T(4,128)} %pad_maximum_fusion.4.refs_1_.refs_3_.refs_9_, bf16[384,1152]{1,0:T(8,128)(2,1)} %copy-done.29, ...), custom_call_target="tpu_custom_call" | custom-call | flops 20000000000 | bytes 18432000 | tf_op jit(solution)/shard_map/attend_forward/pallas_call | solution.py:251
  106.9 5.4 %collective-permute-done.26 = bf16[384,384]{1,0:T(8,128)(2,1)S(1)} collective-permute-done((bf16[384,384]{1,0:T(8,128)(2,1)S(1)}, bf16[384,384]{1,0:T(8,128)(2,1)S(1)}, u32[]{:S(2)}, u32[]{:S(2)}) %collective-permute-start.26) | collective-permute-done | bytes 294944 | tf_op jit(solution)/shard_map/ppermute | solution.py:599
  113.0 4.8 %collective-permute-done.23 = bf16[96,1536]{1,0:T(8,128)(2,1)S(1)} collective-permute-done((bf16[96,1536]{1,0:T(8,128)(2,1)S(1)}, bf16[96,1536]{1,0:T(8,128)(2,1)S(1)}, u32[]{:S(2)}, u32[]{:S(2)}) %collective-permute-start.23) | collective-permute-done | bytes 294944 | tf_op jit(solution)/shard_map/ppermute | solution.py:599
  126.7 44.2 %block_middle.1 = (bf16[192,1200]{1,0:T(8,128)(2,1)}, bf16[192,1200]{1,0:T(8,128)(2,1)}, bf16[192,1200]{1,0:T(8,128)(2,1)}, bf16[192,1200]{1,0:T(8,128)(2,1)}, b...) custom-call(s32[4]{0:T(128)} %copy-done.22, ...), custom_call_target="tpu_custom_call" | custom-call | flops 25480396800 | bytes 29491200 | tf_op jit(solution)/shard_map/block_middle/pallas_call | solution.py:503
  170.9 7.4 %fusion.9 = bf16[768,1536]{1,0:T(8,128)(2,1)} fusion(bf16[1200,768]{1,0:T(8,128)(2,1)} %get-tuple-element.175, bf16[1200,3072]{1,0:T(8,128)(2,1)} %get-tuple-element.176), kind=kOutput, calls=%fused_computation.10 | convolution fusion | flops 2832334848 | bytes 7888896 | tf_op jit(solution)/shard_map/dot_general | solution.py:32
  178.5 4.6 fusion.6
  192.2 6.0 %add_convert_fusion = bf16[768,1536]{1,0:T(8,128)(2,1)S(1)} fusion(bf16[768,1536]{1,0:T(8,128)(2,1)} %collective-permute-done.30, bf16[1200,768]{1,0:T(8,128)(2,1)S(1)} %copy-done.62, bf16[1200,3072]{1,0:T(8,128)(2,1)} %get-tuple-element.176), kind=kOutput, calls=%fused_computation | convolution fusion | flops 2834694144 | bytes 10248192 | tf_op jit(solution)/shard_map/dot_general | solution.py:32
  198.3 4.9 %add_convert_fusion.1 = bf16[1536,768]{1,0:T(8,128)(2,1)S(1)} fusion(bf16[1536,768]{1,0:T(8,128)(2,1)} %collective-permute-done.29, bf16[1200,768]{1,0:T(8,128)(2,1)S(1)} %copy-done.13, bf16[1200,3072]{1,0:T(8,128)(2,1)S(1)} %bitcast.73), kind=kOutput, calls=%fused_computation.1 | convolution fusion | flops 2834694144 | bytes 10248192 | tf_op jit(solution)/shard_map/dot_general | solution.py:32
  207.9 18.7 %attend_backward.2 = (bf16[1200,1152]{1,0:T(8,128)(2,1)}, f32[1200,768]{1,0:T(8,128)}) custom-call(s32[4]{0:T(128)} %copy-done.22, bf16[1200,2304]{1,0:T(8,128)(2,1)} %get-tuple-element.182.refs_1_, bf16[6,12,208,256]{3,2,1,0:T(8,128)(2,1)} %get-tuple-element.183.refs_2_, bf16[1200,768]{1,0:T(8,128)(2,1)} %get-tuple-element.184.refs_3_, ...), custom_call_target="tpu_custom_call" | custom-call | flops 15000000512 | bytes 11059200 | tf_op jit(solution)/shard_map/attend_backward/pallas_call | solution.py:393
  226.6 13.7 %collective-permute-done.34 = bf16[384,384]{1,0:T(8,128)(2,1)S(1)} collective-permute-done((bf16[384,384]{1,0:T(8,128)(2,1)S(1)}, bf16[384,384]{1,0:T(8,128)(2,1)S(1)}, u32[]{:S(2)}, u32[]{:S(2)}) %collective-permute-start.34) | collective-permute-done | bytes 294944 | tf_op jit(solution)/shard_map/ppermute | solution.py:596
  245.6 3.9 convolution_convert_fusion
  254.1 24.6 %attend_backward.3 = (bf16[1200,1152]{1,0:T(8,128)(2,1)}, bf16[192,1200]{1,0:T(8,128)(2,1)}, bf16[192,1200]{1,0:T(8,128)(2,1)}, bf16[192,1200]{1,0:T(8,128)(2,1)...) custom-call(s32[4]{0:T(128)} %copy-done.22, bf16[1200,2304]{1,0:T(8,128)(2,1)} %get-tuple-element.182.refs_1_, ...), custom_call_target="tpu_custom_call" | custom-call | flops 15000000512 | bytes 11059200 | tf_op jit(solution)/shard_map/attend_backward/pallas_call | solution.py:393
  280.2 5.3 %fusion.12 = bf16[768,1152]{1,0:T(8,128)(2,1)S(1)} fusion(bf16[768,1152]{1,0:T(8,128)(2,1)} %collective-permute-done.38, bf16[1200,768]{1,0:T(8,128)(2,1)S(1)} %copy-done.61, bf16[1200,1152]{1,0:T(8,128)(2,1)} %get-tuple-element.198), kind=kOutput, calls=%fused_computation.11 | convolution fusion | flops 2126020608 | bytes 8146944 | tf_op jit(solution)/shard_map/dot_general | solution.py:32
  294.4 15.2 %collective-permute-done.76 = f32[4,192]{1,0:T(4,128)S(1)} collective-permute-done((f32[4,192]{1,0:T(4,128)S(1)}, f32[4,192]{1,0:T(4,128)S(1)}, u32[]{:S(2)}, u32[]{:S(2)}) %collective-permute-start.76) | collective-permute-done | bytes 3104 | tf_op jit(solution)/shard_map/ppermute | solution.py:596
  318.4 4.0 collective-permute-start.44
  327.5 8.0 %collective-permute-start.79 = (f32[4,192]{1,0:T(4,128)S(1)}, f32[4,192]{1,0:T(4,128)S(1)}, u32[]{:S(2)}, u32[]{:S(2)}) collective-permute-start(f32[4,192]{1,0:T(4,128)S(1)} %add.245), channel_id=1, source_target_pairs={{0,8},{4,12},{8,0},{12,4},{16,24},{20,28},{24,16},{28,20},{1,9},{5... | collective-permute-start | bytes 9224 | tf_op jit(solution)/shard_map/ppermute | solution.py:599
  348.6 3.7 collective-permute-start.55
  358.9 3.6 collective-permute-start.60
  362.6 4.4 collective-permute-done.56
  366.9 12.0 %collective-permute-start.66 = (bf16[48,1152]{1,0:T(8,128)(2,1)S(1)}, bf16[48,1152]{1,0:T(8,128)(2,1)S(1)}, u32[]{:S(2)}, u32[]{:S(2)}) collective-permute-start(bf16[48,1152]{1,0:T(8,128)(2,1)S(1)} %get-tuple-element.289), channel_id=1, source_target_pairs={{0,16},{4,20},{8,24},{12,28},{16,0},{20,4},{24,8},{28,12},{1,17},{... | collective-permute-start | bytes 331784 | tf_op jit(solution)/shard_map/ppermute | solution.py:599
  381.2 7.0 %collective-permute-done.66 = bf16[48,1152]{1,0:T(8,128)(2,1)S(1)} collective-permute-done((bf16[48,1152]{1,0:T(8,128)(2,1)S(1)}, bf16[48,1152]{1,0:T(8,128)(2,1)S(1)}, u32[]{:S(2)}, u32[]{:S(2)}) %collective-permute-start.66) | collective-permute-done | bytes 110624 | tf_op jit(solution)/shard_map/ppermute | solution.py:599
  397.3 7.1 %collective-permute-done.54.refs_3_ = bf16[192,1200]{1,0:T(8,128)(2,1)S(1)} collective-permute-done((bf16[192,1200]{1,0:T(8,128)(2,1)S(1)}, bf16[192,1200]{1,0:T(8,128)(2,1)S(1)}, u32[]{:S(2)}, u32[]{:S(2)}) %collective-permute-start.54) | collective-permute-done | bytes 460832 | tf_op jit(solution)/shard_map/ppermute | solution.py:596
  410.0 8.4 %collective-permute-done.50.refs_2_ = bf16[192,1200]{1,0:T(8,128)(2,1)S(1)} collective-permute-done((bf16[192,1200]{1,0:T(8,128)(2,1)S(1)}, bf16[192,1200]{1,0:T(8,128)(2,1)S(1)}, u32[]{:S(2)}, u32[]{:S(2)}) %collective-permute-start.50) | collective-permute-done | bytes 460832 | tf_op jit(solution)/shard_map/ppermute | solution.py:596
  424.0 3.8 collective-permute-done.51.refs_3_
  430.9 16.2 %collective-permute-done.72.there = bf16[4,48,384]{2,1,0:T(8,128)(2,1)S(1)} collective-permute-done((bf16[4,48,384]{2,1,0:T(8,128)(2,1)S(1)}, bf16[4,48,384]{2,1,0:T(8,128)(2,1)S(1)}, u32[]{:S(2)}, u32[]{:S(2)}) %collective-permute-start.72) | collective-permute-done | bytes 147488 | tf_op jit(solution)/shard_map/ppermute | solution.py:599
  450.8 4.9 %adamw_pieces.4 = (f32[384,1152]{1,0:T(8,128)}, f32[384,1152]{1,0:T(8,128)}, f32[384,1152]{1,0:T(8,128)}) custom-call(s32[4]{0:T(128)S(1)} %copy-done.23, f32[384,1152]{1,0:T(8,128)S(1)} %copy-done.3, f32[384,1152]{1,0:T(8,128)S(1)} %copy-done.14, f32[384,1152]{1,0:T(8,128)S(1)} %copy-done.15, bf16[4,48,1152]{2,1,0:T(8,128)(2,1)S(1)} %pad_maximum_fusion.2.here, ...), custom_call_target="tpu_custom_call" | custom-call | flops 8847360 | bytes 12386304 | tf_op jit(solution)/shard_map/adamw_pieces/pallas_call | solution.py:548
  455.7 5.5 %adamw_pieces.7 = (f32[1536,384]{1,0:T(8,128)}, f32[1536,384]{1,0:T(8,128)}, f32[1536,384]{1,0:T(8,128)}) custom-call(s32[4]{0:T(128)S(1)} %copy-done.23, f32[1536,384]{1,0:T(8,128)S(1)} %copy-done, f32[1536,384]{1,0:T(8,128)S(1)} %copy-done.5, f32[1536,384]{1,0:T(8,128)S(1)} %copy-done.6, bf16[4,192,384]{2,1,0:T(8,128)(2,1)S(1)} %pad_maximum_fusion.1.here, ...), custom_call_target="tpu_custom_call" | custom-call | flops 11796480 | bytes 16515072 | tf_op jit(solution)/shard_map/adamw_pieces/pallas_call | solution.py:548
  461.2 5.6 %adamw_pieces.6 = (f32[384,1536]{1,0:T(8,128)}, f32[384,1536]{1,0:T(8,128)}, f32[384,1536]{1,0:T(8,128)}) custom-call(s32[4]{0:T(128)S(1)} %copy-done.23, f32[384,1536]{1,0:T(8,128)S(1)} %copy-done.2, f32[384,1536]{1,0:T(8,128)S(1)} %copy-done.7, f32[384,1536]{1,0:T(8,128)S(1)} %copy-done.8, bf16[4,48,1536]{2,1,0:T(8,128)(2,1)S(1)} %pad_maximum_fusion.here, ...), custom_call_target="tpu_custom_call" | custom-call | flops 11796480 | bytes 16515072 | tf_op jit(solution)/shard_map/adamw_pieces/pallas_call | solution.py:548
  (338 shorter events, 160.7 us)
Async XLA Ops:
  10.1 26.8 %collective-permute-start.2 = (bf16[1182,192]{0,1:T(8,128)(2,1)}, bf16[1182,192]{0,1:T(8,128)(2,1)}, u32[]{:S(2)}, u32[]{:S(2)}) collective-permute-start(bf16[1182,192]{0,1:T(8,128)(2,1)} %get-tuple-element.276), channel_id=1, source_target_pairs={{0,3},{1,2},{2,1},{3,0},{4,7},{5,6},{6,5},{7,4},{8,11},{9,10},{10,... | collective-permute-start | bytes 1361672 | tf_op jit(solution)/shard_map/ppermute | solution.py:596
  36.9 20.7 %collective-permute-start.7 = (bf16[192,1152]{1,0:T(8,128)(2,1)}, bf16[192,1152]{1,0:T(8,128)(2,1)}, u32[]{:S(2)}, u32[]{:S(2)}) collective-permute-start(bf16[192,1152]{1,0:T(8,128)(2,1)} %collective-permute-done.3), channel_id=1, source_target_pairs={{0,4},{4,0},{8,12},{12,8},{16,20},{20,16},{24,28},{28,24},{1,5},{5... | collective-permute-start | bytes 1327112 | tf_op jit(solution)/shard_map/ppermute | solution.py:599
  38.4 35.2 %collective-permute-start.11 = (bf16[384,1152]{1,0:T(8,128)(2,1)}, bf16[384,1152]{1,0:T(8,128)(2,1)}, u32[]{:S(2)}, u32[]{:S(2)}) collective-permute-start(bf16[384,1152]{1,0:T(8,128)(2,1)} %copy-done.29), channel_id=1, source_target_pairs={{0,1},{1,0},{2,3},{3,2},{4,5},{5,4},{6,7},{7,6},{8,9},{9,8},{10,11... | collective-permute-start | bytes 2654216 | tf_op jit(solution)/shard_map/ppermute | solution.py:596
  60.2 20.2 %collective-permute-start.12 = (bf16[384,1152]{1,0:T(8,128)(2,1)}, bf16[384,1152]{1,0:T(8,128)(2,1)}, u32[]{:S(2)}, u32[]{:S(2)}) collective-permute-start(bf16[384,1152]{1,0:T(8,128)(2,1)} %maximum_select_fusion.2.refs_3_.refs_5_), channel_id=1, source_target_pairs={{0,1},{1,0},{2,3},{3,2},{4,5},{5,4},{6,7},{7,6},{8,9},{9,8},{10,11... | collective-permute-start | bytes 2654216 | tf_op jit(solution)/shard_map/ppermute | solution.py:596
  73.6 27.7 %collective-permute-start.15 = (bf16[384,384]{1,0:T(8,128)(2,1)}, bf16[384,384]{1,0:T(8,128)(2,1)S(1)}, u32[]{:S(2)}, u32[]{:S(2)}) collective-permute-start(bf16[384,384]{1,0:T(8,128)(2,1)} %collective-permute-done.9), channel_id=1, source_target_pairs={{0,4},{4,0},{8,12},{12,8},{16,20},{20,16},{24,28},{28,24},{1,5},{5... | collective-permute-start | bytes 884744 | tf_op jit(solution)/shard_map/ppermute | solution.py:599
  76.1 25.4 %collective-permute-start.16 = (bf16[384,384]{1,0:T(8,128)(2,1)}, bf16[384,384]{1,0:T(8,128)(2,1)S(1)}, u32[]{:S(2)}, u32[]{:S(2)}) collective-permute-start(bf16[384,384]{1,0:T(8,128)(2,1)} %collective-permute-done.9), channel_id=1, source_target_pairs={{0,8},{4,12},{8,0},{12,4},{16,24},{20,28},{24,16},{28,20},{1,9},{5... | collective-permute-start | bytes 884744 | tf_op jit(solution)/shard_map/ppermute | solution.py:599
  78.5 23.4 %collective-permute-start.18 = (bf16[1182,192]{0,1:T(8,128)(2,1)S(1)}, bf16[1182,192]{0,1:T(8,128)(2,1)S(1)}, u32[]{:S(2)}, u32[]{:S(2)}) collective-permute-start(bf16[1182,192]{0,1:T(8,128)(2,1)S(1)} %copy-done.39), channel_id=1, source_target_pairs={{0,1},{1,0},{2,3},{3,2},{4,5},{5,4},{6,7},{7,6},{8,9},{9,8},{10,11... | collective-permute-start | bytes 1361672 | tf_op jit(solution)/shard_map/ppermute | solution.py:596
  78.5 23.4 %collective-permute-start.19 = (bf16[1182,192]{0,1:T(8,128)(2,1)S(1)}, bf16[1182,192]{0,1:T(8,128)(2,1)S(1)}, u32[]{:S(2)}, u32[]{:S(2)}) collective-permute-start(bf16[1182,192]{0,1:T(8,128)(2,1)S(1)} %copy-done.38), channel_id=1, source_target_pairs={{0,2},{1,3},{2,0},{3,1},{4,6},{5,7},{6,4},{7,5},{8,10},{9,11},{10,... | collective-permute-start | bytes 1361672 | tf_op jit(solution)/shard_map/ppermute | solution.py:596
  80.4 22.0 %collective-permute-start.20 = (bf16[1182,192]{0,1:T(8,128)(2,1)S(1)}, bf16[1182,192]{0,1:T(8,128)(2,1)S(1)}, u32[]{:S(2)}, u32[]{:S(2)}) collective-permute-start(bf16[1182,192]{0,1:T(8,128)(2,1)S(1)} %copy-done.37), channel_id=1, source_target_pairs={{0,3},{1,2},{2,1},{3,0},{4,7},{5,6},{6,5},{7,4},{8,11},{9,10},{10,... | collective-permute-start | bytes 1361672 | tf_op jit(solution)/shard_map/ppermute | solution.py:596
  101.3 23.0 %collective-permute-start.24 = (bf16[384,1536]{1,0:T(8,128)(2,1)S(1)}, bf16[384,1536]{1,0:T(8,128)(2,1)S(1)}, u32[]{:S(2)}, u32[]{:S(2)}) collective-permute-start(bf16[384,1536]{1,0:T(8,128)(2,1)S(1)} %copy-done.31), channel_id=1, source_target_pairs={{0,1},{1,0},{2,3},{3,2},{4,5},{5,4},{6,7},{7,6},{8,9},{9,8},{10,11... | collective-permute-start | bytes 3538952 | tf_op jit(solution)/shard_map/ppermute | solution.py:596
  101.5 22.8 %collective-permute-start.27 = (bf16[1536,384]{1,0:T(8,128)(2,1)S(1)}, bf16[1536,384]{1,0:T(8,128)(2,1)S(1)}, u32[]{:S(2)}, u32[]{:S(2)}) collective-permute-start(bf16[1536,384]{1,0:T(8,128)(2,1)S(1)} %copy-done.30), channel_id=1, source_target_pairs={{0,1},{1,0},{2,3},{3,2},{4,5},{5,4},{6,7},{7,6},{8,9},{9,8},{10,11... | collective-permute-start | bytes 3538952 | tf_op jit(solution)/shard_map/ppermute | solution.py:596
  204.3 35.9 %collective-permute-start.33 = (bf16[2,192,1536]{2,1,0:T(8,128)(2,1)}, bf16[2,192,1536]{2,1,0:T(8,128)(2,1)}, u32[]{:S(2)}, u32[]{:S(2)}) collective-permute-start(bf16[2,192,1536]{2,1,0:T(8,128)(2,1)} %constant_dynamic-slice_fusion.19), channel_id=1, source_target_pairs={{0,4},{4,0},{8,12},{12,8},{16,20},{20,16},{24,28},{28,24},{1,5},{5... | collective-permute-start | bytes 3538952 | tf_op jit(solution)/shard_map/ppermute | solution.py:599
  205.8 34.5 %collective-permute-start.32 = (bf16[1536,384]{1,0:T(8,128)(2,1)}, bf16[1536,384]{1,0:T(8,128)(2,1)S(1)}, u32[]{:S(2)}, u32[]{:S(2)}) collective-permute-start(bf16[1536,384]{1,0:T(8,128)(2,1)} %slice.55), channel_id=1, source_target_pairs={{0,2},{1,3},{2,0},{3,1},{4,6},{5,7},{6,4},{7,5},{8,10},{9,11},{10,... | collective-permute-start | bytes 3538952 | tf_op jit(solution)/shard_map/ppermute | solution.py:596
  207.5 32.7 %collective-permute-start.34 = (bf16[384,384]{1,0:T(8,128)(2,1)S(1)}, bf16[384,384]{1,0:T(8,128)(2,1)S(1)}, u32[]{:S(2)}, u32[]{:S(2)}) collective-permute-start(bf16[384,384]{1,0:T(8,128)(2,1)S(1)} %slice.56), channel_id=1, source_target_pairs={{0,2},{1,3},{2,0},{3,1},{4,6},{5,7},{6,4},{7,5},{8,10},{9,11},{10,... | collective-permute-start | bytes 884744 | tf_op jit(solution)/shard_map/ppermute | solution.py:596
  250.3 28.4 %collective-permute-start.38 = (bf16[768,1152]{1,0:T(8,128)(2,1)}, bf16[768,1152]{1,0:T(8,128)(2,1)}, u32[]{:S(2)}, u32[]{:S(2)}) collective-permute-start(bf16[768,1152]{1,0:T(8,128)(2,1)} %convolution_convert_fusion), channel_id=1, source_target_pairs={{0,1},{1,0},{2,3},{3,2},{4,5},{5,4},{6,7},{7,6},{8,9},{9,8},{10,11... | collective-permute-start | bytes 5308424 | tf_op jit(solution)/shard_map/ppermute | solution.py:596
  250.3 28.4 %collective-permute-start.35 = (bf16[768,384]{1,0:T(8,128)(2,1)}, bf16[768,384]{1,0:T(8,128)(2,1)S(1)}, u32[]{:S(2)}, u32[]{:S(2)}) collective-permute-start(bf16[768,384]{1,0:T(8,128)(2,1)} %constant_dynamic-slice_fusion.18), channel_id=1, source_target_pairs={{0,4},{4,0},{8,12},{12,8},{16,20},{20,16},{24,28},{28,24},{1,5},{5... | collective-permute-start | bytes 1769480 | tf_op jit(solution)/shard_map/ppermute | solution.py:599
  252.1 26.7 %collective-permute-start.36 = (bf16[192,1536]{1,0:T(8,128)(2,1)}, bf16[192,1536]{1,0:T(8,128)(2,1)S(1)}, u32[]{:S(2)}, u32[]{:S(2)}) collective-permute-start(bf16[192,1536]{1,0:T(8,128)(2,1)} %slice_bitcast_fusion.1), channel_id=1, source_target_pairs={{0,2},{1,3},{2,0},{3,1},{4,6},{5,7},{6,4},{7,5},{8,10},{9,11},{10,... | collective-permute-start | bytes 1769480 | tf_op jit(solution)/shard_map/ppermute | solution.py:596
  253.8 24.9 %collective-permute-start.37 = (bf16[192,384]{1,0:T(8,128)(2,1)S(1)}, bf16[192,384]{1,0:T(8,128)(2,1)S(1)}, u32[]{:S(2)}, u32[]{:S(2)}) collective-permute-start(bf16[192,384]{1,0:T(8,128)(2,1)S(1)} %constant_dynamic-slice_fusion.17), channel_id=1, source_target_pairs={{0,4},{4,0},{8,12},{12,8},{16,20},{20,16},{24,28},{28,24},{1,5},{5... | collective-permute-start | bytes 442376 | tf_op jit(solution)/shard_map/ppermute | solution.py:599
  287.9 50.2 %collective-permute-start.48 = (bf16[384,1152]{1,0:T(8,128)(2,1)}, bf16[384,1152]{1,0:T(8,128)(2,1)}, u32[]{:S(2)}, u32[]{:S(2)}) collective-permute-start(bf16[384,1152]{1,0:T(8,128)(2,1)} %slice.64), channel_id=1, source_target_pairs={{0,2},{1,3},{2,0},{3,1},{4,6},{5,7},{6,4},{7,5},{8,10},{9,11},{10,... | collective-permute-start | bytes 2654216 | tf_op jit(solution)/shard_map/ppermute | solution.py:596
  288.3 21.2 %collective-permute-start.76 = (f32[4,192]{1,0:T(4,128)S(1)}, f32[4,192]{1,0:T(4,128)S(1)}, u32[]{:S(2)}, u32[]{:S(2)}) collective-permute-start(f32[4,192]{1,0:T(4,128)S(1)} %get-tuple-element.296), channel_id=1, source_target_pairs={{0,2},{1,3},{2,0},{3,1},{4,6},{5,7},{6,4},{7,5},{8,10},{9,11},{10,... | collective-permute-start | bytes 9224 | tf_op jit(solution)/shard_map/ppermute | solution.py:596
  291.0 33.4 %collective-permute-start.42 = (bf16[48,1536]{1,0:T(8,128)(2,1)}, bf16[48,1536]{1,0:T(8,128)(2,1)}, u32[]{:S(2)}, u32[]{:S(2)}) collective-permute-start(bf16[48,1536]{1,0:T(8,128)(2,1)} %get-tuple-element.282), channel_id=1, source_target_pairs={{0,8},{4,12},{8,0},{12,4},{16,24},{20,28},{24,16},{28,20},{1,9},{5... | collective-permute-start | bytes 442376 | tf_op jit(solution)/shard_map/ppermute | solution.py:599
  291.8 33.0 %collective-permute-start.43 = (bf16[48,1536]{1,0:T(8,128)(2,1)}, bf16[48,1536]{1,0:T(8,128)(2,1)}, u32[]{:S(2)}, u32[]{:S(2)}) collective-permute-start(bf16[48,1536]{1,0:T(8,128)(2,1)} %get-tuple-element.281), channel_id=1, source_target_pairs={{0,16},{4,20},{8,24},{12,28},{16,0},{20,4},{24,8},{28,12},{1,17},{... | collective-permute-start | bytes 442376 | tf_op jit(solution)/shard_map/ppermute | solution.py:599
  327.5 25.1 %collective-permute-start.79 = (f32[4,192]{1,0:T(4,128)S(1)}, f32[4,192]{1,0:T(4,128)S(1)}, u32[]{:S(2)}, u32[]{:S(2)}) collective-permute-start(f32[4,192]{1,0:T(4,128)S(1)} %add.245), channel_id=1, source_target_pairs={{0,8},{4,12},{8,0},{12,4},{16,24},{20,28},{24,16},{28,20},{1,9},{5... | collective-permute-start | bytes 9224 | tf_op jit(solution)/shard_map/ppermute | solution.py:599
  356.0 22.9 %collective-permute-start.58 = (bf16[48,1536]{1,0:T(8,128)(2,1)S(1)}, bf16[48,1536]{1,0:T(8,128)(2,1)S(1)}, u32[]{:S(2)}, u32[]{:S(2)}) collective-permute-start(bf16[48,1536]{1,0:T(8,128)(2,1)S(1)} %add_convert_fusion.8), channel_id=1, source_target_pairs={{0,8},{4,12},{8,0},{12,4},{16,24},{20,28},{24,16},{28,20},{1,9},{5... | collective-permute-start | bytes 442376 | tf_op jit(solution)/shard_map/ppermute | solution.py:599
  356.6 24.1 %collective-permute-start.59 = (bf16[48,1536]{1,0:T(8,128)(2,1)S(1)}, bf16[48,1536]{1,0:T(8,128)(2,1)S(1)}, u32[]{:S(2)}, u32[]{:S(2)}) collective-permute-start(bf16[48,1536]{1,0:T(8,128)(2,1)S(1)} %add_convert_fusion.8), channel_id=1, source_target_pairs={{0,16},{4,20},{8,24},{12,28},{16,0},{20,4},{24,8},{28,12},{1,17},{... | collective-permute-start | bytes 442376 | tf_op jit(solution)/shard_map/ppermute | solution.py:599
  358.9 21.8 %collective-permute-start.60 = (bf16[48,1536]{1,0:T(8,128)(2,1)S(1)}, bf16[48,1536]{1,0:T(8,128)(2,1)S(1)}, u32[]{:S(2)}, u32[]{:S(2)}) collective-permute-start(bf16[48,1536]{1,0:T(8,128)(2,1)S(1)} %add_convert_fusion.8), channel_id=1, source_target_pairs={{0,24},{4,28},{8,16},{12,20},{16,8},{20,12},{24,0},{28,4},{1,25},{... | collective-permute-start | bytes 442376 | tf_op jit(solution)/shard_map/ppermute | solution.py:599
  366.9 21.2 %collective-permute-start.66 = (bf16[48,1152]{1,0:T(8,128)(2,1)S(1)}, bf16[48,1152]{1,0:T(8,128)(2,1)S(1)}, u32[]{:S(2)}, u32[]{:S(2)}) collective-permute-start(bf16[48,1152]{1,0:T(8,128)(2,1)S(1)} %get-tuple-element.289), channel_id=1, source_target_pairs={{0,16},{4,20},{8,24},{12,28},{16,0},{20,4},{24,8},{28,12},{1,17},{... | collective-permute-start | bytes 331784 | tf_op jit(solution)/shard_map/ppermute | solution.py:599
  404.8 22.9 %collective-permute-start.51 = (bf16[192,1200]{1,0:T(8,128)(2,1)S(1)}, bf16[192,1200]{1,0:T(8,128)(2,1)S(1)}, u32[]{:S(2)}, u32[]{:S(2)}) collective-permute-start(bf16[192,1200]{1,0:T(8,128)(2,1)S(1)} %copy-done.51), channel_id=1, source_target_pairs={{0,3},{1,2},{2,1},{3,0},{4,7},{5,6},{6,5},{7,4},{8,11},{9,10},{10,... | collective-permute-start | bytes 1382408 | tf_op jit(solution)/shard_map/ppermute | solution.py:596
  406.1 49.5 %collective-permute-start.74 = (bf16[4,192,384]{2,1,0:T(8,128)(2,1)S(1)}, bf16[4,192,384]{2,1,0:T(8,128)(2,1)S(1)}, u32[]{:S(2)}, u32[]{:S(2)}) collective-permute-start(bf16[4,192,384]{2,1,0:T(8,128)(2,1)S(1)} %pad_maximum_fusion.1.here), channel_id=1, source_target_pairs={{0,4},{4,0},{8,12},{12,8},{16,20},{20,16},{24,28},{28,24},{1,5},{5... | collective-permute-start | bytes 1769480 | tf_op jit(solution)/shard_map/ppermute | solution.py:599
  407.8 53.4 %collective-permute-start.73 = (bf16[4,48,1536]{2,1,0:T(8,128)(2,1)S(1)}, bf16[4,48,1536]{2,1,0:T(8,128)(2,1)S(1)}, u32[]{:S(2)}, u32[]{:S(2)}) collective-permute-start(bf16[4,48,1536]{2,1,0:T(8,128)(2,1)S(1)} %pad_maximum_fusion.here), channel_id=1, source_target_pairs={{0,4},{4,0},{8,12},{12,8},{16,20},{20,16},{24,28},{28,24},{1,5},{5... | collective-permute-start | bytes 1769480 | tf_op jit(solution)/shard_map/ppermute | solution.py:599
  408.2 42.5 %collective-permute-start.71 = (bf16[4,48,1152]{2,1,0:T(8,128)(2,1)S(1)}, bf16[4,48,1152]{2,1,0:T(8,128)(2,1)S(1)}, u32[]{:S(2)}, u32[]{:S(2)}) collective-permute-start(bf16[4,48,1152]{2,1,0:T(8,128)(2,1)S(1)} %pad_maximum_fusion.2.here), channel_id=1, source_target_pairs={{0,4},{4,0},{8,12},{12,8},{16,20},{20,16},{24,28},{28,24},{1,5},{5... | collective-permute-start | bytes 1327112 | tf_op jit(solution)/shard_map/ppermute | solution.py:599
  418.5 28.6 %collective-permute-start.72 = (bf16[4,48,384]{2,1,0:T(8,128)(2,1)S(1)}, bf16[4,48,384]{2,1,0:T(8,128)(2,1)S(1)}, u32[]{:S(2)}, u32[]{:S(2)}) collective-permute-start(bf16[4,48,384]{2,1,0:T(8,128)(2,1)S(1)} %pad_maximum_fusion.3.here), channel_id=1, source_target_pairs={{0,4},{4,0},{8,12},{12,8},{16,20},{20,16},{24,28},{28,24},{1,5},{5... | collective-permute-start | bytes 442376 | tf_op jit(solution)/shard_map/ppermute | solution.py:599
  (115 other events, 1443.3 us)

commit v5 on v4

--- a/solution.py
+++ b/solution.py
@@ -11,9 +11,12 @@
 KROWS = 256
 STEP = 10
 ROWS = 1200
-BLOCK = 240
+BLOCK = 608
 STEPS = 6
 GROUPED = 2
+WIDE = 384
+CHUNK = 768
+MLP_ROWS = 1536
 
 norm_epsilon = 1e-06
 beta_first = 0.9
@@ -39,7 +42,9 @@
 def gelu_and_slope(value):
     size = jnp.abs(value)
     density = jnp.exp(value * value * -0.5)
-    t = 1.0 / (1.0 + (0.3275911 * 0.5**0.5) * size)
+    base = 1.0 + (0.3275911 * 0.5**0.5) * size
+    t = pl.reciprocal(base, approx=True)
+    t = t * (2.0 - base * t)
     series = t * (
         0.254829592
         + t * (-0.284496736 + t * (1.421413741 + t * (-1.453152027 + t * 1.061405429)))
@@ -58,6 +63,10 @@
         first_hat / (jnp.sqrt(second_hat) + adam_epsilon) + decay_value * weight
     )
     return (moved, first_new, second_new)
+
+
+def row_blocks(rows, size=BLOCK):
+    return [slice(start, min(start + size, rows)) for start in range(0, rows, size)]
 
 
 def norm_rows(values):
@@ -197,14 +206,12 @@
 
     @pl.when(pl.program_id(0) == 0)
     def _():
-        for start in range(0, rows, BLOCK):
-            block = slice(start, start + BLOCK)
+        for block in row_blocks(rows):
             normed, _ = norm_rows(resid_ref[block, :].astype(f32))
             h_ref[block, :] = (normed * params[0:1, :] + params[1:2, :]).astype(bf16)
 
     weight = side_weight(weights, STEPS, 0)
-    for start in range(0, rows, BLOCK):
-        block = slice(start, start + BLOCK)
+    for block in row_blocks(rows):
         mixed = dot(h_ref[block, :], weight).astype(bf16)
         mixed_ref[block, :] = mixed
         wide[block, :] = mixed.astype(f32)
@@ -265,7 +272,7 @@
             jax.ShapeDtypeStruct(pair_probs, bf16),
         ],
         scratch_shapes=[pltpu.VMEM((padded, 384), f32), pltpu.VMEM((padded, 128), f32)],
-        compiler_params=pltpu.CompilerParams(vmem_limit_bytes=54 * 2**20),
+        compiler_params=pltpu.CompilerParams(vmem_limit_bytes=48 * 2**20),
         cost_estimate=pl.CostEstimate(
             flops=20 * 10**9, bytes_accessed=rows * width * 20, transcendentals=10**6
         ),
@@ -344,8 +351,7 @@
     def _():
         total[...] = before_ref[...] if last else jnp.zeros_like(total)
 
-    for start in range(0, rows, BLOCK):
-        block = slice(start, start + BLOCK)
+    for block in row_blocks(rows):
         grad_mixed = gathered[block, :].astype(bf16)
         out_ref[block, :] = grad_mixed
         total[block, :] += dot(grad_mixed, weight, ((1,), (1,)))
@@ -357,8 +363,7 @@
     def _():
         gain = jnp.zeros((1, total.shape[1]), f32)
         shift = jnp.zeros((1, total.shape[1]), f32)
-        for start in range(0, rows, BLOCK):
-            block = slice(start, start + BLOCK)
+        for block in row_blocks(rows):
             grad_one = total[block, :]
             normed, scaled = norm_rows(resid_ref[block, :].astype(f32))
             gain += jnp.sum(grad_one * normed, axis=0, keepdims=True)
@@ -409,23 +414,21 @@
             scratch_shapes=scratch,
         ),
         out_shape=[jax.ShapeDtypeStruct((rows, steps * 384), bf16), *extra],
-        compiler_params=pltpu.CompilerParams(vmem_limit_bytes=54 * 2**20),
-        cost_estimate=pl.CostEstimate(
-            flops=15 * 10**9, bytes_accessed=rows * width * 12, transcendentals=0
-        ),
+        compiler_params=pltpu.CompilerParams(vmem_limit_bytes=48 * 2**20),
         name="attend_backward",
     )(place, mixed, probs, grad_attended, *weights[2 * side : 2 * side + 2], *rest)
 
 
 def block_kernel(place, *refs):
     resid_ref, attended_ref, grad_ref, params = refs[:4]
-    proj, expand, contract = refs[4:8], refs[8:12], refs[12:16]
+    expand, contract, proj = refs[4:8], refs[8:12], refs[12:16]
     out_parts = refs[16:20]
     h_ref, hidden_ref, pre_ref, middle_ref, attended_grad_ref, sums_ref = refs[20:26]
-    middle, output, grad_two = refs[26:]
+    output, grad_two = refs[26:]
+    middle = middle_ref
     rows = resid_ref.shape[0]
     step = pl.program_id(0)
-    blocks = [slice(start, start + BLOCK) for start in range(0, rows, BLOCK)]
+    blocks = row_blocks(rows, 400)
 
     def proj_low():
         own = jnp.concatenate([proj[0][...], proj[1][...]], axis=1)
@@ -442,8 +445,21 @@
             normed, _ = norm_rows(value)
             h_ref[block, :] = (normed * params[2:3, :] + params[3:4, :]).astype(bf16)
 
-    expand_low = side_weight(expand, STEPS, 0)
-    contract_low = side_weight(contract, STEPS, 1)
+    own_side = step < pl.num_programs(0) // 2
+
+    def expand_side(own, other):
+        upper = jnp.concatenate([own[at : at + WIDE, :] for at in range(0, CHUNK, WIDE)], axis=1)
+        lower = jnp.concatenate([other[at : at + WIDE, :] for at in range(0, CHUNK, WIDE)], axis=1)
+        return jnp.concatenate([upper, lower], axis=0)
+
+    expand_low = jnp.where(
+        own_side, expand_side(expand[0], expand[1]), expand_side(expand[2], expand[3])
+    )
+    contract_low = jnp.where(
+        own_side,
+        jnp.concatenate([contract[0][...], contract[1][...]], axis=1),
+        jnp.concatenate([contract[2][...], contract[3][...]], axis=1),
+    )
 
     def products(block):
         return (
@@ -464,7 +480,7 @@
         output[block, :] += dot(hidden, contract_low)
         grad_two[block, :] += dot(grad_pre, expand_low, ((1,), (1,)))
 
-    @pl.when(step == STEPS - 1)
+    @pl.when(step == pl.num_programs(0) - 1)
     def _():
         weight = proj_low()
         gain = jnp.zeros((1, middle.shape[1]), f32)
@@ -487,10 +503,21 @@
             part_ref[...] = part.astype(bf16)
 
 
-def block_middle(place, resid, attended, grad, params, proj, expand, contract):
+def chunk_blocks(first, steps):
+    def own(i, *_):
+        return (first + jnp.minimum(i, steps // 2 - 1), 0)
+
+    def other(i, *_):
+        return (first + jnp.maximum(i - steps // 2, 0), 0)
+
+    return [pl.BlockSpec((CHUNK, WIDE), own)] * 2 + [pl.BlockSpec((CHUNK, WIDE), other)] * 2
+
+
+def block_middle(place, resid, attended, grad, params, weights):
     rows, width = resid.shape
-    ff = 2 * expand[0].shape[1]
-    chunk = ff // STEPS
+    ff = 2 * MLP_ROWS
+    chunk = CHUNK
+    steps = ff // CHUNK
     part = jax.ShapeDtypeStruct((width // 4, rows), bf16)
     narrow = jax.ShapeDtypeStruct((rows, width), bf16)
     broad = jax.ShapeDtypeStruct((rows, ff), bf16)
@@ -498,17 +525,25 @@
     sums = jax.ShapeDtypeStruct((2, width), f32)
 
     def fixed(shape):
-        return pl.BlockSpec(shape.shape, lambda i, *_: (0, 0))
+        return pl.BlockSpec(shape.shape, lambda i, *_: (0, 0), pipeline_mode=pl.Buffered(1))
 
     return pl.pallas_call(
         block_kernel,
         grid_spec=pltpu.PrefetchScalarGridSpec(
             num_scalar_prefetch=1,
-            grid=(STEPS,),
+            grid=(steps,),
             in_specs=[
-                *[resident(each) for each in (resid, attended, grad, params, *proj)],
-                *side_blocks(expand[0].shape[0], chunk, 1, STEPS),
-                *side_blocks(chunk, contract[0].shape[1], 0, STEPS),
+                *[resident(each) for each in (resid, attended, grad, params)],
+                *chunk_blocks(0, steps),
+                *chunk_blocks(steps // 2, steps),
+                *[
+                    pl.BlockSpec(
+                        (WIDE, WIDE),
+                        lambda i, *_: (2 * MLP_ROWS // WIDE, 0),
+                        pipeline_mode=pl.Buffered(1),
+                    )
+                ]
+                * 4,
             ],
             out_specs=[
                 *[fixed(part)] * 4,
@@ -519,37 +554,41 @@
                 fixed(narrow),
                 fixed(sums),
             ],
-            scratch_shapes=[pltpu.VMEM((rows, width), f32)] * 3,
+            scratch_shapes=[pltpu.VMEM((rows, width), f32)] * 2,
         ),
         out_shape=[*[part] * 4, narrow, broad, broad, wide, narrow, sums],
-        compiler_params=pltpu.CompilerParams(vmem_limit_bytes=58 * 2**20),
+        compiler_params=pltpu.CompilerParams(vmem_limit_bytes=56 * 2**20),
         cost_estimate=pl.CostEstimate(
             flops=2 * rows * width * (4 * ff + 2 * width),
             bytes_accessed=rows * ff * 8,
             transcendentals=2 * rows * ff,
         ),
         name="block_middle",
-    )(place, resid, attended, grad, params, *proj, *expand, *contract)
-
-
-def adamw_kernel(place, weight, first, second, here, there, weight_out, first_out, second_out):
-    x = place[2]
-    mine = jnp.where(pl.program_id(0) // 4 == x, here[0].astype(f32), there[0].astype(f32))
+    )(place, resid, attended, grad, params, *weights, *weights, *weights)
+
+
+def adamw_kernel(first_block, place, weight, first, second, here, there, *outs):
+    block = pl.program_id(0) + first_block
+    mine = jnp.where(block // 2 == place[2], here[0].astype(f32), there[0].astype(f32))
     results = adamw_update(
         weight[...], mine, first[...], second[...], rate_matrix, decay_matrix
     )
-    weight_out[...], first_out[...], second_out[...] = results
-
-
-def adamw_pieces(place, weight, first, second, here, there):
+    for out, result in zip(outs, results):
+        out[...] = result
+
+
+def adamw_blocks(place, weight, first, second, here, there, unit, first_block):
     rows, width = weight.shape
-    piece = pl.BlockSpec((rows // 8, width), lambda i, place: (i, 0))
-    part = pl.BlockSpec((1, rows // 8, width), lambda i, place: ((i % 4) ^ place[3], 0, 0))
+    if rows == WIDE:
+        piece = pl.BlockSpec((WIDE, WIDE), lambda i, *_: (0, i))
+    else:
+        piece = pl.BlockSpec((WIDE, WIDE), lambda i, *_: (i, 0))
+    part = pl.BlockSpec((1, WIDE, WIDE), lambda i, *_: (unit, (i + first_block) % 2, 0))
     return pl.pallas_call(
-        adamw_kernel,
+        lambda *refs: adamw_kernel(first_block, *refs),
         grid_spec=pltpu.PrefetchScalarGridSpec(
             num_scalar_prefetch=1,
-            grid=(8,),
+            grid=(rows * width // WIDE**2,),
             in_specs=[piece, piece, piece, part, part],
             out_specs=[piece] * 3,
         ),
@@ -558,7 +597,7 @@
         cost_estimate=pl.CostEstimate(
             flops=20 * rows * width, bytes_accessed=28 * rows * width, transcendentals=0
         ),
-        name="adamw_pieces",
+        name="adamw_blocks",
     )(place, weight, first, second, here, there)
 
 
@@ -630,48 +669,40 @@
         [in_order(col, params[0], params[1]), in_order(col, params[2], params[3])], axis=1
     )
     x, z = dp % 2, dp // 2
+
+    def stack(array):
+        blocks = [array[..., at : at + WIDE] for at in range(0, array.shape[-1], WIDE)]
+        return jnp.concatenate(blocks, axis=-2)
+
     qkv_mine = qkv_weight.astype(bf16)
     qkv_got = swap_row(dp_part(qkv_mine, 2))
-    expand_mine = expand_weight.astype(bf16)
-    contract_mine = contract_weight.astype(bf16)
-    proj_mine = proj_weight.astype(bf16)
-
-    resid_parts, qkv_got, *sends = lax.optimization_barrier(
-        (
-            resid_parts,
-            qkv_got,
-            dp_part(expand_mine, 4),
-            dp_part(contract_mine, 4),
-            dp_part(proj_mine, 2),
-        )
+    rest_mine = jnp.concatenate(
+        [stack(expand_weight), contract_weight, proj_weight], axis=0
+    ).astype(bf16)
+
+    resid_parts, params, qkv_got, rest_got = lax.optimization_barrier(
+        (resid_parts, params, qkv_got, dp_part(rest_mine, 4))
     )
     qkv_next = swap_dp(qkv_got, 1)
-    expand_got, contract_got, proj_got = [swap_row(each) for each in sends]
-    qkv_got, qkv_next, expand_got, contract_got, proj_got, grad_blocks = lax.optimization_barrier(
-        (qkv_got, qkv_next, expand_got, contract_got, proj_got, token_blocks(out_grad))
+    rest_got = swap_row(rest_got)
+    resid = tokens_together(place, [each.T for each in resid_parts])
+    qkv_got, qkv_next, grad_blocks, resid = lax.optimization_barrier(
+        (qkv_got, qkv_next, token_blocks(out_grad), resid)
     )
     qkv_low = all_blocks(qkv_mine, ordered(x, qkv_got, qkv_next))
-    quarters = [[each, swap_dp(each, 1), swap_dp(each, 2)] for each in (expand_got, contract_got)]
-    proj_next = swap_dp(proj_got, 1)
+    qkv_low, rest_got, grad_blocks = lax.optimization_barrier((qkv_low, rest_got, grad_blocks))
+    rest_x, rest_z = swap_dp(rest_got, 1), swap_dp(rest_got, 2)
     grad_parts = swap_all(grad_blocks)
-    resid = tokens_together(place, [each.T for each in resid_parts])
     h_one, mixed, attended, probs = attend_forward(resid, params, qkv_low)
-    attended, quarters, proj_next, grad_parts = lax.optimization_barrier(
-        (attended, quarters, proj_next, grad_parts)
-    )
-    expand_row, contract_row = [
-        ordered(
-            z % 2,
-            ordered(x, each[0], each[1]),
-            ordered(x, each[2], swap_dp(each[2], 1)),
-        )
-        for each in quarters
-    ]
-    proj_low = all_blocks(proj_mine, ordered(x, proj_got, proj_next))
-    expand_low = all_blocks(expand_mine, expand_row)
-    contract_low = all_blocks(contract_mine, contract_row)
+    attended, rest_x, rest_z, grad_parts = lax.optimization_barrier(
+        (attended, rest_x, rest_z, grad_parts)
+    )
+    rest_row = ordered(
+        z % 2, ordered(x, rest_got, rest_x), ordered(x, rest_z, swap_dp(rest_z, 1))
+    )
+    rest_low = all_blocks(rest_mine, rest_row)
     grad_low = tokens_together(place, [each.T for each in grad_parts])
-    outs = block_middle(place, resid, attended, grad_low, params, proj_low, expand_low, contract_low)
+    outs = block_middle(place, resid, attended, grad_low, params, rest_low)
     output_parts = outs[:4]
     h_two, hidden, grad_pre, grad_middle, grad_attended, sums_two = outs[4:]
 
@@ -686,59 +717,56 @@
         total = dot(left, right, ((0,), (0,))) + received.astype(f32)
         return total.astype(bf16)
 
-    def split_x(array, axis):
-        size = array.shape[axis] // 2
-        kept = lax.dynamic_slice_in_dim(array, x * size, size, axis)
-        return kept, lax.dynamic_slice_in_dim(array, (1 - x) * size, size, axis)
+    def split(array, bit):
+        size = array.shape[1] // 2
+        kept = lax.dynamic_slice_in_dim(array, bit * size, size, 1)
+        return kept, lax.dynamic_slice_in_dim(array, (1 - bit) * size, size, 1)
 
     def add(kept, received):
         return (kept.astype(f32) + received.astype(f32)).astype(bf16)
 
+    def join(bit, mine, partner):
+        return jnp.where(
+            bit == 0,
+            jnp.concatenate([mine, partner], axis=1),
+            jnp.concatenate([partner, mine], axis=1),
+        )
+
     def over_z(total):
-        rows = total.shape[0] // 4
-        pieces = [lax.dynamic_slice_in_dim(total, (z ^ d) * rows, rows) for d in range(4)]
-        return [pieces[0]] + [swap_dp(pieces[d], 2 * d) for d in range(1, 4)]
-
-    def sum_z(pieces):
-        return sum(piece.astype(f32) for piece in pieces).astype(bf16)
-
-    def gather_z(mine):
-        return [mine] + [swap_dp(mine, 2 * d) for d in range(1, 4)]
-
-    def gather_x(pieces):
-        here = jnp.stack(pieces)
-        return here, swap_dp(here, 1)
+        if n_dp != 8:
+            same_x = [[i for i in range(n_dp) if i % 2 == bit] for bit in range(2)]
+            return lax.psum(total, "dp", axis_index_groups=same_x)
+        for distance, bit in ((2, z % 2), (4, z // 2)):
+            kept, away = split(total, bit)
+            total = add(kept, swap_dp(away, distance))
+        for distance, bit in ((4, z // 2), (2, z % 2)):
+            total = join(bit, total, swap_dp(total, distance))
+        return total
 
     hidden_own, hidden_other = halves(hidden, 1)
     pre_own, pre_other = halves(grad_pre, 1)
     attended_own, attended_other = halves(attended, 1)
     branch = grad_middle.astype(bf16)
-    contract_away = swap_col(dot(hidden_other, grad_low, ((0,), (0,))).astype(bf16))
-    expand_away = swap_col(dot(h_two, pre_other, ((0,), (0,))).astype(bf16))
-    proj_away = swap_col(dot(attended_other, branch, ((0,), (0,))).astype(bf16))
-    contract_sum = over_col(hidden_own, grad_low, contract_away)
-    expand_sum = over_col(h_two, pre_own, expand_away)
-    proj_sum = over_col(attended_own, branch, proj_away)
-    contract_sum, expand_sum, proj_sum, grad_attended = lax.optimization_barrier(
-        (contract_sum, expand_sum, proj_sum, grad_attended)
-    )
+    contract_got = swap_col(dot(hidden_other, grad_low, ((0,), (0,))).astype(bf16))
+    expand_got = swap_col(dot(h_two, pre_other, ((0,), (0,))).astype(bf16))
+    proj_got = swap_col(dot(attended_other, branch, ((0,), (0,))).astype(bf16))
+    contract_sum = over_col(hidden_own, grad_low, contract_got)
     contract_kept, contract_away = halves(contract_sum, 1)
-    proj_kept, proj_away = halves(proj_sum, 1)
-    expand_sum = expand_sum.reshape(2, expand_sum.shape[0] // 2, expand_sum.shape[1])
-    expand_kept, expand_away = split_x(expand_sum, 1)
-    contract_got, expand_got, proj_got = (
-        swap_row(contract_away),
-        swap_dp(expand_away, 1),
-        swap_row(proj_away),
-    )
+    expand_sum = over_col(h_two, pre_own, expand_got)
+    expand_sum = stack(expand_sum.reshape(2, WIDE, expand_sum.shape[1]))
+    expand_kept, expand_away = split(expand_sum, x)
+    proj_kept, proj_away = halves(over_col(attended_own, branch, proj_got), 1)
+    contract_away, expand_away, proj_away, grad_attended = lax.optimization_barrier(
+        (contract_away, expand_away, proj_away, grad_attended)
+    )
+    contract_got, expand_got = swap_row(contract_away), swap_dp(expand_away, 1)
     mixed_other, grad_other = attend_backward(
         place, mixed, probs, grad_attended, qkv_low, 1, []
     )
-    contract_got, expand_got, proj_got, mixed_other, grad_other = lax.optimization_barrier(
-        (contract_got, expand_got, proj_got, mixed_other, grad_other)
-    )
-    contract_kept, contract_away = split_x(add(contract_kept, contract_got), 0)
-    proj_kept, proj_away = split_x(add(proj_kept, proj_got), 0)
+    contract_got, expand_got, mixed_other, grad_other = lax.optimization_barrier(
+        (contract_got, expand_got, mixed_other, grad_other)
+    )
+    contract_kept, contract_away = split(add(contract_kept, contract_got)[None], x)
     expand_kept, expand_away = add(expand_kept, expand_got)
     qkv_away = dot(h_one, mixed_other, ((0,), (0,))).astype(bf16)
     contract_away, proj_away, expand_away, qkv_away, grad_other = lax.optimization_barrier(
@@ -747,7 +775,7 @@
     contract_got, expand_got, proj_got, qkv_got = (
         swap_dp(contract_away, 1),
         swap_row(expand_away),
-        swap_dp(proj_away, 1),
+        swap_row(proj_away),
         swap_col(qkv_away),
     )
     outs = attend_backward(
@@ -758,39 +786,20 @@
         (contract_got, expand_got, proj_got, qkv_got, mixed_own)
     )
     qkv_kept, qkv_away = halves(over_col(h_one, mixed_own, qkv_got), 0)
-    contract_sum = add(contract_kept, contract_got)
-    expand_sum = add(expand_kept, expand_got)
-    proj_sum = add(proj_kept, proj_got)
-    qkv_away, contract_sum, expand_sum, proj_sum = lax.optimization_barrier(
-        (qkv_away, contract_sum, expand_sum, proj_sum)
-    )
+    mlp_sum = jnp.concatenate(
+        [add(contract_kept, contract_got), add(expand_kept, expand_got)[None]], axis=0
+    )
+    qkv_away, mlp_sum = lax.optimization_barrier((qkv_away, mlp_sum))
     qkv_got = swap_row(qkv_away)
-    if n_dp == 8:
-        first_pieces = [over_z(each) for each in (contract_sum, expand_sum, proj_sum)]
-        first_pieces, qkv_got, output_parts, input_parts = lax.optimization_barrier(
-            (first_pieces, qkv_got, output_parts, input_parts)
-        )
-        qkv_kept, qkv_away = split_x(add(qkv_kept, qkv_got), 0)
-        qkv_got = swap_dp(qkv_away, 1)
-        mine = [sum_z(each) for each in first_pieces]
-        mine, qkv_away = lax.optimization_barrier((mine, qkv_away))
-        gathered = [gather_z(each) for each in mine]
-        qkv_pieces = over_z(add(qkv_kept, qkv_got))
-        gathered, qkv_pieces = lax.optimization_barrier((gathered, qkv_pieces))
-        contract_sum, expand_sum, proj_sum = [gather_x(each) for each in gathered]
-        qkv_sum = gather_x(gather_z(sum_z(qkv_pieces)))
-    else:
-        def whole(total):
-            total = lax.psum(total, tuple(["dp"]), axis_index_groups=same_x)
-            other = swap_dp(total, 1)
-            return ordered(x, total, other).astype(f32)
-
-        same_x = [[i for i in range(n_dp) if i % 2 == bit] for bit in range(2)]
-        contract_sum, expand_sum, proj_sum = [
-            whole(each) for each in (contract_sum, expand_sum, proj_sum)
-        ]
-        qkv_kept, qkv_away = split_x(add(qkv_kept, qkv_got), 0)
-        qkv_sum = whole(add(qkv_kept, swap_dp(qkv_away, 1)))
+    mlp_sum = over_z(mlp_sum)
+    qkv_got, output_parts, input_parts = lax.optimization_barrier(
+        (qkv_got, output_parts, input_parts)
+    )
+    both = jnp.concatenate([stack(add(qkv_kept, qkv_got)), add(proj_kept, proj_got)], axis=0)
+    both_kept, both_away = split(both[None], x)
+    both_sum = over_z(add(both_kept, swap_dp(both_away, 1)))
+    mlp_sum = (mlp_sum, swap_dp(mlp_sum, 1))
+    both_sum = (both_sum, swap_dp(both_sum, 1))
 
     norm_parts = split_features(col, jnp.concatenate([sums_one, sums_two], axis=0))
     norm_sum = norm_parts[0] + sum(swap(norm_parts[d], d) for d in range(1, 4))
@@ -804,16 +813,13 @@
         tokens_apart(place, tokens, swap_all(output_parts)),
         tokens_apart(place, tokens, swap_all(input_parts)),
     )
-    for weight, gradient, first, second in (
-        (qkv_weight, qkv_sum, qkv_first, qkv_second),
-        (proj_weight, proj_sum, proj_first, proj_second),
-        (expand_weight, expand_sum, expand_first, expand_second),
-        (contract_weight, contract_sum, contract_first, contract_second),
+    for weight, gradient, first, second, unit, block in (
+        (qkv_weight, both_sum, qkv_first, qkv_second, 0, 0),
+        (proj_weight, both_sum, proj_first, proj_second, 0, 3),
+        (expand_weight, mlp_sum, expand_first, expand_second, 1, 0),
+        (contract_weight, mlp_sum, contract_first, contract_second, 0, 0),
     ):
-        if n_dp == 8:
-            results += tuple(adamw_pieces(place, weight, first, second, *gradient))
-        else:
-            results += adamw_update(weight, gradient, first, second, rate_matrix, decay_matrix)
+        results += tuple(adamw_blocks(place, weight, first, second, *gradient, unit, block))
     return results + adamw_update(norm_params, norm_sum, norm_first, norm_second, rate_norm, 0.0)
 
 

time: 476 us -> 470 us (0.987)
  starting transfers between devices: 106 us -> 43.8 us
  waiting for transfers between devices: 131 us -> 179 us
  other arithmetic: 19.9 us -> 30.4 us
  Pallas kernels: 137 us -> 130 us
    ppermute x43 -> x20, starting transfers between devices: 81.5 us -> 22.5 us  [swap_dp(): return lax.ppermute(array, 'dp', [(i, i ^ distance) for i in range(n_dp)])]
    ppermute x43 -> x20, waiting for transfers between devices: 47.5 us -> 99.6 us  [swap_dp(): return lax.ppermute(array, 'dp', [(i, i ^ distance) for i in range(n_dp)])]
    convert_element_type x8 -> x10, other arithmetic: 4.07 us -> 12.9 us  [add(): return (kept.astype(f32) + received.astype(f32)).astype(bf16)]
    unnamed x132 -> x168, local copies, waits for them, and re-layouts: 13.6 us -> 21.1 us
    convert_element_type x7 -> x0, other arithmetic: 5.14 us -> none  [the longest x4 2.11 us: sum_z(): return sum((piece.astype(f32) for piece in pieces)).astype(bf16)]
    ppermute x38 -> x32, waiting for transfers between devices: 84 us -> 79.6 us  [swap(): return lax.ppermute(array, GROUP, [(i, i ^ distance) for i in range(4)])]
    ppermute x38 -> x32, starting transfers between devices: 24.1 us -> 21.3 us  [swap(): return lax.ppermute(array, GROUP, [(i, i ^ distance) for i in range(4)])]
  transfers between devices with their start and end apart: 81 -> 52, of which waited for: 26 -> 22; matrix products, arithmetic and copies ran while one was open for 10% -> 11% of each run, Pallas kernels for 19% -> 17%
where the time goes in v5:
time: 470 us; the launch traced here: 460 us
  waiting for transfers between devices  179 us (38%)
  Pallas kernels  130 us (28%)
  starting transfers between devices  43.8 us (9%)
  matrix products  37.6 us (8%)
  local copies, waits for them, and re-layouts  37.4 us (8%)
  other arithmetic  30.4 us (6%)
    ppermute x20, waiting for transfers between devices, swap_dp(): return lax.ppermute(array, 'dp', [(i, i ^ distance) for i in range(n_dp)])  99.6 us
    ppermute x32, waiting for transfers between devices, swap(): return lax.ppermute(array, GROUP, [(i, i ^ distance) for i in range(4)])  79.6 us
    pallas_call x1, Pallas kernels, block_middle(): pl.pallas_call(block_kernel, grid_spec=pltpu.PrefetchScalarGridSpec(num_s...  44.2 us
    pallas_call x2, Pallas kernels, attend_backward(): pl.pallas_call(lambda *refs: backward_kernel(bool(rest), *refs), grid_spe...  40.3 us
    dot_general x8, matrix products, dot(): lax.dot_general(left, right, (dims, ((), ())), preferred_element_type=f32)  37.6 us
    ppermute x20, starting transfers between devices, swap_dp(): return lax.ppermute(array, 'dp', [(i, i ^ distance) for i in range(n_dp)])  22.5 us
    ppermute x32, starting transfers between devices, swap(): return lax.ppermute(array, GROUP, [(i, i ^ distance) for i in range(4)])  21.3 us
    unnamed x168, local copies, waits for them, and re-layouts  21.1 us
  transfers between devices with their start and end apart: 52, of which 22 were waited for; matrix products, arithmetic and copies ran while one was open for 11% of the time, Pallas kernels for 17%

profile of v5, /device:TPU:0, one launch (start us, length us, event | category | flops | bytes accessed | tf_op | source)
XLA Modules:
  0.0 460.5 jit_solution(15388413507724888732)
XLA Ops:
  21.1 18.6 %collective-permute-done.5 = f32[4,192]{1,0:T(4,128)S(1)} collective-permute-done((f32[4,192]{1,0:T(4,128)S(1)}, f32[4,192]{1,0:T(4,128)S(1)}, u32[]{:S(2)}, u32[]{:S(2)}) %collective-permute-start.5) | collective-permute-done | bytes 3104 | tf_op jit(solution)/shard_map/ppermute | solution.py:635
  41.4 3.2 constant_dynamic-slice_fusion.5
  48.0 4.4 collective-permute-done.7
  54.6 17.0 %collective-permute-done.10 = bf16[864,384]{1,0:T(8,128)(2,1)S(1)} collective-permute-done((bf16[864,384]{1,0:T(8,128)(2,1)S(1)}, bf16[864,384]{1,0:T(8,128)(2,1)S(1)}, u32[]{:S(2)}, u32[]{:S(2)}) %collective-permute-start.10) | collective-permute-done | bytes 663584 | tf_op jit(solution)/shard_map/ppermute | solution.py:635
  76.5 20.0 %attend_forward.1 = (bf16[1200,768]{1,0:T(8,128)(2,1)S(1)}, bf16[1200,2304]{1,0:T(8,128)(2,1)}, bf16[1200,768]{1,0:T(8,128)(2,1)}, bf16[6,12,208,256]{3,2,1,0:T(8,128)(2,1)}) custom-call(bf16[1200,768]{1,0:T(8,128)(2,1)} %copy-done.2, f32[4,768]{1,0:T(4,128)S(1)} %pad_maximum_fusion.3.refs_1_.refs_3_.refs_9_, ...), custom_call_target="tpu_custom_call" | custom-call | flops 20000000000 | bytes 18432000 | tf_op jit(solution)/shard_map/attend_forward/pallas_call | solution.py:258
  103.7 14.6 %collective-permute-done.16 = bf16[864,384]{1,0:T(8,128)(2,1)} collective-permute-done((bf16[864,384]{1,0:T(8,128)(2,1)}, bf16[864,384]{1,0:T(8,128)(2,1)}, u32[]{:S(2)}, u32[]{:S(2)}) %collective-permute-start.16) | collective-permute-done | bytes 663584 | tf_op jit(solution)/shard_map/ppermute | solution.py:638
  126.4 44.2 %block_middle.1 = (bf16[192,1200]{1,0:T(8,128)(2,1)}, bf16[192,1200]{1,0:T(8,128)(2,1)}, bf16[192,1200]{1,0:T(8,128)(2,1)}, bf16[192,1200]{1,0:T(8,128)(2,1)}, b...) custom-call(s32[4]{0:T(128)} %copy-done.34, ...), custom_call_target="tpu_custom_call" | custom-call | flops 25480396800 | bytes 29491200 | tf_op jit(solution)/shard_map/block_middle/pallas_call | solution.py:530
  170.7 7.4 %fusion.9 = bf16[768,1536]{1,0:T(8,128)(2,1)} fusion(bf16[1200,768]{1,0:T(8,128)(2,1)} %get-tuple-element.143, bf16[1200,3072]{1,0:T(8,128)(2,1)} %get-tuple-element.144), kind=kOutput, calls=%fused_computation.10 | convolution fusion | flops 2832334848 | bytes 7888896 | tf_op jit(solution)/shard_map/dot_general | solution.py:35
  178.3 4.6 %fusion.6 = bf16[1536,768]{1,0:T(8,128)(2,1)} fusion(bf16[1200,768]{1,0:T(8,128)(2,1)S(1)} %copy-done.17, bf16[1200,3072]{1,0:T(8,128)(2,1)S(1)} %copy-done.79), kind=kOutput, calls=%fused_computation.9 | convolution fusion | flops 2832334848 | bytes 7888896 | tf_op jit(solution)/shard_map/dot_general | solution.py:35
  185.2 3.4 collective-permute-done.21
  188.6 3.6 fusion.13
  193.8 6.0 %add_convert_fusion = bf16[768,1536]{1,0:T(8,128)(2,1)S(1)} fusion(bf16[768,1536]{1,0:T(8,128)(2,1)} %collective-permute-done.20, bf16[1200,768]{1,0:T(8,128)(2,1)S(1)} %copy-done.78, bf16[1200,3072]{1,0:T(8,128)(2,1)} %get-tuple-element.144), kind=kOutput, calls=%fused_computation | convolution fusion | flops 2834694144 | bytes 10248192 | tf_op jit(solution)/shard_map/dot_general | solution.py:35
  201.3 4.9 %add_convert_fusion.1 = bf16[1536,768]{1,0:T(8,128)(2,1)S(1)} fusion(bf16[1536,768]{1,0:T(8,128)(2,1)} %collective-permute-done.19, bf16[1200,768]{1,0:T(8,128)(2,1)S(1)} %copy-done.18, bf16[1200,3072]{1,0:T(8,128)(2,1)S(1)} %bitcast.57), kind=kOutput, calls=%fused_computation.1 | convolution fusion | flops 2834694144 | bytes 10248192 | tf_op jit(solution)/shard_map/dot_general | solution.py:35
  214.3 17.6 %attend_backward.2 = (bf16[1200,1152]{1,0:T(8,128)(2,1)}, f32[1200,768]{1,0:T(8,128)}) custom-call(s32[4]{0:T(128)S(1)} %copy-done.35, bf16[1200,2304]{1,0:T(8,128)(2,1)} %get-tuple-element.149.refs_1_, bf16[6,12,208,256]{3,2,1,0:T(8,128)(2,1)} %get-tuple-element.150.refs_2_, bf16[1200,768]{1,0:T(8,128)(2,1)S(1)} %copy-done.3, ...), custom_call_target="tpu_custom_call" | custom-call | tf_op jit(solution)/shard_map/attend_backward/pallas_call | solution.py:398
  231.9 7.2 %collective-permute-done.22 = bf16[1536,384]{1,0:T(8,128)(2,1)} collective-permute-done((bf16[1536,384]{1,0:T(8,128)(2,1)}, bf16[1536,384]{1,0:T(8,128)(2,1)}, u32[]{:S(2)}, u32[]{:S(2)}) %collective-permute-start.22) | collective-permute-done | bytes 1179680 | tf_op jit(solution)/shard_map/ppermute | solution.py:635
  245.0 3.9 convolution_convert_fusion
  254.1 22.6 %attend_backward.3 = (bf16[1200,1152]{1,0:T(8,128)(2,1)}, bf16[192,1200]{1,0:T(8,128)(2,1)S(1)}, bf16[192,1200]{1,0:T(8,128)(2,1)S(1)}, bf16[192,1200]{1,0:T(8,1...) custom-call(s32[4]{0:T(128)S(1)} %copy-done.35, bf16[1200,2304]{1,0:T(8,128)(2,1)} %get-tuple-element.149.refs_1_, ...), custom_call_target="tpu_custom_call" | custom-call | tf_op jit(solution)/shard_map/attend_backward/pallas_call | solution.py:398
  280.1 5.4 %fusion.12 = bf16[768,1152]{1,0:T(8,128)(2,1)S(1)} fusion(bf16[768,1152]{1,0:T(8,128)(2,1)} %collective-permute-done.27, bf16[1200,768]{1,0:T(8,128)(2,1)S(1)} %copy-done.46, bf16[1200,1152]{1,0:T(8,128)(2,1)} %get-tuple-element.165), kind=kOutput, calls=%fused_computation.11 | convolution fusion | flops 2126020608 | bytes 8146944 | tf_op jit(solution)/shard_map/dot_general | solution.py:35
  290.7 13.3 %collective-permute-done.41 = bf16[2,384,384]{2,1,0:T(8,128)(2,1)} collective-permute-done((bf16[2,384,384]{2,1,0:T(8,128)(2,1)}, bf16[2,384,384]{2,1,0:T(8,128)(2,1)}, u32[]{:S(2)}, u32[]{:S(2)}) %collective-permute-start.41) | collective-permute-done | bytes 589856 | tf_op jit(solution)/shard_map/ppermute | solution.py:638
  315.2 11.9 %collective-permute-done.42 = bf16[2,192,384]{2,1,0:T(8,128)(2,1)S(1)} collective-permute-done((bf16[2,192,384]{2,1,0:T(8,128)(2,1)S(1)}, bf16[2,192,384]{2,1,0:T(8,128)(2,1)S(1)}, u32[]{:S(2)}, u32[]{:S(2)}) %collective-permute-start.42) | collective-permute-done | bytes 294944 | tf_op jit(solution)/shard_map/ppermute | solution.py:638
  333.6 9.9 %collective-permute-done.43 = bf16[2,192,384]{2,1,0:T(8,128)(2,1)} collective-permute-done((bf16[2,192,384]{2,1,0:T(8,128)(2,1)S(1)}, bf16[2,192,384]{2,1,0:T(8,128)(2,1)}, u32[]{:S(2)}, u32[]{:S(2)}) %collective-permute-start.43) | collective-permute-done | bytes 294944 | tf_op jit(solution)/shard_map/ppermute | solution.py:638
  348.9 12.1 %collective-permute-done.37 = bf16[1,192,384]{2,1,0:T(8,128)(2,1)S(1)} collective-permute-done((bf16[1,192,384]{2,1,0:T(8,128)(2,1)S(1)}, bf16[1,192,384]{2,1,0:T(8,128)(2,1)S(1)}, u32[]{:S(2)}, u32[]{:S(2)}) %collective-permute-start.37) | collective-permute-done | bytes 147488 | tf_op jit(solution)/shard_map/ppermute | solution.py:638
  361.1 3.4 collective-permute-start.38
  371.9 24.2 %collective-permute-done.49 = f32[4,192]{1,0:T(4,128)S(1)} collective-permute-done((f32[4,192]{1,0:T(4,128)S(1)}, f32[4,192]{1,0:T(4,128)S(1)}, u32[]{:S(2)}, u32[]{:S(2)}) %collective-permute-start.49) | collective-permute-done | bytes 3104 | tf_op jit(solution)/shard_map/ppermute | solution.py:638
  401.2 3.2 collective-permute-done.51
  405.1 5.2 %collective-permute-done.33.refs_2_ = bf16[192,1200]{1,0:T(8,128)(2,1)S(1)} collective-permute-done((bf16[192,1200]{1,0:T(8,128)(2,1)S(1)}, bf16[192,1200]{1,0:T(8,128)(2,1)S(1)}, u32[]{:S(2)}, u32[]{:S(2)}) %collective-permute-start.33) | collective-permute-done | bytes 460832 | tf_op jit(solution)/shard_map/ppermute | solution.py:635
  411.8 8.1 %collective-permute-done.34.refs_3_ = bf16[192,1200]{1,0:T(8,128)(2,1)S(1)} collective-permute-done((bf16[192,1200]{1,0:T(8,128)(2,1)S(1)}, bf16[192,1200]{1,0:T(8,128)(2,1)S(1)}, u32[]{:S(2)}, u32[]{:S(2)}) %collective-permute-start.34) | collective-permute-done | bytes 460832 | tf_op jit(solution)/shard_map/ppermute | solution.py:635
  425.5 5.8 %collective-permute-done.30.refs_2_ = bf16[192,1200]{1,0:T(8,128)(2,1)S(1)} collective-permute-done((bf16[192,1200]{1,0:T(8,128)(2,1)S(1)}, bf16[192,1200]{1,0:T(8,128)(2,1)S(1)}, u32[]{:S(2)}, u32[]{:S(2)}) %collective-permute-start.30) | collective-permute-done | bytes 460832 | tf_op jit(solution)/shard_map/ppermute | solution.py:635
  431.4 9.6 %collective-permute-done.31.refs_3_ = bf16[192,1200]{1,0:T(8,128)(2,1)S(1)} collective-permute-done((bf16[192,1200]{1,0:T(8,128)(2,1)S(1)}, bf16[192,1200]{1,0:T(8,128)(2,1)S(1)}, u32[]{:S(2)}, u32[]{:S(2)}) %collective-permute-start.31) | collective-permute-done | bytes 460832 | tf_op jit(solution)/shard_map/ppermute | solution.py:635
  444.1 4.8 %adamw_blocks.7 = (f32[1536,384]{1,0:T(8,128)}, f32[1536,384]{1,0:T(8,128)}, f32[1536,384]{1,0:T(8,128)}) custom-call(s32[4]{0:T(128)S(1)} %copy-done.35, f32[1536,384]{1,0:T(8,128)S(1)} %copy-done, f32[1536,384]{1,0:T(8,128)S(1)} %copy-done.10, f32[1536,384]{1,0:T(8,128)S(1)} %copy-done.11, bf16[2,768,384]{2,1,0:T(8,128)(2,1)S(1)} %maximum_select_fusion.3.refs_4_, ...), custom_call_target="tpu_custom_call" | custom-call | flops 11796480 | bytes 16515072 | tf_op jit(solution)/shard_map/adamw_blocks/pallas_call | solution.py:587
  449.0 4.8 %adamw_blocks.6 = (f32[384,1536]{1,0:T(8,128)}, f32[384,1536]{1,0:T(8,128)}, f32[384,1536]{1,0:T(8,128)}) custom-call(s32[4]{0:T(128)S(1)} %copy-done.35, f32[384,1536]{1,0:T(8,128)S(1)} %copy-done.1, f32[384,1536]{1,0:T(8,128)S(1)} %copy-done.12, f32[384,1536]{1,0:T(8,128)S(1)} %copy-done.13, bf16[2,768,384]{2,1,0:T(8,128)(2,1)S(1)} %maximum_select_fusion.3.refs_4_, ...), custom_call_target="tpu_custom_call" | custom-call | flops 11796480 | bytes 16515072 | tf_op jit(solution)/shard_map/adamw_blocks/pallas_call | solution.py:587
  455.8 4.1 adamw_blocks.4
  (314 shorter events, 129.2 us)
Async XLA Ops:
  6.1 33.7 %collective-permute-start.6 = (bf16[192,1152]{1,0:T(8,128)(2,1)}, bf16[192,1152]{1,0:T(8,128)(2,1)}, u32[]{:S(2)}, u32[]{:S(2)}) collective-permute-start(bf16[192,1152]{1,0:T(8,128)(2,1)} %constant_dynamic-slice_fusion.10), channel_id=1, source_target_pairs={{0,2},{1,3},{2,0},{3,1},{4,6},{5,7},{6,4},{7,5},{8,10},{9,11},{10,... | collective-permute-start | bytes 1327112 | tf_op jit(solution)/shard_map/ppermute | solution.py:635
  8.6 31.2 %collective-permute-start = (bf16[1182,192]{0,1:T(8,128)(2,1)}, bf16[1182,192]{0,1:T(8,128)(2,1)}, u32[]{:S(2)}, u32[]{:S(2)}) collective-permute-start(bf16[1182,192]{0,1:T(8,128)(2,1)} %get-tuple-element.215), channel_id=1, source_target_pairs={{0,1},{1,0},{2,3},{3,2},{4,5},{5,4},{6,7},{7,6},{8,9},{9,8},{10,11... | collective-permute-start | bytes 1361672 | tf_op jit(solution)/shard_map/ppermute | solution.py:635
  8.9 30.9 %collective-permute-start.1 = (bf16[1182,192]{0,1:T(8,128)(2,1)}, bf16[1182,192]{0,1:T(8,128)(2,1)}, u32[]{:S(2)}, u32[]{:S(2)}) collective-permute-start(bf16[1182,192]{0,1:T(8,128)(2,1)} %get-tuple-element.217), channel_id=1, source_target_pairs={{0,2},{1,3},{2,0},{3,1},{4,6},{5,7},{6,4},{7,5},{8,10},{9,11},{10,... | collective-permute-start | bytes 1361672 | tf_op jit(solution)/shard_map/ppermute | solution.py:635
  17.3 22.5 %collective-permute-start.2 = (bf16[1182,192]{0,1:T(8,128)(2,1)}, bf16[1182,192]{0,1:T(8,128)(2,1)}, u32[]{:S(2)}, u32[]{:S(2)}) collective-permute-start(bf16[1182,192]{0,1:T(8,128)(2,1)} %get-tuple-element.214), channel_id=1, source_target_pairs={{0,3},{1,2},{2,1},{3,0},{4,7},{5,6},{6,5},{7,4},{8,11},{9,10},{10,... | collective-permute-start | bytes 1361672 | tf_op jit(solution)/shard_map/ppermute | solution.py:635
  19.3 20.3 %collective-permute-start.5 = (f32[4,192]{1,0:T(4,128)S(1)}, f32[4,192]{1,0:T(4,128)S(1)}, u32[]{:S(2)}, u32[]{:S(2)}) collective-permute-start(f32[4,192]{1,0:T(4,128)S(1)} %copy-done.71), channel_id=1, source_target_pairs={{0,3},{1,2},{2,1},{3,0},{4,7},{5,6},{6,5},{7,4},{8,11},{9,10},{10,... | collective-permute-start | bytes 9224 | tf_op jit(solution)/shard_map/ppermute | solution.py:635
  54.1 17.4 %collective-permute-start.9 = (bf16[384,1152]{1,0:T(8,128)(2,1)S(1)}, bf16[384,1152]{1,0:T(8,128)(2,1)S(1)}, u32[]{:S(2)}, u32[]{:S(2)}) collective-permute-start(bf16[384,1152]{1,0:T(8,128)(2,1)S(1)} %maximum_select_fusion.4.refs_3_.refs_5_), channel_id=1, source_target_pairs={{0,1},{1,0},{2,3},{3,2},{4,5},{5,4},{6,7},{7,6},{8,9},{9,8},{10,11... | collective-permute-start | bytes 2654216 | tf_op jit(solution)/shard_map/ppermute | solution.py:635
  54.2 17.3 %collective-permute-start.10 = (bf16[864,384]{1,0:T(8,128)(2,1)S(1)}, bf16[864,384]{1,0:T(8,128)(2,1)S(1)}, u32[]{:S(2)}, u32[]{:S(2)}) collective-permute-start(bf16[864,384]{1,0:T(8,128)(2,1)S(1)} %copy-done.66), channel_id=1, source_target_pairs={{0,2},{1,3},{2,0},{3,1},{4,6},{5,7},{6,4},{7,5},{8,10},{9,11},{10,... | collective-permute-start | bytes 1990664 | tf_op jit(solution)/shard_map/ppermute | solution.py:635
  71.5 28.5 %collective-permute-start.11 = (bf16[864,384]{1,0:T(8,128)(2,1)S(1)}, bf16[864,384]{1,0:T(8,128)(2,1)S(1)}, u32[]{:S(2)}, u32[]{:S(2)}) collective-permute-start(bf16[864,384]{1,0:T(8,128)(2,1)S(1)} %collective-permute-done.10), channel_id=1, source_target_pairs={{0,4},{4,0},{8,12},{12,8},{16,20},{20,16},{24,28},{28,24},{1,5},{5... | collective-permute-start | bytes 1990664 | tf_op jit(solution)/shard_map/ppermute | solution.py:638
  73.1 27.0 %collective-permute-start.12 = (bf16[864,384]{1,0:T(8,128)(2,1)S(1)}, bf16[864,384]{1,0:T(8,128)(2,1)}, u32[]{:S(2)}, u32[]{:S(2)}) collective-permute-start(bf16[864,384]{1,0:T(8,128)(2,1)S(1)} %collective-permute-done.10), channel_id=1, source_target_pairs={{0,8},{4,12},{8,0},{12,4},{16,24},{20,28},{24,16},{28,20},{1,9},{5... | collective-permute-start | bytes 1990664 | tf_op jit(solution)/shard_map/ppermute | solution.py:638
  74.7 23.1 %collective-permute-start.13 = (bf16[1182,192]{0,1:T(8,128)(2,1)S(1)}, bf16[1182,192]{0,1:T(8,128)(2,1)S(1)}, u32[]{:S(2)}, u32[]{:S(2)}) collective-permute-start(bf16[1182,192]{0,1:T(8,128)(2,1)S(1)} %get-tuple-element.132), channel_id=1, source_target_pairs={{0,1},{1,0},{2,3},{3,2},{4,5},{5,4},{6,7},{7,6},{8,9},{9,8},{10,11... | collective-permute-start | bytes 1361672 | tf_op jit(solution)/shard_map/ppermute | solution.py:635
  74.7 23.8 %collective-permute-start.14 = (bf16[1182,192]{0,1:T(8,128)(2,1)S(1)}, bf16[1182,192]{0,1:T(8,128)(2,1)S(1)}, u32[]{:S(2)}, u32[]{:S(2)}) collective-permute-start(bf16[1182,192]{0,1:T(8,128)(2,1)S(1)} %get-tuple-element.133), channel_id=1, source_target_pairs={{0,2},{1,3},{2,0},{3,1},{4,6},{5,7},{6,4},{7,5},{8,10},{9,11},{10,... | collective-permute-start | bytes 1361672 | tf_op jit(solution)/shard_map/ppermute | solution.py:635
  75.2 24.1 %collective-permute-start.15 = (bf16[1182,192]{0,1:T(8,128)(2,1)S(1)}, bf16[1182,192]{0,1:T(8,128)(2,1)S(1)}, u32[]{:S(2)}, u32[]{:S(2)}) collective-permute-start(bf16[1182,192]{0,1:T(8,128)(2,1)S(1)} %get-tuple-element.134), channel_id=1, source_target_pairs={{0,3},{1,2},{2,1},{3,0},{4,7},{5,6},{6,5},{7,4},{8,11},{9,10},{10,... | collective-permute-start | bytes 1361672 | tf_op jit(solution)/shard_map/ppermute | solution.py:635
  100.9 17.4 %collective-permute-start.16 = (bf16[864,384]{1,0:T(8,128)(2,1)}, bf16[864,384]{1,0:T(8,128)(2,1)}, u32[]{:S(2)}, u32[]{:S(2)}) collective-permute-start(bf16[864,384]{1,0:T(8,128)(2,1)} %collective-permute-done.12), channel_id=1, source_target_pairs={{0,4},{4,0},{8,12},{12,8},{16,20},{20,16},{24,28},{28,24},{1,5},{5... | collective-permute-start | bytes 1990664 | tf_op jit(solution)/shard_map/ppermute | solution.py:638
  101.5 23.0 %collective-permute-start.17 = (bf16[3456,384]{1,0:T(8,128)(2,1)}, bf16[3456,384]{1,0:T(8,128)(2,1)}, u32[]{:S(2)}, u32[]{:S(2)}) collective-permute-start(bf16[3456,384]{1,0:T(8,128)(2,1)} %convert_dynamic-update-slice_fusion.1.refs_4_.refs_8_.refs_12_), channel_id=1, source_target_pairs={{0,1},{1,0},{2,3},{3,2},{4,5},{5,4},{6,7},{7,6},{8,9},{9,8},{10,11... | collective-permute-start | bytes 7962632 | tf_op jit(solution)/shard_map/ppermute | solution.py:635
  182.9 17.2 %collective-permute-start.19 = (bf16[1536,768]{1,0:T(8,128)(2,1)}, bf16[1536,768]{1,0:T(8,128)(2,1)}, u32[]{:S(2)}, u32[]{:S(2)}) collective-permute-start(bf16[1536,768]{1,0:T(8,128)(2,1)} %fusion.6), channel_id=1, source_target_pairs={{0,1},{1,0},{2,3},{3,2},{4,5},{5,4},{6,7},{7,6},{8,9},{9,8},{10,11... | collective-permute-start | bytes 7077896 | tf_op jit(solution)/shard_map/ppermute | solution.py:635
  210.6 28.6 %collective-permute-start.22 = (bf16[1536,384]{1,0:T(8,128)(2,1)}, bf16[1536,384]{1,0:T(8,128)(2,1)}, u32[]{:S(2)}, u32[]{:S(2)}) collective-permute-start(bf16[1536,384]{1,0:T(8,128)(2,1)} %slice.117), channel_id=1, source_target_pairs={{0,2},{1,3},{2,0},{3,1},{4,6},{5,7},{6,4},{7,5},{8,10},{9,11},{10,... | collective-permute-start | bytes 3538952 | tf_op jit(solution)/shard_map/ppermute | solution.py:635
  211.1 28.3 %collective-permute-start.23 = (bf16[2,768,384]{2,1,0:T(8,128)(2,1)}, bf16[2,768,384]{2,1,0:T(8,128)(2,1)}, u32[]{:S(2)}, u32[]{:S(2)}) collective-permute-start(bf16[2,768,384]{2,1,0:T(8,128)(2,1)} %constant_dynamic-slice_fusion.4), channel_id=1, source_target_pairs={{0,4},{4,0},{8,12},{12,8},{16,20},{20,16},{24,28},{28,24},{1,5},{5... | collective-permute-start | bytes 3538952 | tf_op jit(solution)/shard_map/ppermute | solution.py:638
  248.9 28.0 %collective-permute-start.27 = (bf16[768,1152]{1,0:T(8,128)(2,1)}, bf16[768,1152]{1,0:T(8,128)(2,1)}, u32[]{:S(2)}, u32[]{:S(2)}) collective-permute-start(bf16[768,1152]{1,0:T(8,128)(2,1)} %convolution_convert_fusion), channel_id=1, source_target_pairs={{0,1},{1,0},{2,3},{3,2},{4,5},{5,4},{6,7},{7,6},{8,9},{9,8},{10,11... | collective-permute-start | bytes 5308424 | tf_op jit(solution)/shard_map/ppermute | solution.py:635
  248.9 27.9 %collective-permute-start.24 = (bf16[1,768,384]{2,1,0:T(8,128)(2,1)}, bf16[1,768,384]{2,1,0:T(8,128)(2,1)}, u32[]{:S(2)}, u32[]{:S(2)}) collective-permute-start(bf16[1,768,384]{2,1,0:T(8,128)(2,1)} %dynamic-slice_bitcast_fusion.1), channel_id=1, source_target_pairs={{0,4},{4,0},{8,12},{12,8},{16,20},{20,16},{24,28},{28,24},{1,5},{5... | collective-permute-start | bytes 1769480 | tf_op jit(solution)/shard_map/ppermute | solution.py:638
  249.4 27.4 %collective-permute-start.25 = (bf16[768,384]{1,0:T(8,128)(2,1)}, bf16[768,384]{1,0:T(8,128)(2,1)}, u32[]{:S(2)}, u32[]{:S(2)}) collective-permute-start(bf16[768,384]{1,0:T(8,128)(2,1)} %slice_bitcast_fusion.1), channel_id=1, source_target_pairs={{0,2},{1,3},{2,0},{3,1},{4,6},{5,7},{6,4},{7,5},{8,10},{9,11},{10,... | collective-permute-start | bytes 1769480 | tf_op jit(solution)/shard_map/ppermute | solution.py:635
  250.9 25.9 %collective-permute-start.26 = (bf16[384,384]{1,0:T(8,128)(2,1)}, bf16[384,384]{1,0:T(8,128)(2,1)}, u32[]{:S(2)}, u32[]{:S(2)}) collective-permute-start(bf16[384,384]{1,0:T(8,128)(2,1)} %slice.122), channel_id=1, source_target_pairs={{0,2},{1,3},{2,0},{3,1},{4,6},{5,7},{6,4},{7,5},{8,10},{9,11},{10,... | collective-permute-start | bytes 884744 | tf_op jit(solution)/shard_map/ppermute | solution.py:635
  286.6 21.6 %collective-permute-start.28 = (bf16[384,1152]{1,0:T(8,128)(2,1)}, bf16[384,1152]{1,0:T(8,128)(2,1)}, u32[]{:S(2)}, u32[]{:S(2)}) collective-permute-start(bf16[384,1152]{1,0:T(8,128)(2,1)} %slice.123), channel_id=1, source_target_pairs={{0,2},{1,3},{2,0},{3,1},{4,6},{5,7},{6,4},{7,5},{8,10},{9,11},{10,... | collective-permute-start | bytes 2654216 | tf_op jit(solution)/shard_map/ppermute | solution.py:635
  310.9 17.3 %collective-permute-start.35 = (bf16[1,768,384]{2,1,0:T(8,128)(2,1)S(1)}, bf16[1,768,384]{2,1,0:T(8,128)(2,1)}, u32[]{:S(2)}, u32[]{:S(2)}) collective-permute-start(bf16[1,768,384]{2,1,0:T(8,128)(2,1)S(1)} %dynamic-slice_bitcast_fusion), channel_id=1, source_target_pairs={{0,4},{4,0},{8,12},{12,8},{16,20},{20,16},{24,28},{28,24},{1,5},{5... | collective-permute-start | bytes 1769480 | tf_op jit(solution)/shard_map/ppermute | solution.py:638
  344.8 22.6 %collective-permute-start.44 = (bf16[2,384,384]{2,1,0:T(8,128)(2,1)S(1)}, bf16[2,384,384]{2,1,0:T(8,128)(2,1)S(1)}, u32[]{:S(2)}, u32[]{:S(2)}) collective-permute-start(bf16[2,384,384]{2,1,0:T(8,128)(2,1)S(1)} %maximum_select_fusion.6), channel_id=1, source_target_pairs={{0,8},{4,12},{8,0},{12,4},{16,24},{20,28},{24,16},{28,20},{1,9},{5... | collective-permute-start | bytes 1769480 | tf_op jit(solution)/shard_map/ppermute | solution.py:638
  367.7 76.4 %collective-permute-start.45 = (bf16[2,768,384]{2,1,0:T(8,128)(2,1)S(1)}, bf16[2,768,384]{2,1,0:T(8,128)(2,1)S(1)}, u32[]{:S(2)}, u32[]{:S(2)}) collective-permute-start(bf16[2,768,384]{2,1,0:T(8,128)(2,1)S(1)} %maximum_select_fusion.3.refs_4_), channel_id=1, source_target_pairs={{0,4},{4,0},{8,12},{12,8},{16,20},{20,16},{24,28},{28,24},{1,5},{5... | collective-permute-start | bytes 3538952 | tf_op jit(solution)/shard_map/ppermute | solution.py:638
  371.2 28.6 %collective-permute-start.39 = (bf16[1,384,384]{2,1,0:T(8,128)(2,1)S(1)}, bf16[1,384,384]{2,1,0:T(8,128)(2,1)S(1)}, u32[]{:S(2)}, u32[]{:S(2)}) collective-permute-start(bf16[1,384,384]{2,1,0:T(8,128)(2,1)S(1)} %maximum_select_fusion.8), channel_id=1, source_target_pairs={{0,8},{4,12},{8,0},{12,4},{16,24},{20,28},{24,16},{28,20},{1,9},{5... | collective-permute-start | bytes 884744 | tf_op jit(solution)/shard_map/ppermute | solution.py:638
  371.4 24.7 %collective-permute-start.49 = (f32[4,192]{1,0:T(4,128)S(1)}, f32[4,192]{1,0:T(4,128)S(1)}, u32[]{:S(2)}, u32[]{:S(2)}) collective-permute-start(f32[4,192]{1,0:T(4,128)S(1)} %add_add_fusion), channel_id=1, source_target_pairs={{0,4},{4,0},{8,12},{12,8},{16,20},{20,16},{24,28},{28,24},{1,5},{5... | collective-permute-start | bytes 9224 | tf_op jit(solution)/shard_map/ppermute | solution.py:638
  399.7 20.2 %collective-permute-start.34 = (bf16[192,1200]{1,0:T(8,128)(2,1)S(1)}, bf16[192,1200]{1,0:T(8,128)(2,1)S(1)}, u32[]{:S(2)}, u32[]{:S(2)}) collective-permute-start(bf16[192,1200]{1,0:T(8,128)(2,1)S(1)} %copy-done.39), channel_id=1, source_target_pairs={{0,3},{1,2},{2,1},{3,0},{4,7},{5,6},{6,5},{7,4},{8,11},{9,10},{10,... | collective-permute-start | bytes 1382408 | tf_op jit(solution)/shard_map/ppermute | solution.py:635
  404.4 49.4 %collective-permute-start.40 = (bf16[1,768,384]{2,1,0:T(8,128)(2,1)S(1)}, bf16[1,768,384]{2,1,0:T(8,128)(2,1)S(1)}, u32[]{:S(2)}, u32[]{:S(2)}) collective-permute-start(bf16[1,768,384]{2,1,0:T(8,128)(2,1)S(1)} %maximum_select_fusion.5.refs_4_), channel_id=1, source_target_pairs={{0,4},{4,0},{8,12},{12,8},{16,20},{20,16},{24,28},{28,24},{1,5},{5... | collective-permute-start | bytes 1769480 | tf_op jit(solution)/shard_map/ppermute | solution.py:638
  404.9 20.6 %collective-permute-start.29 = (bf16[192,1200]{1,0:T(8,128)(2,1)S(1)}, bf16[192,1200]{1,0:T(8,128)(2,1)S(1)}, u32[]{:S(2)}, u32[]{:S(2)}) collective-permute-start(bf16[192,1200]{1,0:T(8,128)(2,1)S(1)} %copy-done.77), channel_id=1, source_target_pairs={{0,1},{1,0},{2,3},{3,2},{4,5},{5,4},{6,7},{7,6},{8,9},{9,8},{10,11... | collective-permute-start | bytes 1382408 | tf_op jit(solution)/shard_map/ppermute | solution.py:635
  410.3 21.1 %collective-permute-start.30 = (bf16[192,1200]{1,0:T(8,128)(2,1)S(1)}, bf16[192,1200]{1,0:T(8,128)(2,1)S(1)}, u32[]{:S(2)}, u32[]{:S(2)}) collective-permute-start(bf16[192,1200]{1,0:T(8,128)(2,1)S(1)} %copy-done.76), channel_id=1, source_target_pairs={{0,2},{1,3},{2,0},{3,1},{4,6},{5,7},{6,4},{7,5},{8,10},{9,11},{10,... | collective-permute-start | bytes 1382408 | tf_op jit(solution)/shard_map/ppermute | solution.py:635
  419.9 21.1 %collective-permute-start.31 = (bf16[192,1200]{1,0:T(8,128)(2,1)S(1)}, bf16[192,1200]{1,0:T(8,128)(2,1)S(1)}, u32[]{:S(2)}, u32[]{:S(2)}) collective-permute-start(bf16[192,1200]{1,0:T(8,128)(2,1)S(1)} %copy-done.75), channel_id=1, source_target_pairs={{0,3},{1,2},{2,1},{3,0},{4,7},{5,6},{6,5},{7,4},{8,11},{9,10},{10,... | collective-permute-start | bytes 1382408 | tf_op jit(solution)/shard_map/ppermute | solution.py:635
  (102 other events, 1299.8 us)
